TPU v7x, 32 devices: a whole 2x2x4 slice. The times are simulated.
32 devices in a mesh: group: 2 (over x), tp: 16 (over z, y, core).
Axes of the slice: x: 2, y: 2, z: 4, core: 2. Of those that a mesh axis runs over, the one named last changes fastest.
Arguments:
- states: bfloat16 [2048, 7168], P(('group', 'tp')), parts along dimension 0, may hold values from -6 to 6
- norm_gain: float32 [7168], replicated, may hold values from 0.1 to 1.9
- w_gate: bfloat16 [7168, 4096], P(None, 'tp'), may hold values from -0.0625 to 0.0625
- w_up: bfloat16 [7168, 4096], P(None, 'tp'), may hold values from -0.0625 to 0.0625
- w_down: bfloat16 [4096, 7168], P('tp'), may hold values from -0.125 to 0.125
- expert_ids: int32 [2048, 8], P(('group', 'tp')), parts along dimension 0, may hold values from 0 to 255, as said below
- gate_weights: float32 [2048, 8], P(('group', 'tp')), parts along dimension 0, may hold values from 0.2 to 2
Outputs:
- routed: bfloat16 [2048, 7168], P(('group', 'tp')), parts along dimension 0
There are 2 independent parts, one for each index of `group`. A program takes and returns all parts, laid end to end along the dimension named above; an argument that names none is the same for every part. Nothing has to cross between parts.
Inputs may be any that keep to these rules, and one draw needn't show every extreme that they name: `expert_ids`: each row names 8 different experts, two from each of 4 different nodes, the node of an expert being its id divided by 32. Among the rows of one device, each expert k * 32 with k < 2 is named by at least one and at most 8 rows, and in every draw one of these experts is named by exactly 8 rows of every device. No row names more than two of these experts.
All inputs are finite; a program needn't handle non-finite values.
Results may differ from a plain program's by a relative error of at most 0.007.
Values may be sent and summed in bfloat16 or wider, within the bound.
No kernel may reach another device: no remote copies, remote signals or barrier semaphores. Data moves between devices by JAX's collectives and lax.ppermute only.
A program may use at most 128 MiB of HBM per device.

v0:
```python
import jax
import jax.numpy as jnp
from jax import lax
from jax.sharding import PartitionSpec as P

EXPERTS = 256
NODES = 8
SPLIT = 8
CAP = 8


epsilon = 1e-06


def expert_block(row_block, w_gate, w_up, w_down):
    leading = row_block.shape[:-1]
    flattened = row_block.reshape(-1, row_block.shape[-1])
    gated_pre = jnp.dot(flattened, w_gate, preferred_element_type=jnp.float32)
    up_pre = jnp.dot(flattened, w_up, preferred_element_type=jnp.float32)
    active = (jax.nn.silu(gated_pre) * up_pre).astype(jnp.bfloat16)
    partial_out = jnp.dot(active, w_down, preferred_element_type=jnp.float32).astype(jnp.bfloat16)
    return partial_out.reshape(leading + (w_down.shape[1],))


def local(states, norm_gain, w_gate, w_up, w_down, expert_ids, gate_weights):
    model_width = states.shape[1]
    dev_count = lax.axis_size("tp")
    wave_count = dev_count // SPLIT
    squares = jnp.mean(jnp.square(states.astype(jnp.float32)), axis=1, keepdims=True)
    normed = (states.astype(jnp.float32) * lax.rsqrt(squares + epsilon) * norm_gain).astype(
        jnp.bfloat16
    )
    targets = jnp.arange(wave_count, dtype=jnp.int32) * (EXPERTS // NODES)
    matched = expert_ids[:, :, None] == targets[None, None, :]
    weight_hit = jnp.sum(jnp.where(matched, gate_weights[:, :, None], 0.0), axis=1)
    hit_mask = jnp.any(matched, axis=1).astype(jnp.int32)
    slot_pos = jnp.cumsum(hit_mask, axis=0) - 1
    slot_ids = jnp.arange(CAP, dtype=jnp.int32)
    selector = (hit_mask.T[:, None, :] == 1) & (slot_pos.T[:, None, :] == slot_ids[None, :, None])
    packed = jnp.einsum(
        "kct,td->ckd", selector.astype(jnp.bfloat16), normed, preferred_element_type=jnp.float32
    ).astype(jnp.bfloat16)
    weighted = jnp.where(selector, weight_hit.T[:, None, :], 0.0)
    copies = jnp.broadcast_to(packed[:, :, None, :], (CAP, wave_count, SPLIT, model_width))
    copies = copies.reshape(CAP, dev_count, model_width)
    partial_out = expert_block(
        lax.all_to_all(copies, "tp", split_axis=1, concat_axis=1, tiled=True), w_gate, w_up, w_down
    )
    returned = lax.all_to_all(partial_out, "tp", split_axis=1, concat_axis=1, tiled=True)
    summed = returned.reshape(CAP, wave_count, SPLIT, model_width).astype(jnp.float32).sum(axis=2)
    routed = jnp.einsum("kct,ckd->td", weighted, summed, precision=lax.Precision.HIGHEST)
    return routed.astype(jnp.bfloat16)


def solution(mesh):
    in_specs = (
        P(("group", "tp"), None),
        P(),
        P(None, "tp"),
        P(None, "tp"),
        P("tp", None),
        P(("group", "tp"), None),
        P(("group", "tp"), None),
    )
    out_specs = P(("group", "tp"), None)
    return jax.shard_map(local, mesh=mesh, in_specs=in_specs, out_specs=out_specs, check_vma=False)
```

profile of v0, /device:TPU:15, one launch (start us, length us, event | category | flops | bytes accessed | tf_op | source)
XLA Modules:
  0.0 115.3 jit_solution(14194490852027498219)
XLA Ops:
  0.0 0.8 compare_reduce_fusion
  0.8 0.1 copy.28
  0.9 0.1 reduce_window_sum.11
  1.0 0.1 copy.29
  1.1 1.5 %fusion.2 = f32[64]{0:T(128)S(1)} fusion(bf16[64,7168]{1,0:T(8,128)(2,1)} %param.7), kind=kLoop, calls=%fused_computation.8 | loop fusion | flops 1376192 | bytes 917760 | tf_op jit(solution)/shard_map/reduce_sum | solution.py:29
  2.5 1.6 %fusion.1 = bf16[8,2,7168]{2,0,1:T(8,128)(2,1)S(1)} fusion(bf16[64,7168]{1,0:T(8,128)(2,1)} %param.7, f32[7168]{0:T(1024)} %param.8, f32[64]{0:T(128)S(1)} %add_rsqrt_fusion, s32[2,64]{1,0:T(2,128)S(1)} %copy.29, pred[2,64]{1,0:T(4,128)(4,1)S(1)} %get-tuple-element.5), kind=kOutput, calls=%fused_computation.4 | convolution fusion | flops 16631808 | bytes 1176448 | tf_op jit(solution)/shard_map/kct,td->ckd/dot_general | solution.py:40
  4.1 0.2 broadcast_in_dim.43
  4.3 48.0 %all_to_all.10 = bf16[8,16,7168]{2,0,1:T(8,128)(2,1)S(1)} all-to-all(bf16[8,16,7168]{2,0,1:T(8,128)(2,1)S(1)} %bitcast.28), channel_id=1, replica_groups=mesh['group'=2,'tp'=16] {'tp'}, dimensions={1} | all-to-all | bytes 3670016 | tf_op jit(solution)/shard_map/all_to_all | solution.py:47
  52.4 0.0 copy-start
  52.4 1.0 copy.30
  53.4 1.0 copy-done
  54.4 0.7 fusion.29
  55.1 6.5 %convolution_convert_fusion = bf16[128,7168]{1,0:T(8,128)(2,1)} fusion(bf16[256,7168]{1,0:T(8,128)(2,1)} %param.11, bf16[128,7168]{1,0:T(8,128)(2,1)S(1)} %bitcast.27, bf16[7168,256]{1,0:T(8,128)(2,1)} %param.10, f32[128,256]{1,0:T(8,128)S(1)} %fusion.29), kind=kOutput, calls=%fused_computation | convolution fusion | flops 940638208 | bytes 11141120 | tf_op jit(solution)/shard_map/dot_general | solution.py:21
  61.7 3.7 %copy.31 = bf16[8,16,7168]{2,0,1:T(8,128)(2,1)} copy(bf16[8,16,7168]{2,1,0:T(8,128)(2,1)} %bitcast.29) | data formatting | bytes 3670016 | tf_op jit(solution)/shard_map/reshape | solution.py:22
  65.4 0.0 copy-start.1
  65.4 0.0 copy-start.2
  65.4 5.2 %all-to-all-start.1 = ((bf16[8,16,7168]{2,0,1:T(8,128)(2,1)}), bf16[8,16,7168]{2,0,1:T(8,128)(2,1)S(1)}, u32[]{:S(2)}, u32[]{:S(2)}) async-start(bf16[8,16,7168]{2,0,1:T(8,128)(2,1)} %copy.31), calls=%async_computation.1 | async-start | bytes 3670016 | tf_op jit(solution)/shard_map/all_to_all | solution.py:49
  70.6 0.0 copy-done.1
  70.6 0.0 copy-done.2
  70.7 0.1 fusion.16
  70.7 41.7 %all-to-all-done.1 = bf16[8,16,7168]{2,0,1:T(8,128)(2,1)S(1)} async-done(((bf16[8,16,7168]{2,0,1:T(8,128)(2,1)}), bf16[8,16,7168]{2,0,1:T(8,128)(2,1)S(1)}, u32[]{:S(2)}, u32[]{:S(2)}) %all-to-all-start.1) | async-done | bytes 1835040 | tf_op jit(solution)/shard_map/all_to_all | solution.py:49
  112.4 0.3 convert_reduce_fusion
  112.7 2.6 %fusion = bf16[64,7168]{1,0:T(8,128)(2,1)} fusion(f32[8,2,7168]{2,0,1:T(8,128)S(1)} %convert_reduce_fusion, f32[2,64]{1,0:T(2,128)S(1)} %bitcast.30, s32[2,64]{1,0:T(2,128)S(1)} %copy.29, pred[2,64]{1,0:T(4,128)(4,1)S(1)} %get-tuple-element.5), kind=kOutput, calls=%fused_computation.2 | convolution fusion | flops 88542208 | bytes 1377408 | tf_op jit(solution)/shard_map/kct,ckd->td/dot_general | solution.py:51
  (4 shorter events, 0.0 us)
Async XLA Ops:
  52.4 2.0 %copy-start = (bf16[7168,256]{1,0:T(8,128)(2,1)S(1)}, bf16[7168,256]{1,0:T(8,128)(2,1)}, u32[]{:S(2)}) copy-start(bf16[7168,256]{1,0:T(8,128)(2,1)} %param.9) | copy-start | bytes 11010052
  65.4 5.2 %copy-start.1 = (s32[64,8]{0,1:T(8,128)S(1)}, s32[64,8]{0,1:T(8,128)}, u32[]{:S(2)}) copy-start(s32[64,8]{0,1:T(8,128)} %param.12) | copy-start | bytes 6148
  65.4 5.2 %copy-start.2 = (f32[64,8]{0,1:T(8,128)S(1)}, f32[64,8]{0,1:T(8,128)}, u32[]{:S(2)}) copy-start(f32[64,8]{0,1:T(8,128)} %param.13) | copy-start | bytes 6148
  65.4 47.0 %all-to-all-start.1 = ((bf16[8,16,7168]{2,0,1:T(8,128)(2,1)}), bf16[8,16,7168]{2,0,1:T(8,128)(2,1)S(1)}, u32[]{:S(2)}, u32[]{:S(2)}) async-start(bf16[8,16,7168]{2,0,1:T(8,128)(2,1)} %copy.31), calls=%async_computation.1 | async-start | bytes 3670016 | tf_op jit(solution)/shard_map/all_to_all | solution.py:49
where the time goes:
time: 116 us; the launch traced here: 115 us
  blocking collectives  48 us (41%)
  waiting for transfers between devices  41.7 us (36%)
  matrix products  11.4 us (10%)
  local copies, waits for them, and re-layouts  6.13 us (5%)
  starting transfers between devices  5.22 us (4%)
  other arithmetic  2.7 us (2%)
    all_to_all x1, blocking collectives, local(): lax.all_to_all(copies, 'tp', split_axis=1, concat_axis=1, tiled=True)  48 us
    all_to_all x1, waiting for transfers between devices, local(): lax.all_to_all(partial_out, 'tp', split_axis=1, concat_axis=1, tiled=True)  41.7 us
    dot_general x1, matrix products, expert_block(): jnp.dot(active, w_down, preferred_element_type=jnp.float32)  6.55 us
    all_to_all x1, starting transfers between devices, local(): lax.all_to_all(partial_out, 'tp', split_axis=1, concat_axis=1, tiled=True)  5.22 us
    reshape x1, local copies, waits for them, and re-layouts, expert_block(): return partial_out.reshape(leading + (w_down.shape[1],))  3.74 us
    dot_general x1, matrix products, local(): jnp.einsum('kct,ckd->td', weighted, summed, precision=lax.Precision.HIGHEST)  2.56 us
  transfers between devices with their start and end apart: 1, of which 1 were waited for; matrix products, arithmetic and copies ran while one was open for 0% of the time, Pallas kernels for 0%

commit v1 on v0

v1 whole, which is shorter than its diff:
```python
import jax
import jax.numpy as jnp
from jax import lax
from jax.sharding import PartitionSpec as P

EXPERTS = 256
NODES = 8
SPLIT = 8
CAP = 8
EPSILON = 1e-06
SQUARE = (2, 4, 6)


def local(states, norm_gain, w_gate, w_up, w_down, expert_ids, gate_weights):
    width = states.shape[1]
    devices = lax.axis_size("tp")
    waves = devices // SPLIT
    me = lax.axis_index("tp")
    own = me // SPLIT

    def swap(x, mask):
        return lax.ppermute(x, "tp", [(i, i ^ mask) for i in range(devices)])

    targets = (own ^ jnp.arange(waves, dtype=jnp.int32)) * (EXPERTS // NODES)
    matched = expert_ids[:, :, None] == targets[None, None, :]
    score = jnp.sum(jnp.where(matched, gate_weights[:, :, None], 0.0), axis=1)
    hit = jnp.any(matched, axis=1).astype(jnp.int32)
    position = jnp.cumsum(hit, axis=0) - 1
    slots = jnp.arange(CAP, dtype=jnp.int32)
    selector = (hit.T[:, None, :] == 1) & (position.T[:, None, :] == slots[None, :, None])
    rows = jnp.einsum(
        "kct,td->kcd", selector.astype(jnp.bfloat16), states, preferred_element_type=jnp.float32
    )
    squares = jnp.mean(jnp.square(rows), axis=2, keepdims=True)
    packed = (rows * lax.rsqrt(squares + EPSILON) * norm_gain).astype(jnp.bfloat16)
    cross = [SPLIT * j + 4 for j in range(1, waves)]

    blocks = []
    for j in range(waves):
        block = packed[j] if j == 0 else swap(packed[j], cross[j - 1])
        blocks += [block] + [swap(block, s) for s in SQUARE]
    mine = jnp.concatenate(blocks, axis=0)
    theirs = swap(mine, 1)
    both = jnp.concatenate([mine, theirs], axis=0)

    gated = jnp.dot(both, w_gate, preferred_element_type=jnp.float32)
    up = jnp.dot(both, w_up, preferred_element_type=jnp.float32)
    hidden = (jax.nn.silu(gated) * up).astype(jnp.bfloat16)
    half = hidden.shape[0] // 2
    theirs_out = jnp.dot(hidden[half:], w_down, preferred_element_type=jnp.float32).astype(jnp.bfloat16)
    back = swap(theirs_out, 1)
    mine_out = jnp.dot(hidden[:half], w_down, preferred_element_type=jnp.float32)
    pair = (mine_out + back.astype(jnp.float32)).astype(jnp.bfloat16)
    pair = pair.reshape(waves, 1 + len(SQUARE), CAP, width)

    results = [None] * waves
    for j in list(range(1, waves)) + [0]:
        total = pair[j, 0].astype(jnp.float32)
        for n, s in enumerate(SQUARE):
            total = total + swap(pair[j, n + 1], s).astype(jnp.float32)
        if j:
            total = swap(total.astype(jnp.bfloat16), cross[j - 1]).astype(jnp.float32)
        results[j] = total
    summed = jnp.stack(results)
    weighted = jnp.where(selector, score.T[:, None, :], 0.0)
    routed = jnp.einsum("kct,kcd->td", weighted, summed, precision=lax.Precision.HIGHEST)
    return routed.astype(jnp.bfloat16)


def solution(mesh):
    rows = P(("group", "tp"), None)
    in_specs = (rows, P(), P(None, "tp"), P(None, "tp"), P("tp", None), rows, rows)
    return jax.shard_map(local, mesh=mesh, in_specs=in_specs, out_specs=rows, check_vma=False)
```

time: 116 us -> 59.3 us (0.51)
  the two profiles are of different devices: /device:TPU:15 before, /device:TPU:0 now
where the time goes in v1:
time: 59.3 us; the launch traced here: 59 us
  waiting for transfers between devices  27.1 us (46%)
  starting transfers between devices  20.6 us (35%)
  matrix products  5.69 us (10%)
  local copies, waits for them, and re-layouts  3.26 us (5%)
  other arithmetic  2.07 us (3%)
    ppermute x16, waiting for transfers between devices, swap(): return lax.ppermute(x, 'tp', [(i, i ^ mask) for i in range(devices)])  27.1 us
    ppermute x16, starting transfers between devices, swap(): return lax.ppermute(x, 'tp', [(i, i ^ mask) for i in range(devices)])  20.6 us
    unnamed x19, local copies, waits for them, and re-layouts  2.95 us
    dot_general x1, matrix products, local(): jnp.einsum('kct,kcd->td', weighted, summed, precision=lax.Precision.HIGHEST)  2.57 us
  transfers between devices with their start and end apart: 16, of which 12 were waited for; matrix products, arithmetic and copies ran while one was open for 0% of the time, Pallas kernels for 0%

profile of v1, /device:TPU:0, one launch (start us, length us, event | category | flops | bytes accessed | tf_op | source)
XLA Modules:
  0.0 59.0 jit_solution(18169096767486983075)
XLA Ops:
  0.0 0.9 %compare_reduce_fusion = pred[64,2]{0,1:T(4,128)(4,1)S(1)} fusion(s32[64,8]{0,1:T(8,128)} %param.12, s32[2]{0:T(128)S(1)} %xor_multiply_fusion), kind=kLoop, calls=%fused_computation.53 | loop fusion | flops 1920 | bytes 2184 | tf_op jit(solution)/shard_map/reduce_or | solution.py:27
  1.5 0.9 %multiply_convert_fusion = bf16[2,8,7168]{2,1,0:T(8,128)(2,1)S(1)} fusion(f32[2,8,7168]{2,1,0:T(8,128)S(1)} %get-tuple-element.34, f32[7168]{0:T(1024)} %param.8, f32[2,8]{1,0:T(2,128)S(1)} %add_rsqrt_fusion), kind=kLoop, calls=%fused_computation.9 | loop fusion | flops 344064 | bytes 716864 | tf_op jit(solution)/shard_map/convert_element_type | solution.py:35
  2.4 3.0 %collective-permute-start = (bf16[8,7168]{1,0:T(8,128)(2,1)S(1)}, bf16[8,7168]{1,0:T(8,128)(2,1)S(1)}, u32[]{:S(2)}, u32[]{:S(2)}) collective-permute-start(bf16[8,7168]{1,0:T(8,128)(2,1)S(1)} %get-tuple-element.16), channel_id=1, source_target_pairs={{0,2},{1,3},{2,0},{3,1},{4,6},{5,7},{6,4},{7,5},{8,10},{9,11},{10,... | collective-permute-start | bytes 344072 | tf_op jit(solution)/shard_map/ppermute | solution.py:22
  5.5 1.6 %collective-permute-start.1 = (bf16[8,7168]{1,0:T(8,128)(2,1)S(1)}, bf16[8,7168]{1,0:T(8,128)(2,1)S(1)}, u32[]{:S(2)}, u32[]{:S(2)}) collective-permute-start(bf16[8,7168]{1,0:T(8,128)(2,1)S(1)} %get-tuple-element.16), channel_id=1, source_target_pairs={{0,4},{1,5},{2,6},{3,7},{4,0},{5,1},{6,2},{7,3},{8,12},{9,13},{10,... | collective-permute-start | bytes 344072 | tf_op jit(solution)/shard_map/ppermute | solution.py:22
  7.0 4.0 %collective-permute-start.3 = (bf16[8,7168]{1,0:T(8,128)(2,1)S(1)}, bf16[8,7168]{1,0:T(8,128)(2,1)S(1)}, u32[]{:S(2)}, u32[]{:S(2)}) collective-permute-start(bf16[8,7168]{1,0:T(8,128)(2,1)S(1)} %get-tuple-element.15), channel_id=1, source_target_pairs={{0,12},{1,13},{2,14},{3,15},{4,8},{5,9},{6,10},{7,11},{8,4},{9,5},... | collective-permute-start | bytes 344072 | tf_op jit(solution)/shard_map/ppermute | solution.py:22
  11.1 6.0 %collective-permute-done.3 = bf16[8,7168]{1,0:T(8,128)(2,1)S(1)} collective-permute-done((bf16[8,7168]{1,0:T(8,128)(2,1)S(1)}, bf16[8,7168]{1,0:T(8,128)(2,1)S(1)}, u32[]{:S(2)}, u32[]{:S(2)}) %collective-permute-start.3) | collective-permute-done | bytes 114720 | tf_op jit(solution)/shard_map/ppermute | solution.py:22
  17.0 0.7 %collective-permute-start.4 = (bf16[8,7168]{1,0:T(8,128)(2,1)S(1)}, bf16[8,7168]{1,0:T(8,128)(2,1)S(1)}, u32[]{:S(2)}, u32[]{:S(2)}) collective-permute-start(bf16[8,7168]{1,0:T(8,128)(2,1)S(1)} %collective-permute-done.3), channel_id=1, source_target_pairs={{0,2},{1,3},{2,0},{3,1},{4,6},{5,7},{6,4},{7,5},{8,10},{9,11},{10,... | collective-permute-start | bytes 344072 | tf_op jit(solution)/shard_map/ppermute | solution.py:22
  17.7 2.8 %collective-permute-start.6 = (bf16[8,7168]{1,0:T(8,128)(2,1)S(1)}, bf16[8,7168]{1,0:T(8,128)(2,1)S(1)}, u32[]{:S(2)}, u32[]{:S(2)}) collective-permute-start(bf16[8,7168]{1,0:T(8,128)(2,1)S(1)} %collective-permute-done.3), channel_id=1, source_target_pairs={{0,6},{1,7},{2,4},{3,5},{4,2},{5,3},{6,0},{7,1},{8,14},{9,15},{10,... | collective-permute-start | bytes 344072 | tf_op jit(solution)/shard_map/ppermute | solution.py:22
  20.6 2.3 %collective-permute-done.4 = bf16[8,7168]{1,0:T(8,128)(2,1)S(1)} collective-permute-done((bf16[8,7168]{1,0:T(8,128)(2,1)S(1)}, bf16[8,7168]{1,0:T(8,128)(2,1)S(1)}, u32[]{:S(2)}, u32[]{:S(2)}) %collective-permute-start.4) | collective-permute-done | bytes 114720 | tf_op jit(solution)/shard_map/ppermute | solution.py:22
  23.0 1.6 %collective-permute-done.6 = bf16[8,7168]{1,0:T(8,128)(2,1)S(1)} collective-permute-done((bf16[8,7168]{1,0:T(8,128)(2,1)S(1)}, bf16[8,7168]{1,0:T(8,128)(2,1)S(1)}, u32[]{:S(2)}, u32[]{:S(2)}) %collective-permute-start.6) | collective-permute-done | bytes 114720 | tf_op jit(solution)/shard_map/ppermute | solution.py:22
  24.6 2.5 %collective-permute-done.7 = bf16[64,7168]{1,0:T(8,128)(2,1)S(1)} collective-permute-done((bf16[64,7168]{1,0:T(8,128)(2,1)S(1)}, bf16[64,7168]{1,0:T(8,128)(2,1)S(1)}, u32[]{:S(2)}, u32[]{:S(2)}) %collective-permute-start.7) | collective-permute-done | bytes 917536 | tf_op jit(solution)/shard_map/ppermute | solution.py:22
  27.2 0.6 %fusion.30 = f32[128,256]{1,0:T(8,128)S(1)} fusion(bf16[128,7168]{1,0:T(8,128)(2,1)S(1)} %constant_dynamic-update-slice_fusion.8, bf16[7168,256]{1,0:T(8,128)(2,1)S(1)} %copy-done.2), kind=kOutput, calls=%fused_computation.69 | convolution fusion | flops 469762048 | bytes 5636096 | tf_op jit(solution)/shard_map/dot_general | solution.py:46
  27.8 1.4 %copy-done.3 = bf16[7168,256]{1,0:T(8,128)(2,1)S(1)} copy-done((bf16[7168,256]{1,0:T(8,128)(2,1)S(1)}, bf16[7168,256]{1,0:T(8,128)(2,1)}, u32[]{:S(2)}) %copy-start.3) | copy-done | bytes 3670040
  29.2 0.6 %multiply_convert_fusion.1 = bf16[128,256]{1,0:T(8,128)(2,1)S(1)} fusion(f32[128,256]{1,0:T(8,128)S(1)} %fusion.30, bf16[128,7168]{1,0:T(8,128)(2,1)S(1)} %constant_dynamic-update-slice_fusion.8, bf16[7168,256]{1,0:T(8,128)(2,1)S(1)} %copy-done.3), kind=kOutput, calls=%fused_computation.19 | convolution fusion | flops 469958656 | bytes 5701632 | tf_op jit(solution)/shard_map/dot_general | solution.py:47
  29.8 1.4 %copy-done.1 = bf16[256,7168]{1,0:T(8,128)(2,1)S(1)} copy-done((bf16[256,7168]{1,0:T(8,128)(2,1)S(1)}, bf16[256,7168]{1,0:T(8,128)(2,1)}, u32[]{:S(2)}) %copy-start.1) | copy-done | bytes 3670040
  31.2 0.8 %convolution_convert_fusion = bf16[64,7168]{1,0:T(8,128)(2,1)S(1)} fusion(bf16[256,7168]{1,0:T(8,128)(2,1)S(1)} %copy-done.1, bf16[128,256]{1,0:T(8,128)(2,1)S(1)} %multiply_convert_fusion.1), kind=kOutput, calls=%fused_computation.2 | convolution fusion | flops 235339776 | bytes 4620288 | tf_op jit(solution)/shard_map/dot_general | solution.py:50
  32.2 2.3 %collective-permute-done.8 = bf16[64,7168]{1,0:T(8,128)(2,1)S(1)} collective-permute-done((bf16[64,7168]{1,0:T(8,128)(2,1)S(1)}, bf16[64,7168]{1,0:T(8,128)(2,1)S(1)}, u32[]{:S(2)}, u32[]{:S(2)}) %collective-permute-start.8) | collective-permute-done | bytes 917536 | tf_op jit(solution)/shard_map/ppermute | solution.py:22
  34.5 0.8 %add_convert_fusion = bf16[64,7168]{1,0:T(8,128)(2,1)S(1)} fusion(bf16[64,7168]{1,0:T(8,128)(2,1)S(1)} %collective-permute-done.8, bf16[256,7168]{1,0:T(8,128)(2,1)S(1)} %copy-done.1, bf16[128,256]{1,0:T(8,128)(2,1)S(1)} %multiply_convert_fusion.1), kind=kOutput, calls=%fused_computation.3 | convolution fusion | flops 236257280 | bytes 5537792 | tf_op jit(solution)/shard_map/dot_general | solution.py:52
  35.4 1.0 %collective-permute-start.10 = (bf16[8,7168]{1,0:T(8,128)(2,1)S(1)}, bf16[8,7168]{1,0:T(8,128)(2,1)S(1)}, u32[]{:S(2)}, u32[]{:S(2)}) collective-permute-start(bf16[8,7168]{1,0:T(8,128)(2,1)S(1)} %get-tuple-element.12), channel_id=1, source_target_pairs={{0,4},{1,5},{2,6},{3,7},{4,0},{5,1},{6,2},{7,3},{8,12},{9,13},{10,... | collective-permute-start | bytes 344072 | tf_op jit(solution)/shard_map/ppermute | solution.py:22
  36.3 1.2 %collective-permute-start.11 = (bf16[8,7168]{1,0:T(8,128)(2,1)S(1)}, bf16[8,7168]{1,0:T(8,128)(2,1)S(1)}, u32[]{:S(2)}, u32[]{:S(2)}) collective-permute-start(bf16[8,7168]{1,0:T(8,128)(2,1)S(1)} %get-tuple-element.11), channel_id=1, source_target_pairs={{0,6},{1,7},{2,4},{3,5},{4,2},{5,3},{6,0},{7,1},{8,14},{9,15},{10,... | collective-permute-start | bytes 344072 | tf_op jit(solution)/shard_map/ppermute | solution.py:22
  37.6 1.3 %collective-permute-start.12 = (bf16[8,7168]{1,0:T(8,128)(2,1)S(1)}, bf16[8,7168]{1,0:T(8,128)(2,1)S(1)}, u32[]{:S(2)}, u32[]{:S(2)}) collective-permute-start(bf16[8,7168]{1,0:T(8,128)(2,1)S(1)} %get-tuple-element.10), channel_id=1, source_target_pairs={{0,2},{1,3},{2,0},{3,1},{4,6},{5,7},{6,4},{7,5},{8,10},{9,11},{10,... | collective-permute-start | bytes 344072 | tf_op jit(solution)/shard_map/ppermute | solution.py:22
  38.9 0.9 %collective-permute-start.13 = (bf16[8,7168]{1,0:T(8,128)(2,1)S(1)}, bf16[8,7168]{1,0:T(8,128)(2,1)S(1)}, u32[]{:S(2)}, u32[]{:S(2)}) collective-permute-start(bf16[8,7168]{1,0:T(8,128)(2,1)S(1)} %get-tuple-element.9), channel_id=1, source_target_pairs={{0,4},{1,5},{2,6},{3,7},{4,0},{5,1},{6,2},{7,3},{8,12},{9,13},{10,... | collective-permute-start | bytes 344072 | tf_op jit(solution)/shard_map/ppermute | solution.py:22
  39.8 1.2 %collective-permute-start.14 = (bf16[8,7168]{1,0:T(8,128)(2,1)S(1)}, bf16[8,7168]{1,0:T(8,128)(2,1)S(1)}, u32[]{:S(2)}, u32[]{:S(2)}) collective-permute-start(bf16[8,7168]{1,0:T(8,128)(2,1)S(1)} %get-tuple-element.8), channel_id=1, source_target_pairs={{0,6},{1,7},{2,4},{3,5},{4,2},{5,3},{6,0},{7,1},{8,14},{9,15},{10,... | collective-permute-start | bytes 344072 | tf_op jit(solution)/shard_map/ppermute | solution.py:22
  41.1 0.4 collective-permute-done.10
  41.4 1.0 %collective-permute-start.9 = (bf16[8,7168]{1,0:T(8,128)(2,1)S(1)}, bf16[8,7168]{1,0:T(8,128)(2,1)S(1)}, u32[]{:S(2)}, u32[]{:S(2)}) collective-permute-start(bf16[8,7168]{1,0:T(8,128)(2,1)S(1)} %get-tuple-element.7), channel_id=1, source_target_pairs={{0,2},{1,3},{2,0},{3,1},{4,6},{5,7},{6,4},{7,5},{8,10},{9,11},{10,... | collective-permute-start | bytes 344072 | tf_op jit(solution)/shard_map/ppermute | solution.py:22
  42.4 1.6 %collective-permute-done.11 = bf16[8,7168]{1,0:T(8,128)(2,1)S(1)} collective-permute-done((bf16[8,7168]{1,0:T(8,128)(2,1)S(1)}, bf16[8,7168]{1,0:T(8,128)(2,1)S(1)}, u32[]{:S(2)}, u32[]{:S(2)}) %collective-permute-start.11) | collective-permute-done | bytes 114720 | tf_op jit(solution)/shard_map/ppermute | solution.py:22
  44.0 2.2 %collective-permute-done.12 = bf16[8,7168]{1,0:T(8,128)(2,1)S(1)} collective-permute-done((bf16[8,7168]{1,0:T(8,128)(2,1)S(1)}, bf16[8,7168]{1,0:T(8,128)(2,1)S(1)}, u32[]{:S(2)}, u32[]{:S(2)}) %collective-permute-start.12) | collective-permute-done | bytes 114720 | tf_op jit(solution)/shard_map/ppermute | solution.py:22
  46.3 1.9 %collective-permute-done.14 = bf16[8,7168]{1,0:T(8,128)(2,1)S(1)} collective-permute-done((bf16[8,7168]{1,0:T(8,128)(2,1)S(1)}, bf16[8,7168]{1,0:T(8,128)(2,1)S(1)}, u32[]{:S(2)}, u32[]{:S(2)}) %collective-permute-start.14) | collective-permute-done | bytes 114720 | tf_op jit(solution)/shard_map/ppermute | solution.py:22
  48.2 1.4 %collective-permute-done.9 = bf16[8,7168]{1,0:T(8,128)(2,1)S(1)} collective-permute-done((bf16[8,7168]{1,0:T(8,128)(2,1)S(1)}, bf16[8,7168]{1,0:T(8,128)(2,1)S(1)}, u32[]{:S(2)}, u32[]{:S(2)}) %collective-permute-start.9) | collective-permute-done | bytes 114720 | tf_op jit(solution)/shard_map/ppermute | solution.py:22
  49.7 1.6 %collective-permute-start.15 = (bf16[8,7168]{1,0:T(8,128)(2,1)S(1)}, bf16[8,7168]{1,0:T(8,128)(2,1)S(1)}, u32[]{:S(2)}, u32[]{:S(2)}) collective-permute-start(bf16[8,7168]{1,0:T(8,128)(2,1)S(1)} %get-tuple-element.6), channel_id=1, source_target_pairs={{0,12},{1,13},{2,14},{3,15},{4,8},{5,9},{6,10},{7,11},{8,4},{9,5},... | collective-permute-start | bytes 344072 | tf_op jit(solution)/shard_map/ppermute | solution.py:22
  51.3 5.1 %collective-permute-done.15 = bf16[8,7168]{1,0:T(8,128)(2,1)S(1)} collective-permute-done((bf16[8,7168]{1,0:T(8,128)(2,1)S(1)}, bf16[8,7168]{1,0:T(8,128)(2,1)S(1)}, u32[]{:S(2)}, u32[]{:S(2)}) %collective-permute-start.15) | collective-permute-done | bytes 114720 | tf_op jit(solution)/shard_map/ppermute | solution.py:22
  56.4 2.6 %fusion = bf16[64,7168]{1,0:T(8,128)(2,1)} fusion(f32[1,8,7168]{2,1,0:T(8,128)S(1)} %bitcast_convert_fusion, f32[1,8,7168]{2,1,0:T(8,128)S(1)} %get-tuple-element.5, f32[2,64]{1,0:T(2,128)S(1)} %bitcast.58, s32[2,64]{1,0:T(2,128)S(1)} %copy.13, pred[2,64]{1,0:T(4,128)(4,1)S(1)} %get-tuple-element.31), kind=kOutput, calls=%fused_computation.1 | convolution fusion | flops 88656896 | bytes 1377408 | tf_op jit(solution)/shard_map/kct,kcd->td/dot_general | solution.py:66
  (41 shorter events, 1.6 us)
Async XLA Ops:
  0.0 1.2 %copy-start = (bf16[64,7168]{1,0:T(8,128)(2,1)S(1)}, bf16[64,7168]{1,0:T(8,128)(2,1)}, u32[]{:S(2)}) copy-start(bf16[64,7168]{1,0:T(8,128)(2,1)} %param.7) | copy-start | bytes 2752516
  2.4 15.3 %collective-permute-start = (bf16[8,7168]{1,0:T(8,128)(2,1)S(1)}, bf16[8,7168]{1,0:T(8,128)(2,1)S(1)}, u32[]{:S(2)}, u32[]{:S(2)}) collective-permute-start(bf16[8,7168]{1,0:T(8,128)(2,1)S(1)} %get-tuple-element.16), channel_id=1, source_target_pairs={{0,2},{1,3},{2,0},{3,1},{4,6},{5,7},{6,4},{7,5},{8,10},{9,11},{10,... | collective-permute-start | bytes 344072 | tf_op jit(solution)/shard_map/ppermute | solution.py:22
  5.5 15.1 %collective-permute-start.1 = (bf16[8,7168]{1,0:T(8,128)(2,1)S(1)}, bf16[8,7168]{1,0:T(8,128)(2,1)S(1)}, u32[]{:S(2)}, u32[]{:S(2)}) collective-permute-start(bf16[8,7168]{1,0:T(8,128)(2,1)S(1)} %get-tuple-element.16), channel_id=1, source_target_pairs={{0,4},{1,5},{2,6},{3,7},{4,0},{5,1},{6,2},{7,3},{8,12},{9,13},{10,... | collective-permute-start | bytes 344072 | tf_op jit(solution)/shard_map/ppermute | solution.py:22
  7.0 13.5 %collective-permute-start.2 = (bf16[8,7168]{1,0:T(8,128)(2,1)S(1)}, bf16[8,7168]{1,0:T(8,128)(2,1)S(1)}, u32[]{:S(2)}, u32[]{:S(2)}) collective-permute-start(bf16[8,7168]{1,0:T(8,128)(2,1)S(1)} %get-tuple-element.16), channel_id=1, source_target_pairs={{0,6},{1,7},{2,4},{3,5},{4,2},{5,3},{6,0},{7,1},{8,14},{9,15},{10,... | collective-permute-start | bytes 344072 | tf_op jit(solution)/shard_map/ppermute | solution.py:22
  7.0 10.0 %collective-permute-start.3 = (bf16[8,7168]{1,0:T(8,128)(2,1)S(1)}, bf16[8,7168]{1,0:T(8,128)(2,1)S(1)}, u32[]{:S(2)}, u32[]{:S(2)}) collective-permute-start(bf16[8,7168]{1,0:T(8,128)(2,1)S(1)} %get-tuple-element.15), channel_id=1, source_target_pairs={{0,12},{1,13},{2,14},{3,15},{4,8},{5,9},{6,10},{7,11},{8,4},{9,5},... | collective-permute-start | bytes 344072 | tf_op jit(solution)/shard_map/ppermute | solution.py:22
  17.0 5.9 %collective-permute-start.4 = (bf16[8,7168]{1,0:T(8,128)(2,1)S(1)}, bf16[8,7168]{1,0:T(8,128)(2,1)S(1)}, u32[]{:S(2)}, u32[]{:S(2)}) collective-permute-start(bf16[8,7168]{1,0:T(8,128)(2,1)S(1)} %collective-permute-done.3), channel_id=1, source_target_pairs={{0,2},{1,3},{2,0},{3,1},{4,6},{5,7},{6,4},{7,5},{8,10},{9,11},{10,... | collective-permute-start | bytes 344072 | tf_op jit(solution)/shard_map/ppermute | solution.py:22
  17.7 5.2 %collective-permute-start.5 = (bf16[8,7168]{1,0:T(8,128)(2,1)S(1)}, bf16[8,7168]{1,0:T(8,128)(2,1)S(1)}, u32[]{:S(2)}, u32[]{:S(2)}) collective-permute-start(bf16[8,7168]{1,0:T(8,128)(2,1)S(1)} %collective-permute-done.3), channel_id=1, source_target_pairs={{0,4},{1,5},{2,6},{3,7},{4,0},{5,1},{6,2},{7,3},{8,12},{9,13},{10,... | collective-permute-start | bytes 344072 | tf_op jit(solution)/shard_map/ppermute | solution.py:22
  17.7 6.8 %collective-permute-start.6 = (bf16[8,7168]{1,0:T(8,128)(2,1)S(1)}, bf16[8,7168]{1,0:T(8,128)(2,1)S(1)}, u32[]{:S(2)}, u32[]{:S(2)}) collective-permute-start(bf16[8,7168]{1,0:T(8,128)(2,1)S(1)} %collective-permute-done.3), channel_id=1, source_target_pairs={{0,6},{1,7},{2,4},{3,5},{4,2},{5,3},{6,0},{7,1},{8,14},{9,15},{10,... | collective-permute-start | bytes 344072 | tf_op jit(solution)/shard_map/ppermute | solution.py:22
  20.5 6.6 %copy-start.2 = (bf16[7168,256]{1,0:T(8,128)(2,1)S(1)}, bf16[7168,256]{1,0:T(8,128)(2,1)}, u32[]{:S(2)}) copy-start(bf16[7168,256]{1,0:T(8,128)(2,1)} %param.9) | copy-start | bytes 11010052
  24.5 2.5 %collective-permute-start.7 = (bf16[64,7168]{1,0:T(8,128)(2,1)S(1)}, bf16[64,7168]{1,0:T(8,128)(2,1)S(1)}, u32[]{:S(2)}, u32[]{:S(2)}) collective-permute-start(bf16[64,7168]{1,0:T(8,128)(2,1)S(1)} %get-tuple-element.17), channel_id=1, source_target_pairs={{0,1},{1,0},{2,3},{3,2},{4,5},{5,4},{6,7},{7,6},{8,9},{9,8},{10,11... | collective-permute-start | bytes 2752520 | tf_op jit(solution)/shard_map/ppermute | solution.py:22
  27.1 2.0 %copy-start.3 = (bf16[7168,256]{1,0:T(8,128)(2,1)S(1)}, bf16[7168,256]{1,0:T(8,128)(2,1)}, u32[]{:S(2)}) copy-start(bf16[7168,256]{1,0:T(8,128)(2,1)} %param.10) | copy-start | bytes 11010052
  29.2 2.0 %copy-start.1 = (bf16[256,7168]{1,0:T(8,128)(2,1)S(1)}, bf16[256,7168]{1,0:T(8,128)(2,1)}, u32[]{:S(2)}) copy-start(bf16[256,7168]{1,0:T(8,128)(2,1)} %param.11) | copy-start | bytes 11010052
  32.0 2.5 %collective-permute-start.8 = (bf16[64,7168]{1,0:T(8,128)(2,1)S(1)}, bf16[64,7168]{1,0:T(8,128)(2,1)S(1)}, u32[]{:S(2)}, u32[]{:S(2)}) collective-permute-start(bf16[64,7168]{1,0:T(8,128)(2,1)S(1)} %convolution_convert_fusion), channel_id=1, source_target_pairs={{0,1},{1,0},{2,3},{3,2},{4,5},{5,4},{6,7},{7,6},{8,9},{9,8},{10,11... | collective-permute-start | bytes 2752520 | tf_op jit(solution)/shard_map/ppermute | solution.py:22
  35.3 16.0 %copy-start.4 = (s32[64,8]{0,1:T(8,128)S(1)}, s32[64,8]{0,1:T(8,128)}, u32[]{:S(2)}) copy-start(s32[64,8]{0,1:T(8,128)} %param.12) | copy-start | bytes 6148
  35.3 16.0 %copy-start.5 = (f32[64,8]{0,1:T(8,128)S(1)}, f32[64,8]{0,1:T(8,128)}, u32[]{:S(2)}) copy-start(f32[64,8]{0,1:T(8,128)} %param.13) | copy-start | bytes 6148
  35.4 6.1 %collective-permute-start.10 = (bf16[8,7168]{1,0:T(8,128)(2,1)S(1)}, bf16[8,7168]{1,0:T(8,128)(2,1)S(1)}, u32[]{:S(2)}, u32[]{:S(2)}) collective-permute-start(bf16[8,7168]{1,0:T(8,128)(2,1)S(1)} %get-tuple-element.12), channel_id=1, source_target_pairs={{0,4},{1,5},{2,6},{3,7},{4,0},{5,1},{6,2},{7,3},{8,12},{9,13},{10,... | collective-permute-start | bytes 344072 | tf_op jit(solution)/shard_map/ppermute | solution.py:22
  36.3 7.6 %collective-permute-start.11 = (bf16[8,7168]{1,0:T(8,128)(2,1)S(1)}, bf16[8,7168]{1,0:T(8,128)(2,1)S(1)}, u32[]{:S(2)}, u32[]{:S(2)}) collective-permute-start(bf16[8,7168]{1,0:T(8,128)(2,1)S(1)} %get-tuple-element.11), channel_id=1, source_target_pairs={{0,6},{1,7},{2,4},{3,5},{4,2},{5,3},{6,0},{7,1},{8,14},{9,15},{10,... | collective-permute-start | bytes 344072 | tf_op jit(solution)/shard_map/ppermute | solution.py:22
  37.6 8.6 %collective-permute-start.12 = (bf16[8,7168]{1,0:T(8,128)(2,1)S(1)}, bf16[8,7168]{1,0:T(8,128)(2,1)S(1)}, u32[]{:S(2)}, u32[]{:S(2)}) collective-permute-start(bf16[8,7168]{1,0:T(8,128)(2,1)S(1)} %get-tuple-element.10), channel_id=1, source_target_pairs={{0,2},{1,3},{2,0},{3,1},{4,6},{5,7},{6,4},{7,5},{8,10},{9,11},{10,... | collective-permute-start | bytes 344072 | tf_op jit(solution)/shard_map/ppermute | solution.py:22
  38.9 7.4 %collective-permute-start.13 = (bf16[8,7168]{1,0:T(8,128)(2,1)S(1)}, bf16[8,7168]{1,0:T(8,128)(2,1)S(1)}, u32[]{:S(2)}, u32[]{:S(2)}) collective-permute-start(bf16[8,7168]{1,0:T(8,128)(2,1)S(1)} %get-tuple-element.9), channel_id=1, source_target_pairs={{0,4},{1,5},{2,6},{3,7},{4,0},{5,1},{6,2},{7,3},{8,12},{9,13},{10,... | collective-permute-start | bytes 344072 | tf_op jit(solution)/shard_map/ppermute | solution.py:22
  39.8 8.4 %collective-permute-start.14 = (bf16[8,7168]{1,0:T(8,128)(2,1)S(1)}, bf16[8,7168]{1,0:T(8,128)(2,1)S(1)}, u32[]{:S(2)}, u32[]{:S(2)}) collective-permute-start(bf16[8,7168]{1,0:T(8,128)(2,1)S(1)} %get-tuple-element.8), channel_id=1, source_target_pairs={{0,6},{1,7},{2,4},{3,5},{4,2},{5,3},{6,0},{7,1},{8,14},{9,15},{10,... | collective-permute-start | bytes 344072 | tf_op jit(solution)/shard_map/ppermute | solution.py:22
  41.4 8.2 %collective-permute-start.9 = (bf16[8,7168]{1,0:T(8,128)(2,1)S(1)}, bf16[8,7168]{1,0:T(8,128)(2,1)S(1)}, u32[]{:S(2)}, u32[]{:S(2)}) collective-permute-start(bf16[8,7168]{1,0:T(8,128)(2,1)S(1)} %get-tuple-element.7), channel_id=1, source_target_pairs={{0,2},{1,3},{2,0},{3,1},{4,6},{5,7},{6,4},{7,5},{8,10},{9,11},{10,... | collective-permute-start | bytes 344072 | tf_op jit(solution)/shard_map/ppermute | solution.py:22
  49.7 6.7 %collective-permute-start.15 = (bf16[8,7168]{1,0:T(8,128)(2,1)S(1)}, bf16[8,7168]{1,0:T(8,128)(2,1)S(1)}, u32[]{:S(2)}, u32[]{:S(2)}) collective-permute-start(bf16[8,7168]{1,0:T(8,128)(2,1)S(1)} %get-tuple-element.6), channel_id=1, source_target_pairs={{0,12},{1,13},{2,14},{3,15},{4,8},{5,9},{6,10},{7,11},{8,4},{9,5},... | collective-permute-start | bytes 344072 | tf_op jit(solution)/shard_map/ppermute | solution.py:22

commit v2 on v1

v2 whole, which is shorter than its diff:
```python
import functools

import jax
import jax.numpy as jnp
from jax import lax
from jax.experimental import pallas as pl
from jax.experimental.pallas import tpu as pltpu
from jax.sharding import PartitionSpec as P

EXPERTS = 256
NODES = 8
SPLIT = 8
CAP = 8
EPSILON = 1e-06
SQUARE = (2, 4, 6)
F32 = jnp.float32
BF16 = jnp.bfloat16
VMEM = pl.BlockSpec(memory_space=pltpu.VMEM)


def call(body, outs, flops, moved):
    return pl.pallas_call(
        body,
        out_shape=outs,
        compiler_params=pltpu.CompilerParams(vmem_limit_bytes=16 * 1024 * 1024),
        cost_estimate=pl.CostEstimate(flops=flops, bytes_accessed=moved, transcendentals=0),
    )


def normed(picked, states_ref, gain_ref):
    rows = jnp.dot(picked, states_ref[...], preferred_element_type=F32)
    squares = jnp.mean(rows * rows, axis=1, keepdims=True)
    return (rows * lax.rsqrt(squares + EPSILON) * gain_ref[...]).astype(BF16)


def pick_kernel(waves, states_ref, gain_ref, ids_ref, gates_ref, *outs):
    cross_refs, (own_ref, weighted_ref) = outs[:-2], outs[-2:]
    tokens = ids_ref.shape[1]
    own = lax.axis_index("tp") // SPLIT
    upper = lax.broadcasted_iota(jnp.int32, (tokens, tokens), 0)
    upper = (upper <= lax.broadcasted_iota(jnp.int32, (tokens, tokens), 1)).astype(F32).astype(BF16)
    slot = lax.broadcasted_iota(jnp.int32, (CAP, tokens), 0).astype(F32)
    for j in range(waves):
        target = lax.bitwise_xor(own, j) * (EXPERTS // NODES)
        matched = ids_ref[...] == target
        score = jnp.sum(jnp.where(matched, gates_ref[...], 0.0), axis=0, keepdims=True)
        hit = jnp.sum(jnp.where(matched, 1.0, 0.0), axis=0, keepdims=True)
        hits = jnp.broadcast_to(hit, (CAP, tokens))
        place = jnp.dot(hits.astype(BF16), upper, preferred_element_type=F32) - 1.0
        picked = jnp.where((hits > 0.5) & (place == slot), 1.0, 0.0)
        weighted_ref[CAP * j : CAP * (j + 1), :] = picked * score
        if j:
            cross_refs[j - 1][...] = normed(picked.astype(BF16), states_ref, gain_ref)
        else:
            own_ref[...] = picked


def own_kernel(picked_ref, states_ref, gain_ref, out_ref):
    out_ref[...] = normed(picked_ref[...].astype(BF16), states_ref, gain_ref)


def combine_kernel(waves, weighted_ref, *refs):
    pieces, out_ref = refs[:-1], refs[-1]
    own = pieces[0][...].astype(F32)
    for piece in pieces[1 : 1 + len(SQUARE)]:
        own = own + piece[...].astype(F32)
    rows = jnp.concatenate([own] + [p[...].astype(F32) for p in pieces[1 + len(SQUARE) :]], axis=0)
    high = rows.astype(BF16).astype(F32)
    rows = jnp.concatenate([high, high, rows - high], axis=0).astype(BF16)
    weights = weighted_ref[...]
    high = weights.astype(BF16).astype(F32)
    weights = jnp.concatenate([high, weights - high, high], axis=0).astype(BF16)
    out_ref[...] = lax.dot_general(
        weights, rows, (((0,), (0,)), ((), ())), preferred_element_type=F32
    ).astype(BF16)


def local(states, norm_gain, w_gate, w_up, w_down, expert_ids, gate_weights):
    tokens, width = states.shape
    devices = lax.axis_size("tp")
    waves = devices // SPLIT

    def swap(x, mask):
        return lax.ppermute(x, "tp", [(i, i ^ mask) for i in range(devices)])

    block = jax.ShapeDtypeStruct((CAP, width), BF16)
    gain = norm_gain[None, :]
    *cross, picked, weighted = call(
        functools.partial(pick_kernel, waves),
        [block] * (waves - 1)
        + [jax.ShapeDtypeStruct((CAP, tokens), F32), jax.ShapeDtypeStruct((CAP * waves, tokens), F32)],
        2 * tokens * width * CAP * (waves - 1),
        tokens * width * 2,
    )(states, gain, expert_ids.T, gate_weights.T)
    heads = [None] + [swap(x, SPLIT * j + 4) for j, x in enumerate(cross, 1)]
    heads[0] = call(own_kernel, block, 2 * tokens * width * CAP, tokens * width * 2)(picked, states, gain)

    hidden = []
    for j in range(waves):
        mine = jnp.concatenate([heads[j]] + [swap(heads[j], s) for s in SQUARE], axis=0)
        both = jnp.concatenate([mine, swap(mine, 1)], axis=0)
        gated = jnp.dot(both, w_gate, preferred_element_type=F32)
        up = jnp.dot(both, w_up, preferred_element_type=F32)
        hidden.append((jax.nn.silu(gated) * up).astype(BF16))

    results = []
    for j in list(range(1, waves)) + [0]:
        half = hidden[j].shape[0] // 2
        theirs = jnp.dot(hidden[j][half:], w_down, preferred_element_type=F32).astype(BF16)
        back = swap(theirs, 1)
        mine = jnp.dot(hidden[j][:half], w_down, preferred_element_type=F32)
        pair = (mine + back.astype(F32)).astype(BF16)
        parts = [pair[:CAP]] + [swap(pair[CAP * n : CAP * (n + 1)], s) for n, s in enumerate(SQUARE, 1)]
        if j:
            total = parts[0].astype(F32)
            for part in parts[1:]:
                total = total + part.astype(F32)
            results.append(swap(total.astype(BF16), SPLIT * j + 4))
        else:
            results = parts + results
    return call(
        functools.partial(combine_kernel, waves),
        jax.ShapeDtypeStruct((tokens, width), BF16),
        6 * tokens * width * CAP * waves,
        tokens * width * 4,
    )(weighted, *results)


def solution(mesh):
    rows = P(("group", "tp"), None)
    in_specs = (rows, P(), P(None, "tp"), P(None, "tp"), P("tp", None), rows, rows)
    return jax.shard_map(local, mesh=mesh, in_specs=in_specs, out_specs=rows, check_vma=False)
```

time: 59.3 us -> 54.3 us (0.916)
  waiting for transfers between devices: 27.1 us -> 18.3 us
  starting transfers between devices: 20.6 us -> 23.3 us
  Pallas kernels: 0 us -> 2.2 us
  other arithmetic: 2.07 us -> 0.14 us
  local copies, waits for them, and re-layouts: 3.26 us -> 4.08 us
    ppermute x16 -> x18, waiting for transfers between devices: 27.1 us -> 18.3 us  [swap(): return lax.ppermute(x, 'tp', [(i, i ^ mask) for i in range(devices)])]
    ppermute x16 -> x18, starting transfers between devices: 20.6 us -> 23.3 us  [swap(): return lax.ppermute(x, 'tp', [(i, i ^ mask) for i in range(devices)])]
    pallas_call x0 -> x3, Pallas kernels: none -> 2.2 us  [the longest x1 1.36 us: local(): call(functools.partial(combine_kernel, waves), jax.ShapeDtypeStruct((toke...]
    unnamed x19 -> x22, local copies, waits for them, and re-layouts: 2.95 us -> 3.97 us
    reduce_or x1 -> x0, other arithmetic: 0.85 us -> none  [local(): hit = jnp.any(matched, axis=1).astype(jnp.int32)]
    convert_element_type x1, other arithmetic: 0.87 us -> 0.06 us  [local(): results.append(swap(total.astype(BF16), SPLIT * j + 4))]
    dot_general x6 -> x8, matrix products: 5.69 us -> 5.82 us  [the longest x2 1.48 us: local(): mine = jnp.dot(hidden[j][:half], w_down, preferred_element_type=F32)]
  transfers between devices with their start and end apart: 16 -> 18, of which waited for: 12 -> 9; matrix products, arithmetic and copies ran while one was open for 0% -> 10% of each run, Pallas kernels for 0% -> 0%
where the time goes in v2:
time: 54.3 us; the launch traced here: 54 us
  starting transfers between devices  23.3 us (43%)
  waiting for transfers between devices  18.3 us (34%)
  matrix products  5.82 us (11%)
  local copies, waits for them, and re-layouts  4.08 us (8%)
  Pallas kernels  2.2 us (4%)
    ppermute x18, starting transfers between devices, swap(): return lax.ppermute(x, 'tp', [(i, i ^ mask) for i in range(devices)])  23.3 us
    ppermute x18, waiting for transfers between devices, swap(): return lax.ppermute(x, 'tp', [(i, i ^ mask) for i in range(devices)])  18.3 us
    unnamed x22, local copies, waits for them, and re-layouts  3.97 us
    dot_general x2, matrix products, local(): mine = jnp.dot(hidden[j][:half], w_down, preferred_element_type=F32)  1.48 us
    dot_general x2, matrix products, local(): jnp.dot(hidden[j][half:], w_down, preferred_element_type=F32).astype(BF16)  1.47 us
    dot_general x2, matrix products, local(): gated = jnp.dot(both, w_gate, preferred_element_type=F32)  1.44 us
    dot_general x2, matrix products, local(): up = jnp.dot(both, w_up, preferred_element_type=F32)  1.43 us
    pallas_call x1, Pallas kernels, local(): call(functools.partial(combine_kernel, waves), jax.ShapeDtypeStruct((toke...  1.36 us
  transfers between devices with their start and end apart: 18, of which 9 were waited for; matrix products, arithmetic and copies ran while one was open for 10% of the time, Pallas kernels for 0%

profile of v2, /device:TPU:0, one launch (start us, length us, event | category | flops | bytes accessed | tf_op | source)
XLA Modules:
  0.0 54.0 jit_solution(9778284279662017945)
XLA Ops:
  0.0 1.2 %copy-done = bf16[64,7168]{1,0:T(8,128)(2,1)S(1)} copy-done((bf16[64,7168]{1,0:T(8,128)(2,1)S(1)}, bf16[64,7168]{1,0:T(8,128)(2,1)}, u32[]{:S(2)}) %copy-start) | copy-done | bytes 917528
  1.2 0.7 %copy-done.1 = f32[7168]{0:T(1024)S(1)} copy-done((f32[7168]{0:T(1024)S(1)}, f32[7168]{0:T(1024)}, u32[]{:S(2)}) %copy-start.1) | copy-done | bytes 28696
  1.9 0.7 %copy-done.2 = s32[64,8]{0,1:T(8,128)S(1)} copy-done((s32[64,8]{0,1:T(8,128)S(1)}, s32[64,8]{0,1:T(8,128)}, u32[]{:S(2)}) %copy-start.2) | copy-done | bytes 2072
  2.6 0.7 %copy-done.3 = f32[64,8]{0,1:T(8,128)S(1)} copy-done((f32[64,8]{0,1:T(8,128)S(1)}, f32[64,8]{0,1:T(8,128)}, u32[]{:S(2)}) %copy-start.3) | copy-done | bytes 2072
  4.2 3.0 %collective-permute-start = (bf16[8,7168]{1,0:T(8,128)(2,1)S(1)}, bf16[8,7168]{1,0:T(8,128)(2,1)S(1)}, u32[]{:S(2)}, u32[]{:S(2)}) collective-permute-start(bf16[8,7168]{1,0:T(8,128)(2,1)S(1)} %shard_map.74), channel_id=1, source_target_pairs={{0,2},{1,3},{2,0},{3,1},{4,6},{5,7},{6,4},{7,5},{8,10},{9,11},{10,... | collective-permute-start | bytes 344072 | tf_op jit(solution)/shard_map/ppermute | solution.py:84
  7.2 1.6 %collective-permute-start.1 = (bf16[8,7168]{1,0:T(8,128)(2,1)S(1)}, bf16[8,7168]{1,0:T(8,128)(2,1)S(1)}, u32[]{:S(2)}, u32[]{:S(2)}) collective-permute-start(bf16[8,7168]{1,0:T(8,128)(2,1)S(1)} %shard_map.74), channel_id=1, source_target_pairs={{0,4},{1,5},{2,6},{3,7},{4,0},{5,1},{6,2},{7,3},{8,12},{9,13},{10,... | collective-permute-start | bytes 344072 | tf_op jit(solution)/shard_map/ppermute | solution.py:84
  8.8 4.0 %collective-permute-start.8 = (bf16[8,7168]{1,0:T(8,128)(2,1)S(1)}, bf16[8,7168]{1,0:T(8,128)(2,1)S(1)}, u32[]{:S(2)}, u32[]{:S(2)}) collective-permute-start(bf16[8,7168]{1,0:T(8,128)(2,1)S(1)} %get-tuple-element.10), channel_id=1, source_target_pairs={{0,12},{1,13},{2,14},{3,15},{4,8},{5,9},{6,10},{7,11},{8,4},{9,5},... | collective-permute-start | bytes 344072 | tf_op jit(solution)/shard_map/ppermute | solution.py:84
  13.0 1.5 %collective-permute-done.2 = bf16[8,7168]{1,0:T(8,128)(2,1)S(1)} collective-permute-done((bf16[8,7168]{1,0:T(8,128)(2,1)S(1)}, bf16[8,7168]{1,0:T(8,128)(2,1)S(1)}, u32[]{:S(2)}, u32[]{:S(2)}) %collective-permute-start.2) | collective-permute-done | bytes 114720 | tf_op jit(solution)/shard_map/ppermute | solution.py:84
  14.7 4.0 %collective-permute-done.8 = bf16[8,7168]{1,0:T(8,128)(2,1)S(1)} collective-permute-done((bf16[8,7168]{1,0:T(8,128)(2,1)S(1)}, bf16[8,7168]{1,0:T(8,128)(2,1)S(1)}, u32[]{:S(2)}, u32[]{:S(2)}) %collective-permute-start.8) | collective-permute-done | bytes 114720 | tf_op jit(solution)/shard_map/ppermute | solution.py:84
  18.8 0.7 %collective-permute-start.9 = (bf16[8,7168]{1,0:T(8,128)(2,1)S(1)}, bf16[8,7168]{1,0:T(8,128)(2,1)S(1)}, u32[]{:S(2)}, u32[]{:S(2)}) collective-permute-start(bf16[8,7168]{1,0:T(8,128)(2,1)S(1)} %collective-permute-done.8), channel_id=1, source_target_pairs={{0,2},{1,3},{2,0},{3,1},{4,6},{5,7},{6,4},{7,5},{8,10},{9,11},{10,... | collective-permute-start | bytes 344072 | tf_op jit(solution)/shard_map/ppermute | solution.py:84
  19.5 2.8 %collective-permute-start.11 = (bf16[8,7168]{1,0:T(8,128)(2,1)S(1)}, bf16[8,7168]{1,0:T(8,128)(2,1)S(1)}, u32[]{:S(2)}, u32[]{:S(2)}) collective-permute-start(bf16[8,7168]{1,0:T(8,128)(2,1)S(1)} %collective-permute-done.8), channel_id=1, source_target_pairs={{0,6},{1,7},{2,4},{3,5},{4,2},{5,3},{6,0},{7,1},{8,14},{9,15},{10,... | collective-permute-start | bytes 344072 | tf_op jit(solution)/shard_map/ppermute | solution.py:84
  22.4 2.3 %collective-permute-done.9 = bf16[8,7168]{1,0:T(8,128)(2,1)S(1)} collective-permute-done((bf16[8,7168]{1,0:T(8,128)(2,1)S(1)}, bf16[8,7168]{1,0:T(8,128)(2,1)S(1)}, u32[]{:S(2)}, u32[]{:S(2)}) %collective-permute-start.9) | collective-permute-done | bytes 114720 | tf_op jit(solution)/shard_map/ppermute | solution.py:84
  24.7 1.6 %collective-permute-done.11 = bf16[8,7168]{1,0:T(8,128)(2,1)S(1)} collective-permute-done((bf16[8,7168]{1,0:T(8,128)(2,1)S(1)}, bf16[8,7168]{1,0:T(8,128)(2,1)S(1)}, u32[]{:S(2)}, u32[]{:S(2)}) %collective-permute-start.11) | collective-permute-done | bytes 114720 | tf_op jit(solution)/shard_map/ppermute | solution.py:84
  26.6 0.7 %fusion.12 = f32[64,256]{1,0:T(8,128)S(1)} fusion(bf16[64,7168]{1,0:T(8,128)(2,1)S(1)} %constant_dynamic-update-slice_fusion, bf16[7168,256]{1,0:T(8,128)(2,1)S(1)} %copy-done.5), kind=kOutput, calls=%fused_computation.27 | convolution fusion | flops 234881024 | bytes 4653056 | tf_op jit(solution)/shard_map/dot_general | solution.py:102
  27.3 0.7 %multiply_convert_fusion.1 = bf16[64,256]{1,0:T(8,128)(2,1)S(1)} fusion(f32[64,256]{1,0:T(8,128)S(1)} %fusion.12, bf16[64,7168]{1,0:T(8,128)(2,1)S(1)} %constant_dynamic-update-slice_fusion, bf16[7168,256]{1,0:T(8,128)(2,1)S(1)} %copy-done.6), kind=kOutput, calls=%fused_computation.8 | convolution fusion | flops 234979328 | bytes 4685824 | tf_op jit(solution)/shard_map/dot_general | solution.py:103
  28.6 0.7 %convolution_convert_fusion.1 = bf16[32,7168]{1,0:T(8,128)(2,1)S(1)} fusion(bf16[256,7168]{1,0:T(8,128)(2,1)S(1)} %copy-done.4, bf16[64,256]{1,0:T(8,128)(2,1)S(1)} %multiply_convert_fusion.1), kind=kOutput, calls=%fused_computation.1 | convolution fusion | flops 117669888 | bytes 4145152 | tf_op jit(solution)/shard_map/dot_general | solution.py:109
  29.9 0.7 %fusion.13 = f32[64,256]{1,0:T(8,128)S(1)} fusion(bf16[64,7168]{1,0:T(8,128)(2,1)S(1)} %constant_dynamic-update-slice_fusion.5, bf16[7168,256]{1,0:T(8,128)(2,1)S(1)} %copy-done.5), kind=kOutput, calls=%fused_computation.28 | convolution fusion | flops 234881024 | bytes 4653056 | tf_op jit(solution)/shard_map/dot_general | solution.py:102
  30.6 0.7 %multiply_convert_fusion = bf16[64,256]{1,0:T(8,128)(2,1)S(1)} fusion(f32[64,256]{1,0:T(8,128)S(1)} %fusion.13, bf16[64,7168]{1,0:T(8,128)(2,1)S(1)} %constant_dynamic-update-slice_fusion.5, bf16[7168,256]{1,0:T(8,128)(2,1)S(1)} %copy-done.6), kind=kOutput, calls=%fused_computation.7 | convolution fusion | flops 234979328 | bytes 4685824 | tf_op jit(solution)/shard_map/dot_general | solution.py:103
  31.3 0.7 %convolution_convert_fusion = bf16[32,7168]{1,0:T(8,128)(2,1)S(1)} fusion(bf16[256,7168]{1,0:T(8,128)(2,1)S(1)} %copy-done.4, bf16[64,256]{1,0:T(8,128)(2,1)S(1)} %multiply_convert_fusion), kind=kOutput, calls=%fused_computation | convolution fusion | flops 117669888 | bytes 4145152 | tf_op jit(solution)/shard_map/dot_general | solution.py:109
  32.2 0.7 %add_convert_fusion.1 = bf16[32,7168]{1,0:T(8,128)(2,1)S(1)} fusion(bf16[32,7168]{1,0:T(8,128)(2,1)S(1)} %collective-permute-done.4, bf16[256,7168]{1,0:T(8,128)(2,1)S(1)} %copy-done.4, bf16[64,256]{1,0:T(8,128)(2,1)S(1)} %multiply_convert_fusion.1), kind=kOutput, calls=%fused_computation.3 | convolution fusion | flops 118128640 | bytes 4603904 | tf_op jit(solution)/shard_map/dot_general | solution.py:111
  32.9 1.1 %collective-permute-done.13 = bf16[32,7168]{1,0:T(8,128)(2,1)S(1)} collective-permute-done((bf16[32,7168]{1,0:T(8,128)(2,1)S(1)}, bf16[32,7168]{1,0:T(8,128)(2,1)S(1)}, u32[]{:S(2)}, u32[]{:S(2)}) %collective-permute-start.13) | collective-permute-done | bytes 458784 | tf_op jit(solution)/shard_map/ppermute | solution.py:84
  34.0 0.7 %add_convert_fusion = bf16[32,7168]{1,0:T(8,128)(2,1)S(1)} fusion(bf16[32,7168]{1,0:T(8,128)(2,1)S(1)} %collective-permute-done.13, bf16[256,7168]{1,0:T(8,128)(2,1)S(1)} %copy-done.4, bf16[64,256]{1,0:T(8,128)(2,1)S(1)} %multiply_convert_fusion), kind=kOutput, calls=%fused_computation.2 | convolution fusion | flops 118128640 | bytes 4603904 | tf_op jit(solution)/shard_map/dot_general | solution.py:111
  34.7 0.7 %collective-permute-start.14 = (bf16[8,7168]{1,0:T(8,128)(2,1)S(1)}, bf16[8,7168]{1,0:T(8,128)(2,1)S(1)}, u32[]{:S(2)}, u32[]{:S(2)}) collective-permute-start(bf16[8,7168]{1,0:T(8,128)(2,1)S(1)} %get-tuple-element.11), channel_id=1, source_target_pairs={{0,2},{1,3},{2,0},{3,1},{4,6},{5,7},{6,4},{7,5},{8,10},{9,11},{10,... | collective-permute-start | bytes 344072 | tf_op jit(solution)/shard_map/ppermute | solution.py:84
  35.5 1.6 %collective-permute-start.15 = (bf16[8,7168]{1,0:T(8,128)(2,1)S(1)}, bf16[8,7168]{1,0:T(8,128)(2,1)S(1)}, u32[]{:S(2)}, u32[]{:S(2)}) collective-permute-start(bf16[8,7168]{1,0:T(8,128)(2,1)S(1)} %get-tuple-element.13), channel_id=1, source_target_pairs={{0,4},{1,5},{2,6},{3,7},{4,0},{5,1},{6,2},{7,3},{8,12},{9,13},{10,... | collective-permute-start | bytes 344072 | tf_op jit(solution)/shard_map/ppermute | solution.py:84
  37.0 1.2 %collective-permute-start.16 = (bf16[8,7168]{1,0:T(8,128)(2,1)S(1)}, bf16[8,7168]{1,0:T(8,128)(2,1)S(1)}, u32[]{:S(2)}, u32[]{:S(2)}) collective-permute-start(bf16[8,7168]{1,0:T(8,128)(2,1)S(1)} %get-tuple-element.12), channel_id=1, source_target_pairs={{0,6},{1,7},{2,4},{3,5},{4,2},{5,3},{6,0},{7,1},{8,14},{9,15},{10,... | collective-permute-start | bytes 344072 | tf_op jit(solution)/shard_map/ppermute | solution.py:84
  38.3 0.7 %collective-permute-start.5 = (bf16[8,7168]{1,0:T(8,128)(2,1)S(1)}, bf16[8,7168]{1,0:T(8,128)(2,1)S(1)}, u32[]{:S(2)}, u32[]{:S(2)}) collective-permute-start(bf16[8,7168]{1,0:T(8,128)(2,1)S(1)} %get-tuple-element.16), channel_id=1, source_target_pairs={{0,2},{1,3},{2,0},{3,1},{4,6},{5,7},{6,4},{7,5},{8,10},{9,11},{10,... | collective-permute-start | bytes 344072 | tf_op jit(solution)/shard_map/ppermute | solution.py:84
  39.1 1.6 %collective-permute-start.6 = (bf16[8,7168]{1,0:T(8,128)(2,1)S(1)}, bf16[8,7168]{1,0:T(8,128)(2,1)S(1)}, u32[]{:S(2)}, u32[]{:S(2)}) collective-permute-start(bf16[8,7168]{1,0:T(8,128)(2,1)S(1)} %get-tuple-element.15), channel_id=1, source_target_pairs={{0,4},{1,5},{2,6},{3,7},{4,0},{5,1},{6,2},{7,3},{8,12},{9,13},{10,... | collective-permute-start | bytes 344072 | tf_op jit(solution)/shard_map/ppermute | solution.py:84
  40.6 1.2 %collective-permute-start.7 = (bf16[8,7168]{1,0:T(8,128)(2,1)S(1)}, bf16[8,7168]{1,0:T(8,128)(2,1)S(1)}, u32[]{:S(2)}, u32[]{:S(2)}) collective-permute-start(bf16[8,7168]{1,0:T(8,128)(2,1)S(1)} %get-tuple-element.14), channel_id=1, source_target_pairs={{0,6},{1,7},{2,4},{3,5},{4,2},{5,3},{6,0},{7,1},{8,14},{9,15},{10,... | collective-permute-start | bytes 344072 | tf_op jit(solution)/shard_map/ppermute | solution.py:84
  41.9 2.8 %collective-permute-done.16 = bf16[8,7168]{1,0:T(8,128)(2,1)S(1)} collective-permute-done((bf16[8,7168]{1,0:T(8,128)(2,1)S(1)}, bf16[8,7168]{1,0:T(8,128)(2,1)S(1)}, u32[]{:S(2)}, u32[]{:S(2)}) %collective-permute-start.16) | collective-permute-done | bytes 114720 | tf_op jit(solution)/shard_map/ppermute | solution.py:84
  44.7 3.3 %collective-permute-start.17 = (bf16[8,7168]{1,0:T(8,128)(2,1)S(1)}, bf16[8,7168]{1,0:T(8,128)(2,1)S(1)}, u32[]{:S(2)}, u32[]{:S(2)}) collective-permute-start(bf16[8,7168]{1,0:T(8,128)(2,1)S(1)} %add_convert_fusion.2), channel_id=1, source_target_pairs={{0,12},{1,13},{2,14},{3,15},{4,8},{5,9},{6,10},{7,11},{8,4},{9,5},... | collective-permute-start | bytes 344072 | tf_op jit(solution)/shard_map/ppermute | solution.py:84
  48.5 4.1 %collective-permute-done.17.refs_4_ = bf16[8,7168]{1,0:T(8,128)(2,1)S(1)} collective-permute-done((bf16[8,7168]{1,0:T(8,128)(2,1)S(1)}, bf16[8,7168]{1,0:T(8,128)(2,1)S(1)}, u32[]{:S(2)}, u32[]{:S(2)}) %collective-permute-start.17) | collective-permute-done | bytes 114720 | tf_op jit(solution)/shard_map/ppermute | solution.py:84
  52.7 1.4 %shard_map.75 = bf16[64,7168]{1,0:T(8,128)(2,1)} custom-call(f32[16,64]{1,0:T(8,128)S(1)} %get-tuple-element.8.weighted_ref, bf16[8,7168]{1,0:T(8,128)(2,1)S(1)} %get-tuple-element.17.refs_0_, bf16[8,7168]{1,0:T(8,128)(2,1)S(1)} %collective-permute-done.5.refs_1_, bf16[8,7168]{1,0:T(8,128)(2,1)S(1)} %collective-permute-done.6.refs_2_, ...), custom_call_target="tpu_custom_call" | custom-call | flops 44040192 | bytes 1835008 | tf_op jit(solution)/shard_map/pallas_call | solution.py:121
  (44 shorter events, 3.4 us)
Async XLA Ops:
  0.0 1.2 %copy-start = (bf16[64,7168]{1,0:T(8,128)(2,1)S(1)}, bf16[64,7168]{1,0:T(8,128)(2,1)}, u32[]{:S(2)}) copy-start(bf16[64,7168]{1,0:T(8,128)(2,1)} %states_ref.3) | copy-start | bytes 2752516
  1.2 0.7 %copy-start.1 = (f32[7168]{0:T(1024)S(1)}, f32[7168]{0:T(1024)}, u32[]{:S(2)}) copy-start(f32[7168]{0:T(1024)} %param.8) | copy-start | bytes 86020
  1.9 0.7 %copy-start.2 = (s32[64,8]{0,1:T(8,128)S(1)}, s32[64,8]{0,1:T(8,128)}, u32[]{:S(2)}) copy-start(s32[64,8]{0,1:T(8,128)} %param.12) | copy-start | bytes 6148
  2.6 0.7 %copy-start.3 = (f32[64,8]{0,1:T(8,128)S(1)}, f32[64,8]{0,1:T(8,128)}, u32[]{:S(2)}) copy-start(f32[64,8]{0,1:T(8,128)} %param.13) | copy-start | bytes 6148
  3.3 23.2 %copy-start.5 = (bf16[7168,256]{1,0:T(8,128)(2,1)S(1)}, bf16[7168,256]{1,0:T(8,128)(2,1)}, u32[]{:S(2)}) copy-start(bf16[7168,256]{1,0:T(8,128)(2,1)} %param.9) | copy-start | bytes 11010052
  4.2 8.6 %collective-permute-start = (bf16[8,7168]{1,0:T(8,128)(2,1)S(1)}, bf16[8,7168]{1,0:T(8,128)(2,1)S(1)}, u32[]{:S(2)}, u32[]{:S(2)}) collective-permute-start(bf16[8,7168]{1,0:T(8,128)(2,1)S(1)} %shard_map.74), channel_id=1, source_target_pairs={{0,2},{1,3},{2,0},{3,1},{4,6},{5,7},{6,4},{7,5},{8,10},{9,11},{10,... | collective-permute-start | bytes 344072 | tf_op jit(solution)/shard_map/ppermute | solution.py:84
  7.2 5.8 %collective-permute-start.1 = (bf16[8,7168]{1,0:T(8,128)(2,1)S(1)}, bf16[8,7168]{1,0:T(8,128)(2,1)S(1)}, u32[]{:S(2)}, u32[]{:S(2)}) collective-permute-start(bf16[8,7168]{1,0:T(8,128)(2,1)S(1)} %shard_map.74), channel_id=1, source_target_pairs={{0,4},{1,5},{2,6},{3,7},{4,0},{5,1},{6,2},{7,3},{8,12},{9,13},{10,... | collective-permute-start | bytes 344072 | tf_op jit(solution)/shard_map/ppermute | solution.py:84
  8.8 5.8 %collective-permute-start.2 = (bf16[8,7168]{1,0:T(8,128)(2,1)S(1)}, bf16[8,7168]{1,0:T(8,128)(2,1)S(1)}, u32[]{:S(2)}, u32[]{:S(2)}) collective-permute-start(bf16[8,7168]{1,0:T(8,128)(2,1)S(1)} %shard_map.74), channel_id=1, source_target_pairs={{0,6},{1,7},{2,4},{3,5},{4,2},{5,3},{6,0},{7,1},{8,14},{9,15},{10,... | collective-permute-start | bytes 344072 | tf_op jit(solution)/shard_map/ppermute | solution.py:84
  8.8 10.0 %collective-permute-start.8 = (bf16[8,7168]{1,0:T(8,128)(2,1)S(1)}, bf16[8,7168]{1,0:T(8,128)(2,1)S(1)}, u32[]{:S(2)}, u32[]{:S(2)}) collective-permute-start(bf16[8,7168]{1,0:T(8,128)(2,1)S(1)} %get-tuple-element.10), channel_id=1, source_target_pairs={{0,12},{1,13},{2,14},{3,15},{4,8},{5,9},{6,10},{7,11},{8,4},{9,5},... | collective-permute-start | bytes 344072 | tf_op jit(solution)/shard_map/ppermute | solution.py:84
  14.6 11.9 %collective-permute-start.3 = (bf16[32,7168]{1,0:T(8,128)(2,1)S(1)}, bf16[32,7168]{1,0:T(8,128)(2,1)S(1)}, u32[]{:S(2)}, u32[]{:S(2)}) collective-permute-start(bf16[32,7168]{1,0:T(8,128)(2,1)S(1)} %pad_maximum_fusion), channel_id=1, source_target_pairs={{0,1},{1,0},{2,3},{3,2},{4,5},{5,4},{6,7},{7,6},{8,9},{9,8},{10,11... | collective-permute-start | bytes 1376264 | tf_op jit(solution)/shard_map/ppermute | solution.py:84
  18.8 6.0 %collective-permute-start.9 = (bf16[8,7168]{1,0:T(8,128)(2,1)S(1)}, bf16[8,7168]{1,0:T(8,128)(2,1)S(1)}, u32[]{:S(2)}, u32[]{:S(2)}) collective-permute-start(bf16[8,7168]{1,0:T(8,128)(2,1)S(1)} %collective-permute-done.8), channel_id=1, source_target_pairs={{0,2},{1,3},{2,0},{3,1},{4,6},{5,7},{6,4},{7,5},{8,10},{9,11},{10,... | collective-permute-start | bytes 344072 | tf_op jit(solution)/shard_map/ppermute | solution.py:84
  19.4 5.3 %collective-permute-start.10 = (bf16[8,7168]{1,0:T(8,128)(2,1)S(1)}, bf16[8,7168]{1,0:T(8,128)(2,1)S(1)}, u32[]{:S(2)}, u32[]{:S(2)}) collective-permute-start(bf16[8,7168]{1,0:T(8,128)(2,1)S(1)} %collective-permute-done.8), channel_id=1, source_target_pairs={{0,4},{1,5},{2,6},{3,7},{4,0},{5,1},{6,2},{7,3},{8,12},{9,13},{10,... | collective-permute-start | bytes 344072 | tf_op jit(solution)/shard_map/ppermute | solution.py:84
  19.5 6.8 %collective-permute-start.11 = (bf16[8,7168]{1,0:T(8,128)(2,1)S(1)}, bf16[8,7168]{1,0:T(8,128)(2,1)S(1)}, u32[]{:S(2)}, u32[]{:S(2)}) collective-permute-start(bf16[8,7168]{1,0:T(8,128)(2,1)S(1)} %collective-permute-done.8), channel_id=1, source_target_pairs={{0,6},{1,7},{2,4},{3,5},{4,2},{5,3},{6,0},{7,1},{8,14},{9,15},{10,... | collective-permute-start | bytes 344072 | tf_op jit(solution)/shard_map/ppermute | solution.py:84
  22.3 4.9 %copy-start.6 = (bf16[7168,256]{1,0:T(8,128)(2,1)S(1)}, bf16[7168,256]{1,0:T(8,128)(2,1)}, u32[]{:S(2)}) copy-start(bf16[7168,256]{1,0:T(8,128)(2,1)} %param.10) | copy-start | bytes 11010052
  26.4 3.5 %collective-permute-start.12 = (bf16[32,7168]{1,0:T(8,128)(2,1)S(1)}, bf16[32,7168]{1,0:T(8,128)(2,1)S(1)}, u32[]{:S(2)}, u32[]{:S(2)}) collective-permute-start(bf16[32,7168]{1,0:T(8,128)(2,1)S(1)} %pad_maximum_fusion.1), channel_id=1, source_target_pairs={{0,1},{1,0},{2,3},{3,2},{4,5},{5,4},{6,7},{7,6},{8,9},{9,8},{10,11... | collective-permute-start | bytes 1376264 | tf_op jit(solution)/shard_map/ppermute | solution.py:84
  26.5 2.0 %copy-start.4 = (bf16[256,7168]{1,0:T(8,128)(2,1)S(1)}, bf16[256,7168]{1,0:T(8,128)(2,1)}, u32[]{:S(2)}) copy-start(bf16[256,7168]{1,0:T(8,128)(2,1)} %param.11) | copy-start | bytes 11010052
  29.3 2.8 %collective-permute-start.4 = (bf16[32,7168]{1,0:T(8,128)(2,1)S(1)}, bf16[32,7168]{1,0:T(8,128)(2,1)S(1)}, u32[]{:S(2)}, u32[]{:S(2)}) collective-permute-start(bf16[32,7168]{1,0:T(8,128)(2,1)S(1)} %convolution_convert_fusion.1), channel_id=1, source_target_pairs={{0,1},{1,0},{2,3},{3,2},{4,5},{5,4},{6,7},{7,6},{8,9},{9,8},{10,11... | collective-permute-start | bytes 1376264 | tf_op jit(solution)/shard_map/ppermute | solution.py:84
  32.1 1.9 %collective-permute-start.13 = (bf16[32,7168]{1,0:T(8,128)(2,1)S(1)}, bf16[32,7168]{1,0:T(8,128)(2,1)S(1)}, u32[]{:S(2)}, u32[]{:S(2)}) collective-permute-start(bf16[32,7168]{1,0:T(8,128)(2,1)S(1)} %convolution_convert_fusion), channel_id=1, source_target_pairs={{0,1},{1,0},{2,3},{3,2},{4,5},{5,4},{6,7},{7,6},{8,9},{9,8},{10,11... | collective-permute-start | bytes 1376264 | tf_op jit(solution)/shard_map/ppermute | solution.py:84
  34.7 5.9 %collective-permute-start.14 = (bf16[8,7168]{1,0:T(8,128)(2,1)S(1)}, bf16[8,7168]{1,0:T(8,128)(2,1)S(1)}, u32[]{:S(2)}, u32[]{:S(2)}) collective-permute-start(bf16[8,7168]{1,0:T(8,128)(2,1)S(1)} %get-tuple-element.11), channel_id=1, source_target_pairs={{0,2},{1,3},{2,0},{3,1},{4,6},{5,7},{6,4},{7,5},{8,10},{9,11},{10,... | collective-permute-start | bytes 344072 | tf_op jit(solution)/shard_map/ppermute | solution.py:84
  35.5 6.4 %collective-permute-start.15 = (bf16[8,7168]{1,0:T(8,128)(2,1)S(1)}, bf16[8,7168]{1,0:T(8,128)(2,1)S(1)}, u32[]{:S(2)}, u32[]{:S(2)}) collective-permute-start(bf16[8,7168]{1,0:T(8,128)(2,1)S(1)} %get-tuple-element.13), channel_id=1, source_target_pairs={{0,4},{1,5},{2,6},{3,7},{4,0},{5,1},{6,2},{7,3},{8,12},{9,13},{10,... | collective-permute-start | bytes 344072 | tf_op jit(solution)/shard_map/ppermute | solution.py:84
  37.0 7.6 %collective-permute-start.16 = (bf16[8,7168]{1,0:T(8,128)(2,1)S(1)}, bf16[8,7168]{1,0:T(8,128)(2,1)S(1)}, u32[]{:S(2)}, u32[]{:S(2)}) collective-permute-start(bf16[8,7168]{1,0:T(8,128)(2,1)S(1)} %get-tuple-element.12), channel_id=1, source_target_pairs={{0,6},{1,7},{2,4},{3,5},{4,2},{5,3},{6,0},{7,1},{8,14},{9,15},{10,... | collective-permute-start | bytes 344072 | tf_op jit(solution)/shard_map/ppermute | solution.py:84
  38.3 9.7 %collective-permute-start.5 = (bf16[8,7168]{1,0:T(8,128)(2,1)S(1)}, bf16[8,7168]{1,0:T(8,128)(2,1)S(1)}, u32[]{:S(2)}, u32[]{:S(2)}) collective-permute-start(bf16[8,7168]{1,0:T(8,128)(2,1)S(1)} %get-tuple-element.16), channel_id=1, source_target_pairs={{0,2},{1,3},{2,0},{3,1},{4,6},{5,7},{6,4},{7,5},{8,10},{9,11},{10,... | collective-permute-start | bytes 344072 | tf_op jit(solution)/shard_map/ppermute | solution.py:84
  39.1 8.9 %collective-permute-start.6 = (bf16[8,7168]{1,0:T(8,128)(2,1)S(1)}, bf16[8,7168]{1,0:T(8,128)(2,1)S(1)}, u32[]{:S(2)}, u32[]{:S(2)}) collective-permute-start(bf16[8,7168]{1,0:T(8,128)(2,1)S(1)} %get-tuple-element.15), channel_id=1, source_target_pairs={{0,4},{1,5},{2,6},{3,7},{4,0},{5,1},{6,2},{7,3},{8,12},{9,13},{10,... | collective-permute-start | bytes 344072 | tf_op jit(solution)/shard_map/ppermute | solution.py:84
  40.6 7.9 %collective-permute-start.7 = (bf16[8,7168]{1,0:T(8,128)(2,1)S(1)}, bf16[8,7168]{1,0:T(8,128)(2,1)S(1)}, u32[]{:S(2)}, u32[]{:S(2)}) collective-permute-start(bf16[8,7168]{1,0:T(8,128)(2,1)S(1)} %get-tuple-element.14), channel_id=1, source_target_pairs={{0,6},{1,7},{2,4},{3,5},{4,2},{5,3},{6,0},{7,1},{8,14},{9,15},{10,... | collective-permute-start | bytes 344072 | tf_op jit(solution)/shard_map/ppermute | solution.py:84
  44.7 7.9 %collective-permute-start.17 = (bf16[8,7168]{1,0:T(8,128)(2,1)S(1)}, bf16[8,7168]{1,0:T(8,128)(2,1)S(1)}, u32[]{:S(2)}, u32[]{:S(2)}) collective-permute-start(bf16[8,7168]{1,0:T(8,128)(2,1)S(1)} %add_convert_fusion.2), channel_id=1, source_target_pairs={{0,12},{1,13},{2,14},{3,15},{4,8},{5,9},{6,10},{7,11},{8,4},{9,5},... | collective-permute-start | bytes 344072 | tf_op jit(solution)/shard_map/ppermute | solution.py:84

commit v3 on v2

v3 whole, which is shorter than its diff:
```python
import functools

import jax
import jax.numpy as jnp
from jax import lax
from jax.experimental import pallas as pl
from jax.experimental.pallas import tpu as pltpu
from jax.sharding import PartitionSpec as P

EXPERTS = 256
NODES = 8
SPLIT = 8
CAP = 8
EPSILON = 1e-06
SIDES = (2, 4)
CORNER = 6
PICK_LIMIT = 58
OWN_FLOPS = 7_000_000_000
CHUNK = 1024
F32 = jnp.float32
BF16 = jnp.bfloat16


def call(body, outs, args, after=(), far_args=(), scratch=(), flops=0, moved=0, limit=16, out_kind=pltpu.VMEM):
    left, used = len(far_args), len(far_args) + len(args)

    def run(*refs):
        body(*refs[:used], *refs[used + len(after) :])

    def space(kind):
        return pl.BlockSpec(memory_space=kind)

    return pl.pallas_call(
        run,
        out_shape=outs,
        in_specs=[space(pltpu.HBM)] * left + [space(pltpu.VMEM)] * len(args) + [space(pl.ANY)] * len(after),
        out_specs=jax.tree.map(lambda _: space(out_kind), outs),
        scratch_shapes=list(scratch),
        compiler_params=pltpu.CompilerParams(vmem_limit_bytes=limit * 1024 * 1024),
        cost_estimate=pl.CostEstimate(flops=flops, bytes_accessed=moved, transcendentals=0),
    )(*far_args, *args, *after)


def chunks(width):
    return [slice(at, min(at + CHUNK, width)) for at in range(0, width, CHUNK)]


def normed(picked, states_ref, gain_ref):
    rows = jnp.dot(picked, states_ref[...], preferred_element_type=F32)
    squares = jnp.mean(rows * rows, axis=1, keepdims=True)
    return rows * lax.rsqrt(squares + EPSILON) * gain_ref[...]


def pick_kernel(waves, states_hbm, gain_hbm, ids_hbm, gates_hbm, *refs):
    row_refs, weighted_ref = refs[:waves], refs[waves]
    states_ref, gain_ref, ids_ref, gates_ref, sems = refs[waves + 1 :]
    copies = [
        pltpu.make_async_copy(source, target, sems.at[n])
        for n, (source, target) in enumerate(
            [(ids_hbm, ids_ref), (states_hbm, states_ref), (gates_hbm, gates_ref), (gain_hbm, gain_ref)]
        )
    ]
    for copy in copies:
        copy.start()
    tokens = ids_ref.shape[1]
    own = lax.axis_index("tp") // SPLIT
    upper = lax.broadcasted_iota(jnp.int32, (tokens, tokens), 0)
    upper = (upper <= lax.broadcasted_iota(jnp.int32, (tokens, tokens), 1)).astype(F32).astype(BF16)
    slot = lax.broadcasted_iota(jnp.int32, (CAP, tokens), 0).astype(F32)
    copies[0].wait()
    picks = []
    for j in range(waves):
        target = lax.bitwise_xor(own, j) * (EXPERTS // NODES)
        matched = ids_ref[...] == target
        hit = jnp.sum(jnp.where(matched, 1.0, 0.0), axis=0, keepdims=True)
        hits = jnp.broadcast_to(hit, (CAP, tokens))
        place = jnp.dot(hits.astype(BF16), upper, preferred_element_type=F32) - 1.0
        picks.append(jnp.where((hits > 0.5) & (place == slot), 1.0, 0.0))
    for copy in copies[1:]:
        copy.wait()
    for j, picked in enumerate(picks):
        matched = ids_ref[...] == lax.bitwise_xor(own, j) * (EXPERTS // NODES)
        score = jnp.sum(jnp.where(matched, gates_ref[...], 0.0), axis=0, keepdims=True)
        weighted_ref[CAP * j : CAP * (j + 1), :] = picked * score
    rows = normed(jnp.concatenate(picks, axis=0).astype(BF16), states_ref, gain_ref)
    for j, ref in enumerate(row_refs):
        ref[...] = rows[CAP * j : CAP * (j + 1)].astype(BF16)


def copy_kernel(ref, out_ref):
    out_ref[...] = ref[...]


def stack_kernel(*refs):
    for at in chunks(refs[-1].shape[1]):
        parts = [ref[:, at].astype(F32) for ref in refs[:-1]]
        refs[-1][:, at] = jnp.concatenate(parts, axis=0).astype(BF16)


def mark_kernel(ref, out_ref):
    out_ref[...] = ref[:, :128].astype(F32)


def ffn_kernel(gate_ref, up_ref, down_ref, *refs):
    blocks, outs = refs[: len(refs) // 2], refs[len(refs) // 2 :]
    width = blocks[0].shape[1]
    gated = up = 0.0
    for at in chunks(width):
        both = jnp.concatenate([block[:, at].astype(F32) for block in blocks], axis=0).astype(BF16)
        gated += jnp.dot(both, gate_ref[at, :], preferred_element_type=F32)
        up += jnp.dot(both, up_ref[at, :], preferred_element_type=F32)
    hidden = (gated / (1.0 + jnp.exp(-gated)) * up).astype(BF16)
    for at in chunks(width):
        result = jnp.dot(hidden, down_ref[:, at], preferred_element_type=F32)
        first = 0
        for out in outs:
            out[:, at] = result[first : first + out.shape[0]].astype(BF16)
            first += out.shape[0]


def halves(width):
    middle = width // 256 * 128
    return slice(0, middle), slice(middle, width)


def extras(width, blocks, half):
    size = half.stop - half.start
    per = -(-size // (128 * blocks)) * 128
    spans = [(at, min(at + per, size)) for at in range(0, size, per)]
    return [(n, slice(width, width + b - a), slice(half.start + a, half.start + b)) for n, (a, b) in enumerate(spans)]


def message_width(width, blocks):
    return width + max(-(-(h.stop - h.start) // (128 * blocks)) * 128 for h in halves(width))


def rows_of(n):
    return slice(CAP * n, CAP * (n + 1))


def outward_kernel(*refs):
    heads, sides, far_ref, outs = refs[:-5], refs[-5:-3], refs[-3], refs[-2:]
    width = far_ref.shape[1]
    for at in chunks(width):
        far = jnp.concatenate([head[:, at].astype(F32) for head in heads], axis=0).astype(BF16)
        for out in (far_ref,) + outs:
            out[:, at] = far
    for out, side, half in zip(outs, sides[::-1], halves(width)[::-1]):
        parts = extras(width, len(heads), half)
        if len(heads) == 1:
            out[:, parts[0][1]] = side[:, parts[0][2]]
        else:
            size = parts[0][1].stop - width
            held = [side[:, here].astype(F32) for _, _, here in parts]
            held += [jnp.zeros((CAP, size), F32)] * (len(heads) - len(held))
            held = [jnp.pad(x, ((0, 0), (0, size - x.shape[1]))) for x in held]
            out[:, width : width + size] = jnp.concatenate(held, axis=0).astype(BF16)


def arrived_kernel(*refs):
    sides, corner, out_ref = refs[:2], refs[2], refs[3]
    rows, width = corner.shape
    blocks = rows // CAP
    left, right = halves(width)
    corners = {}
    for side, half in zip(sides, (right, left)):
        for n, there, here in extras(width, blocks, half):
            corners[here.start] = (side, n, there)
    edges = sorted(corners)
    for first, last in zip(edges, edges[1:] + [width]):
        for at in chunks(last - first):
            here = slice(first + at.start, first + at.stop)
            side, n, there = corners[first]
            there = slice(there.start + at.start, there.start + at.stop)
            parts = [ref[:, here].astype(F32) for ref in (*sides, corner)]
            parts.append(side[:, there].astype(F32)[rows_of(n)])
            out_ref[:, here] = jnp.concatenate(parts, axis=0).astype(BF16)


def homeward_kernel(home_ref, back_ref, *outs):
    sides, corner = outs[:2], outs[2]
    rows, width = corner.shape
    blocks = rows // CAP
    left, right = halves(width)
    for side, half in zip(sides, (right, left)):
        for n, there, here in extras(width, blocks, half):
            for at in chunks(here.stop - here.start):
                at_here = slice(here.start + at.start, here.start + at.stop)
                at_there = slice(there.start + at.start, there.start + at.stop)
                total = home_ref[:, at_here].astype(F32) + back_ref[:, at_here].astype(F32)
                for k, out in enumerate(outs):
                    out[:, at_here] = total[rows * k : rows * (k + 1)].astype(BF16)
                mine = total[3 * rows :]
                if blocks == 1:
                    side[:, at_there] = mine.astype(BF16)
                else:
                    before = side[:, at_there].astype(F32)
                    pieces = [mine if b == n else before[rows_of(b)] for b in range(blocks)]
                    side[:, at_there] = jnp.concatenate(pieces, axis=0).astype(BF16)


def kept_kernel(skip, home_ref, back_ref, out_ref):
    for at in chunks(home_ref.shape[1]):
        total = home_ref[:, at].astype(F32) + back_ref[:, at].astype(F32)
        out_ref[:, at] = total[skip:]


def total_kernel(*refs):
    arrays, outs = refs[:4], refs[4:]
    for at in chunks(arrays[0].shape[1]):
        total = sum(ref[:, at].astype(F32) for ref in arrays)
        for n, out in enumerate(outs):
            out[:, at] = total[rows_of(n)].astype(BF16)


def near_kernel(home_ref, back_ref, side_one, side_two, kept_ref, one_ref, two_ref):
    width = home_ref.shape[1]
    blocks = side_one.shape[0] // CAP
    left, right = halves(width)
    outs = (one_ref, two_ref)
    for side, half, passed in ((side_two, left, 0), (side_one, right, 1)):
        for n, there, here in extras(width, blocks, half):
            total = home_ref[:, here].astype(F32) + back_ref[:, here].astype(F32)
            kept_ref[:, here] = total[rows_of(0)]
            more = side[:, there].astype(F32)[rows_of(n)]
            outs[passed][:, here] = (total[rows_of(1 + passed)] + more).astype(BF16)
            outs[1 - passed][:, here] = total[rows_of(2 - passed)].astype(BF16)


def combine_kernel(weighted_ref, *refs):
    near, others, (out_ref, held_ref, sems) = refs[:3], refs[3:-3], refs[-3:]
    weights = weighted_ref[...]
    high = weights.astype(BF16).astype(F32)
    weights = jnp.concatenate([high, weights - high, high], axis=0).astype(BF16)
    copies = []
    for n, at in enumerate(chunks(out_ref.shape[1])):
        own = sum(piece[:, at].astype(F32) for piece in near)
        rows = jnp.concatenate([own] + [piece[:, at].astype(F32) for piece in others], axis=0)
        high = rows.astype(BF16).astype(F32)
        rows = jnp.concatenate([high, high, rows - high], axis=0).astype(BF16)
        held_ref[:, at] = lax.dot_general(
            weights, rows, (((0,), (0,)), ((), ())), preferred_element_type=F32
        ).astype(BF16)
        copies.append(pltpu.make_async_copy(held_ref.at[:, at], out_ref.at[:, at], sems.at[n]))
        copies[-1].start()
    for copy in copies:
        copy.wait()


def local(states, norm_gain, w_gate, w_up, w_down, expert_ids, gate_weights):
    tokens, width = states.shape
    hid = w_gate.shape[1]
    devices = lax.axis_size("tp")
    waves = devices // SPLIT
    others = range(1, waves)

    def swap(x, mask):
        return lax.ppermute(x, "tp", [(i, i ^ mask) for i in range(devices)])

    def cross(x, j):
        return swap(x, SPLIT * j + 4)

    def shape(rows, columns, dtype=BF16):
        return jax.ShapeDtypeStruct((rows, columns), dtype)

    block = shape(CAP, width)

    def stack(pieces):
        rows = sum(x.shape[0] for x in pieces)
        return call(stack_kernel, shape(rows, width), pieces, moved=4 * rows * width)

    gain = norm_gain[None, :]
    ids, gates = expert_ids.T, gate_weights.T
    own, *away, weighted = call(
        functools.partial(pick_kernel, waves),
        [block] * waves + [shape(CAP * waves, tokens, F32)],
        [],
        far_args=[states, gain, ids, gates],
        scratch=[
            pltpu.VMEM((tokens, width), BF16),
            pltpu.VMEM((1, width), F32),
            pltpu.VMEM(ids.shape, ids.dtype),
            pltpu.VMEM(gates.shape, F32),
            pltpu.SemaphoreType.DMA((4,)),
        ],
        flops=2 * tokens * width * CAP * waves,
        moved=tokens * width * 2,
        limit=PICK_LIMIT,
    )
    heads = [cross(away[j - 1], j) for j in others]
    own = call(copy_kernel, block, [own], flops=OWN_FLOPS, moved=4 * CAP * width)

    first = [own] + [swap(own, s) for s in SIDES]
    marks = [call(mark_kernel, shape(CAP, 128, F32), [x]) for x in heads]
    rows = CAP * (waves - 1)
    message = shape(rows, message_width(width, waves - 1))
    far, *sides = call(
        outward_kernel,
        [shape(rows, width), message, message],
        heads + first[1:],
        after=marks,
        moved=12 * rows * width,
    )
    early = stack(first + [far])
    sides = [swap(x, s) for x, s in zip(sides, SIDES)]
    late = call(
        arrived_kernel, shape(3 * rows + CAP, width), sides + [swap(far, CORNER)], moved=16 * rows * width
    )
    blocks = [late, early, swap(late, 1), swap(early, 1)]
    late, early, late_away, early_away = call(
        ffn_kernel,
        [shape(*x.shape) for x in blocks],
        [w_gate, w_up, w_down] + blocks,
        flops=6 * sum(x.shape[0] for x in blocks) * width * hid,
        moved=6 * width * hid,
        limit=24,
    )

    *sides, corner = call(
        homeward_kernel,
        [message, message, shape(rows, width)],
        [late, swap(late_away, 1)],
        moved=20 * rows * width,
    )
    sides = [swap(x, s) for x, s in zip(sides, SIDES)]
    corner = swap(corner, CORNER)
    back = swap(early_away, 1)
    kept = call(
        functools.partial(kept_kernel, CAP * len(first)), shape(rows, width, F32), [early, back], moved=8 * rows * width
    )
    totals = call(total_kernel, [block] * (waves - 1), [kept] + sides + [corner], moved=10 * rows * width)
    returned = [cross(totals[j - 1], j) for j in others]
    kept, *near = call(
        near_kernel, [shape(CAP, width, F32), block, block], [early, back] + sides, after=totals, moved=14 * CAP * width
    )
    near = [kept] + [swap(x, s) for x, s in zip(near, SIDES)]
    marks = [call(mark_kernel, shape(CAP, 128, F32), [x]) for x in returned]
    return call(
        combine_kernel,
        shape(tokens, width),
        [weighted] + near + returned,
        after=marks,
        scratch=[pltpu.VMEM((tokens, width), BF16), pltpu.SemaphoreType.DMA((len(chunks(width)),))],
        out_kind=pl.ANY,
        flops=6 * tokens * width * CAP * waves,
        moved=tokens * width * 4,
    )


def solution(mesh):
    rows = P(("group", "tp"), None)
    in_specs = (rows, P(), P(None, "tp"), P(None, "tp"), P("tp", None), rows, rows)
    return jax.shard_map(local, mesh=mesh, in_specs=in_specs, out_specs=rows, check_vma=False)
```

time: 54.3 us -> 48.5 us (0.89)
  waiting for transfers between devices: 18.3 us -> 24.3 us
  starting transfers between devices: 23.3 us -> 17.4 us
  matrix products: 5.82 us -> 0 us
  Pallas kernels: 2.2 us -> 5.63 us
  local copies, waits for them, and re-layouts: 4.08 us -> 0.91 us
    ppermute x18 -> x16, waiting for transfers between devices: 18.3 us -> 24.3 us  [swap(): return lax.ppermute(x, 'tp', [(i, i ^ mask) for i in range(devices)])]
    ppermute x18 -> x16, starting transfers between devices: 23.3 us -> 17.4 us  [swap(): return lax.ppermute(x, 'tp', [(i, i ^ mask) for i in range(devices)])]
    dot_general x8 -> x0, matrix products: 5.82 us -> none  [the longest x2 1.48 us: local(): mine = jnp.dot(hidden[j][:half], w_down, preferred_element_type=F32)]
    pallas_call x3 -> x13, Pallas kernels: 2.2 us -> 5.63 us  [call(): pl.pallas_call(run, out_shape=outs, in_specs=[space(pltpu.HBM)] * left +...]
    unnamed x22 -> x10, local copies, waits for them, and re-layouts: 3.97 us -> 0.91 us
  transfers between devices with their start and end apart: 18 -> 16, of which waited for: 9 -> 8; matrix products, arithmetic and copies ran while one was open for 10% -> 0% of each run, Pallas kernels for 0% -> 1%
where the time goes in v3:
time: 48.5 us; the launch traced here: 48.4 us
  waiting for transfers between devices  24.3 us (50%)
  starting transfers between devices  17.4 us (36%)
  Pallas kernels  5.63 us (12%)
  local copies, waits for them, and re-layouts  0.91 us (2%)
    ppermute x16, waiting for transfers between devices, swap(): return lax.ppermute(x, 'tp', [(i, i ^ mask) for i in range(devices)])  24.3 us
    ppermute x16, starting transfers between devices, swap(): return lax.ppermute(x, 'tp', [(i, i ^ mask) for i in range(devices)])  17.4 us
    pallas_call x13, Pallas kernels, call(): pl.pallas_call(run, out_shape=outs, in_specs=[space(pltpu.HBM)] * left +...  5.63 us
  transfers between devices with their start and end apart: 16, of which 8 were waited for; matrix products, arithmetic and copies ran while one was open for 0% of the time, Pallas kernels for 1%

profile of v3, /device:TPU:0, one launch (start us, length us, event | category | flops | bytes accessed | tf_op | source)
XLA Modules:
  0.0 48.4 jit_solution(17641385601264391133)
XLA Ops:
  0.0 2.3 %shard_map.73 = (bf16[8,7168]{1,0:T(8,128)(2,1)}, bf16[8,7168]{1,0:T(8,128)(2,1)}, f32[16,64]{1,0:T(8,128)}) custom-call(bf16[64,7168]{1,0:T(8,128)(2,1)} %refs_0_.2, f32[1,7168]{1,0:T(1,128)} %bitcast.3, s32[8,64]{1,0:T(8,128)} %bitcast.4, f32[8,64]{1,0:T(8,128)} %bitcast.5), custom_call_target="tpu_custom_call" | custom-call | flops 14680064 | bytes 917504 | tf_op jit(solution)/shard_map/pallas_call | solution.py:33
  2.3 5.1 %collective-permute-start = (bf16[8,7168]{1,0:T(8,128)(2,1)}, bf16[8,7168]{1,0:T(8,128)(2,1)S(1)}, u32[]{:S(2)}, u32[]{:S(2)}) collective-permute-start(bf16[8,7168]{1,0:T(8,128)(2,1)} %get-tuple-element.22), channel_id=1, source_target_pairs={{0,12},{1,13},{2,14},{3,15},{4,8},{5,9},{6,10},{7,11},{8,4},{9,5},... | collective-permute-start | bytes 344072 | tf_op jit(solution)/shard_map/ppermute | solution.py:258
  7.4 0.9 %copy-done.4 = bf16[8,7168]{1,0:T(8,128)(2,1)S(1)} copy-done((bf16[8,7168]{1,0:T(8,128)(2,1)S(1)}, bf16[8,7168]{1,0:T(8,128)(2,1)}, u32[]{:S(2)}) %copy-start.4) | copy-done | bytes 114712
  8.3 0.1 collective-permute-start.2
  8.4 1.6 %collective-permute-start.1 = (bf16[8,7168]{1,0:T(8,128)(2,1)S(1)}, bf16[8,7168]{1,0:T(8,128)(2,1)S(1)}, u32[]{:S(2)}, u32[]{:S(2)}) collective-permute-start(bf16[8,7168]{1,0:T(8,128)(2,1)S(1)} %shard_map.74.refs_0_), channel_id=1, source_target_pairs={{0,2},{1,3},{2,0},{3,1},{4,6},{5,7},{6,4},{7,5},{8,10},{9,11},{10,... | collective-permute-start | bytes 344072 | tf_op jit(solution)/shard_map/ppermute | solution.py:258
  10.0 1.6 %collective-permute-done.refs_0_ = bf16[8,7168]{1,0:T(8,128)(2,1)S(1)} collective-permute-done((bf16[8,7168]{1,0:T(8,128)(2,1)}, bf16[8,7168]{1,0:T(8,128)(2,1)S(1)}, u32[]{:S(2)}, u32[]{:S(2)}) %collective-permute-start) | collective-permute-done | bytes 114720 | tf_op jit(solution)/shard_map/ppermute | solution.py:258
  11.7 1.9 %collective-permute-done.2.refs_2_ = bf16[8,7168]{1,0:T(8,128)(2,1)S(1)} collective-permute-done((bf16[8,7168]{1,0:T(8,128)(2,1)S(1)}, bf16[8,7168]{1,0:T(8,128)(2,1)S(1)}, u32[]{:S(2)}, u32[]{:S(2)}) %collective-permute-start.2) | collective-permute-done | bytes 114720 | tf_op jit(solution)/shard_map/ppermute | solution.py:258
  13.6 0.0 collective-permute-done.1.refs_1_
  13.6 1.7 %collective-permute-start.3 = (bf16[8,10752]{1,0:T(8,128)(2,1)S(1)}, bf16[8,10752]{1,0:T(8,128)(2,1)S(1)}, u32[]{:S(2)}, u32[]{:S(2)}) collective-permute-start(bf16[8,10752]{1,0:T(8,128)(2,1)S(1)} %get-tuple-element.24), channel_id=1, source_target_pairs={{0,2},{1,3},{2,0},{3,1},{4,6},{5,7},{6,4},{7,5},{8,10},{9,11},{10,... | collective-permute-start | bytes 516104 | tf_op jit(solution)/shard_map/ppermute | solution.py:258
  15.3 1.6 %collective-permute-start.4 = (bf16[8,10752]{1,0:T(8,128)(2,1)S(1)}, bf16[8,10752]{1,0:T(8,128)(2,1)S(1)}, u32[]{:S(2)}, u32[]{:S(2)}) collective-permute-start(bf16[8,10752]{1,0:T(8,128)(2,1)S(1)} %get-tuple-element.25), channel_id=1, source_target_pairs={{0,4},{1,5},{2,6},{3,7},{4,0},{5,1},{6,2},{7,3},{8,12},{9,13},{10,... | collective-permute-start | bytes 516104 | tf_op jit(solution)/shard_map/ppermute | solution.py:258
  16.8 0.3 collective-permute-start.5
  17.2 0.1 collective-permute-start.7
  17.3 5.6 %collective-permute-done.5.refs_2_ = bf16[8,7168]{1,0:T(8,128)(2,1)S(1)} collective-permute-done((bf16[8,7168]{1,0:T(8,128)(2,1)S(1)}, bf16[8,7168]{1,0:T(8,128)(2,1)S(1)}, u32[]{:S(2)}, u32[]{:S(2)}) %collective-permute-start.5) | collective-permute-done | bytes 114720 | tf_op jit(solution)/shard_map/ppermute | solution.py:258
  22.9 0.1 collective-permute-start.6
  23.0 1.8 %collective-permute-done.6.refs_5_ = bf16[32,7168]{1,0:T(8,128)(2,1)S(1)} collective-permute-done((bf16[32,7168]{1,0:T(8,128)(2,1)S(1)}, bf16[32,7168]{1,0:T(8,128)(2,1)S(1)}, u32[]{:S(2)}, u32[]{:S(2)}) %collective-permute-start.6) | collective-permute-done | bytes 458784 | tf_op jit(solution)/shard_map/ppermute | solution.py:258
  24.8 1.7 %shard_map.79 = (bf16[32,7168]{1,0:T(8,128)(2,1)S(1)}, bf16[32,7168]{1,0:T(8,128)(2,1)S(1)}, bf16[32,7168]{1,0:T(8,128)(2,1)S(1)}, bf16[32,7168]{1,0:T(8,128)(2,1)S(1)}) custom-call(bf16[7168,256]{1,0:T(8,128)(2,1)S(1)} %copy-done, bf16[7168,256]{1,0:T(8,128)(2,1)S(1)} %copy-done.1, bf16[256,7168]{1,0:T(8,128)(2,1)S(1)} %copy-done.2, ...), custom_call_target="tpu_custom_call" | custom-call | flops 1409286144 | bytes 11010048 | tf_op jit(solution)/shard_map/pallas_call | solution.py:33
  26.6 0.2 collective-permute-start.9
  26.8 0.4 collective-permute-start.8
  27.2 1.3 %collective-permute-done.9.refs_1_ = bf16[32,7168]{1,0:T(8,128)(2,1)S(1)} collective-permute-done((bf16[32,7168]{1,0:T(8,128)(2,1)S(1)}, bf16[32,7168]{1,0:T(8,128)(2,1)S(1)}, u32[]{:S(2)}, u32[]{:S(2)}) %collective-permute-start.9) | collective-permute-done | bytes 458784 | tf_op jit(solution)/shard_map/ppermute | solution.py:258
  28.5 0.1 shard_map.80
  28.6 1.7 %collective-permute-start.10 = (bf16[8,10752]{1,0:T(8,128)(2,1)S(1)}, bf16[8,10752]{1,0:T(8,128)(2,1)S(1)}, u32[]{:S(2)}, u32[]{:S(2)}) collective-permute-start(bf16[8,10752]{1,0:T(8,128)(2,1)S(1)} %get-tuple-element.31), channel_id=1, source_target_pairs={{0,2},{1,3},{2,0},{3,1},{4,6},{5,7},{6,4},{7,5},{8,10},{9,11},{10,... | collective-permute-start | bytes 516104 | tf_op jit(solution)/shard_map/ppermute | solution.py:258
  30.3 1.1 %collective-permute-start.11 = (bf16[8,10752]{1,0:T(8,128)(2,1)S(1)}, bf16[8,10752]{1,0:T(8,128)(2,1)S(1)}, u32[]{:S(2)}, u32[]{:S(2)}) collective-permute-start(bf16[8,10752]{1,0:T(8,128)(2,1)S(1)} %get-tuple-element.32), channel_id=1, source_target_pairs={{0,4},{1,5},{2,6},{3,7},{4,0},{5,1},{6,2},{7,3},{8,12},{9,13},{10,... | collective-permute-start | bytes 516104 | tf_op jit(solution)/shard_map/ppermute | solution.py:258
  31.3 0.8 %collective-permute-start.12 = (bf16[8,7168]{1,0:T(8,128)(2,1)S(1)}, bf16[8,7168]{1,0:T(8,128)(2,1)S(1)}, u32[]{:S(2)}, u32[]{:S(2)}) collective-permute-start(bf16[8,7168]{1,0:T(8,128)(2,1)S(1)} %get-tuple-element.33), channel_id=1, source_target_pairs={{0,6},{1,7},{2,4},{3,5},{4,2},{5,3},{6,0},{7,1},{8,14},{9,15},{10,... | collective-permute-start | bytes 344072 | tf_op jit(solution)/shard_map/ppermute | solution.py:258
  32.2 6.5 %collective-permute-done.12.refs_3_ = bf16[8,7168]{1,0:T(8,128)(2,1)S(1)} collective-permute-done((bf16[8,7168]{1,0:T(8,128)(2,1)S(1)}, bf16[8,7168]{1,0:T(8,128)(2,1)S(1)}, u32[]{:S(2)}, u32[]{:S(2)}) %collective-permute-start.12) | collective-permute-done | bytes 114720 | tf_op jit(solution)/shard_map/ppermute | solution.py:258
  38.7 0.1 shard_map.82.refs_4_
  38.8 1.2 %collective-permute-start.15 = (bf16[8,7168]{1,0:T(8,128)(2,1)S(1)}, bf16[8,7168]{1,0:T(8,128)(2,1)S(1)}, u32[]{:S(2)}, u32[]{:S(2)}) collective-permute-start(bf16[8,7168]{1,0:T(8,128)(2,1)S(1)} %shard_map.82.refs_4_), channel_id=1, source_target_pairs={{0,12},{1,13},{2,14},{3,15},{4,8},{5,9},{6,10},{7,11},{8,4},{9,5},... | collective-permute-start | bytes 344072 | tf_op jit(solution)/shard_map/ppermute | solution.py:258
  39.9 0.1 shard_map.83
  40.0 1.6 %collective-permute-start.13 = (bf16[8,7168]{1,0:T(8,128)(2,1)S(1)}, bf16[8,7168]{1,0:T(8,128)(2,1)S(1)}, u32[]{:S(2)}, u32[]{:S(2)}) collective-permute-start(bf16[8,7168]{1,0:T(8,128)(2,1)S(1)} %get-tuple-element.35), channel_id=1, source_target_pairs={{0,2},{1,3},{2,0},{3,1},{4,6},{5,7},{6,4},{7,5},{8,10},{9,11},{10,... | collective-permute-start | bytes 344072 | tf_op jit(solution)/shard_map/ppermute | solution.py:258
  41.6 0.1 collective-permute-start.14
  41.7 4.5 %collective-permute-done.15.refs_0_.refs_4_ = bf16[8,7168]{1,0:T(8,128)(2,1)S(1)} collective-permute-done((bf16[8,7168]{1,0:T(8,128)(2,1)S(1)}, bf16[8,7168]{1,0:T(8,128)(2,1)S(1)}, u32[]{:S(2)}, u32[]{:S(2)}) %collective-permute-start.15) | collective-permute-done | bytes 114720 | tf_op jit(solution)/shard_map/ppermute | solution.py:258
  46.2 0.9 %collective-permute-done.14.refs_3_ = bf16[8,7168]{1,0:T(8,128)(2,1)S(1)} collective-permute-done((bf16[8,7168]{1,0:T(8,128)(2,1)S(1)}, bf16[8,7168]{1,0:T(8,128)(2,1)S(1)}, u32[]{:S(2)}, u32[]{:S(2)}) %collective-permute-start.14) | collective-permute-done | bytes 114720 | tf_op jit(solution)/shard_map/ppermute | solution.py:258
  47.2 1.2 %shard_map.85 = bf16[64,7168]{1,0:T(8,128)(2,1)} custom-call(f32[16,64]{1,0:T(8,128)S(1)} %copy-done.3, f32[8,7168]{1,0:T(8,128)S(1)} %get-tuple-element.34.refs_1_, bf16[8,7168]{1,0:T(8,128)(2,1)S(1)} %collective-permute-done.13.refs_2_, bf16[8,7168]{1,0:T(8,128)(2,1)S(1)} %collective-permute-done.14.refs_3_, ...), custom_call_target="tpu_custom_call" | custom-call | flops 44040192 | bytes 1835008 | tf_op jit(solution)/shard_map/pallas_call | solution.py:33
  (23 shorter events, 0.2 us)
Async XLA Ops:
  2.3 9.3 %collective-permute-start = (bf16[8,7168]{1,0:T(8,128)(2,1)}, bf16[8,7168]{1,0:T(8,128)(2,1)S(1)}, u32[]{:S(2)}, u32[]{:S(2)}) collective-permute-start(bf16[8,7168]{1,0:T(8,128)(2,1)} %get-tuple-element.22), channel_id=1, source_target_pairs={{0,12},{1,13},{2,14},{3,15},{4,8},{5,9},{6,10},{7,11},{8,4},{9,5},... | collective-permute-start | bytes 344072 | tf_op jit(solution)/shard_map/ppermute | solution.py:258
  7.4 0.9 %copy-start.4 = (bf16[8,7168]{1,0:T(8,128)(2,1)S(1)}, bf16[8,7168]{1,0:T(8,128)(2,1)}, u32[]{:S(2)}) copy-start(bf16[8,7168]{1,0:T(8,128)(2,1)} %get-tuple-element.23.refs_0_) | copy-start | bytes 344068
  8.3 16.5 %copy-start = (bf16[7168,256]{1,0:T(8,128)(2,1)S(1)}, bf16[7168,256]{1,0:T(8,128)(2,1)}, u32[]{:S(2)}) copy-start(bf16[7168,256]{1,0:T(8,128)(2,1)} %refs_0_.3) | copy-start | bytes 11010052
  8.3 16.5 %copy-start.1 = (bf16[7168,256]{1,0:T(8,128)(2,1)S(1)}, bf16[7168,256]{1,0:T(8,128)(2,1)}, u32[]{:S(2)}) copy-start(bf16[7168,256]{1,0:T(8,128)(2,1)} %refs_1_.1) | copy-start | bytes 11010052
  8.3 16.5 %copy-start.2 = (bf16[256,7168]{1,0:T(8,128)(2,1)S(1)}, bf16[256,7168]{1,0:T(8,128)(2,1)}, u32[]{:S(2)}) copy-start(bf16[256,7168]{1,0:T(8,128)(2,1)} %refs_2_.1) | copy-start | bytes 11010052
  8.3 5.2 %collective-permute-start.2 = (bf16[8,7168]{1,0:T(8,128)(2,1)S(1)}, bf16[8,7168]{1,0:T(8,128)(2,1)S(1)}, u32[]{:S(2)}, u32[]{:S(2)}) collective-permute-start(bf16[8,7168]{1,0:T(8,128)(2,1)S(1)} %shard_map.74.refs_0_), channel_id=1, source_target_pairs={{0,4},{1,5},{2,6},{3,7},{4,0},{5,1},{6,2},{7,3},{8,12},{9,13},{10,... | collective-permute-start | bytes 344072 | tf_op jit(solution)/shard_map/ppermute | solution.py:258
  8.4 5.1 %collective-permute-start.1 = (bf16[8,7168]{1,0:T(8,128)(2,1)S(1)}, bf16[8,7168]{1,0:T(8,128)(2,1)S(1)}, u32[]{:S(2)}, u32[]{:S(2)}) collective-permute-start(bf16[8,7168]{1,0:T(8,128)(2,1)S(1)} %shard_map.74.refs_0_), channel_id=1, source_target_pairs={{0,2},{1,3},{2,0},{3,1},{4,6},{5,7},{6,4},{7,5},{8,10},{9,11},{10,... | collective-permute-start | bytes 344072 | tf_op jit(solution)/shard_map/ppermute | solution.py:258
  13.6 9.3 %collective-permute-start.3 = (bf16[8,10752]{1,0:T(8,128)(2,1)S(1)}, bf16[8,10752]{1,0:T(8,128)(2,1)S(1)}, u32[]{:S(2)}, u32[]{:S(2)}) collective-permute-start(bf16[8,10752]{1,0:T(8,128)(2,1)S(1)} %get-tuple-element.24), channel_id=1, source_target_pairs={{0,2},{1,3},{2,0},{3,1},{4,6},{5,7},{6,4},{7,5},{8,10},{9,11},{10,... | collective-permute-start | bytes 516104 | tf_op jit(solution)/shard_map/ppermute | solution.py:258
  15.3 7.6 %collective-permute-start.4 = (bf16[8,10752]{1,0:T(8,128)(2,1)S(1)}, bf16[8,10752]{1,0:T(8,128)(2,1)S(1)}, u32[]{:S(2)}, u32[]{:S(2)}) collective-permute-start(bf16[8,10752]{1,0:T(8,128)(2,1)S(1)} %get-tuple-element.25), channel_id=1, source_target_pairs={{0,4},{1,5},{2,6},{3,7},{4,0},{5,1},{6,2},{7,3},{8,12},{9,13},{10,... | collective-permute-start | bytes 516104 | tf_op jit(solution)/shard_map/ppermute | solution.py:258
  16.8 6.0 %collective-permute-start.5 = (bf16[8,7168]{1,0:T(8,128)(2,1)S(1)}, bf16[8,7168]{1,0:T(8,128)(2,1)S(1)}, u32[]{:S(2)}, u32[]{:S(2)}) collective-permute-start(bf16[8,7168]{1,0:T(8,128)(2,1)S(1)} %get-tuple-element.26.refs_3_), channel_id=1, source_target_pairs={{0,6},{1,7},{2,4},{3,5},{4,2},{5,3},{6,0},{7,1},{8,14},{9,15},{10,... | collective-permute-start | bytes 344072 | tf_op jit(solution)/shard_map/ppermute | solution.py:258
  17.2 5.8 %collective-permute-start.7 = (bf16[32,7168]{1,0:T(8,128)(2,1)S(1)}, bf16[32,7168]{1,0:T(8,128)(2,1)S(1)}, u32[]{:S(2)}, u32[]{:S(2)}) collective-permute-start(bf16[32,7168]{1,0:T(8,128)(2,1)S(1)} %shard_map.78.refs_4_), channel_id=1, source_target_pairs={{0,1},{1,0},{2,3},{3,2},{4,5},{5,4},{6,7},{7,6},{8,9},{9,8},{10,11... | collective-permute-start | bytes 1376264 | tf_op jit(solution)/shard_map/ppermute | solution.py:258
  22.9 1.9 %collective-permute-start.6 = (bf16[32,7168]{1,0:T(8,128)(2,1)S(1)}, bf16[32,7168]{1,0:T(8,128)(2,1)S(1)}, u32[]{:S(2)}, u32[]{:S(2)}) collective-permute-start(bf16[32,7168]{1,0:T(8,128)(2,1)S(1)} %shard_map.77.refs_3_), channel_id=1, source_target_pairs={{0,1},{1,0},{2,3},{3,2},{4,5},{5,4},{6,7},{7,6},{8,9},{9,8},{10,11... | collective-permute-start | bytes 1376264 | tf_op jit(solution)/shard_map/ppermute | solution.py:258
  26.6 20.6 %copy-start.3 = (f32[16,64]{1,0:T(8,128)S(1)}, f32[16,64]{1,0:T(8,128)}, u32[]{:S(2)}) copy-start(f32[16,64]{1,0:T(8,128)} %get-tuple-element.21.refs_0_) | copy-start | bytes 12292
  26.6 1.9 %collective-permute-start.9 = (bf16[32,7168]{1,0:T(8,128)(2,1)S(1)}, bf16[32,7168]{1,0:T(8,128)(2,1)S(1)}, u32[]{:S(2)}, u32[]{:S(2)}) collective-permute-start(bf16[32,7168]{1,0:T(8,128)(2,1)S(1)} %get-tuple-element.30), channel_id=1, source_target_pairs={{0,1},{1,0},{2,3},{3,2},{4,5},{5,4},{6,7},{7,6},{8,9},{9,8},{10,11... | collective-permute-start | bytes 1376264 | tf_op jit(solution)/shard_map/ppermute | solution.py:258
  26.8 5.4 %collective-permute-start.8 = (bf16[32,7168]{1,0:T(8,128)(2,1)S(1)}, bf16[32,7168]{1,0:T(8,128)(2,1)S(1)}, u32[]{:S(2)}, u32[]{:S(2)}) collective-permute-start(bf16[32,7168]{1,0:T(8,128)(2,1)S(1)} %get-tuple-element.28), channel_id=1, source_target_pairs={{0,1},{1,0},{2,3},{3,2},{4,5},{5,4},{6,7},{7,6},{8,9},{9,8},{10,11... | collective-permute-start | bytes 1376264 | tf_op jit(solution)/shard_map/ppermute | solution.py:258
  28.6 10.1 %collective-permute-start.10 = (bf16[8,10752]{1,0:T(8,128)(2,1)S(1)}, bf16[8,10752]{1,0:T(8,128)(2,1)S(1)}, u32[]{:S(2)}, u32[]{:S(2)}) collective-permute-start(bf16[8,10752]{1,0:T(8,128)(2,1)S(1)} %get-tuple-element.31), channel_id=1, source_target_pairs={{0,2},{1,3},{2,0},{3,1},{4,6},{5,7},{6,4},{7,5},{8,10},{9,11},{10,... | collective-permute-start | bytes 516104 | tf_op jit(solution)/shard_map/ppermute | solution.py:258
  30.3 8.4 %collective-permute-start.11 = (bf16[8,10752]{1,0:T(8,128)(2,1)S(1)}, bf16[8,10752]{1,0:T(8,128)(2,1)S(1)}, u32[]{:S(2)}, u32[]{:S(2)}) collective-permute-start(bf16[8,10752]{1,0:T(8,128)(2,1)S(1)} %get-tuple-element.32), channel_id=1, source_target_pairs={{0,4},{1,5},{2,6},{3,7},{4,0},{5,1},{6,2},{7,3},{8,12},{9,13},{10,... | collective-permute-start | bytes 516104 | tf_op jit(solution)/shard_map/ppermute | solution.py:258
  31.3 7.4 %collective-permute-start.12 = (bf16[8,7168]{1,0:T(8,128)(2,1)S(1)}, bf16[8,7168]{1,0:T(8,128)(2,1)S(1)}, u32[]{:S(2)}, u32[]{:S(2)}) collective-permute-start(bf16[8,7168]{1,0:T(8,128)(2,1)S(1)} %get-tuple-element.33), channel_id=1, source_target_pairs={{0,6},{1,7},{2,4},{3,5},{4,2},{5,3},{6,0},{7,1},{8,14},{9,15},{10,... | collective-permute-start | bytes 344072 | tf_op jit(solution)/shard_map/ppermute | solution.py:258
  38.8 7.4 %collective-permute-start.15 = (bf16[8,7168]{1,0:T(8,128)(2,1)S(1)}, bf16[8,7168]{1,0:T(8,128)(2,1)S(1)}, u32[]{:S(2)}, u32[]{:S(2)}) collective-permute-start(bf16[8,7168]{1,0:T(8,128)(2,1)S(1)} %shard_map.82.refs_4_), channel_id=1, source_target_pairs={{0,12},{1,13},{2,14},{3,15},{4,8},{5,9},{6,10},{7,11},{8,4},{9,5},... | collective-permute-start | bytes 344072 | tf_op jit(solution)/shard_map/ppermute | solution.py:258
  40.0 6.2 %collective-permute-start.13 = (bf16[8,7168]{1,0:T(8,128)(2,1)S(1)}, bf16[8,7168]{1,0:T(8,128)(2,1)S(1)}, u32[]{:S(2)}, u32[]{:S(2)}) collective-permute-start(bf16[8,7168]{1,0:T(8,128)(2,1)S(1)} %get-tuple-element.35), channel_id=1, source_target_pairs={{0,2},{1,3},{2,0},{3,1},{4,6},{5,7},{6,4},{7,5},{8,10},{9,11},{10,... | collective-permute-start | bytes 344072 | tf_op jit(solution)/shard_map/ppermute | solution.py:258
  41.6 5.6 %collective-permute-start.14 = (bf16[8,7168]{1,0:T(8,128)(2,1)S(1)}, bf16[8,7168]{1,0:T(8,128)(2,1)S(1)}, u32[]{:S(2)}, u32[]{:S(2)}) collective-permute-start(bf16[8,7168]{1,0:T(8,128)(2,1)S(1)} %get-tuple-element.36), channel_id=1, source_target_pairs={{0,4},{1,5},{2,6},{3,7},{4,0},{5,1},{6,2},{7,3},{8,12},{9,13},{10,... | collective-permute-start | bytes 344072 | tf_op jit(solution)/shard_map/ppermute | solution.py:258

commit v4 on v3

--- a/solution.py
+++ b/solution.py
@@ -14,7 +14,6 @@
 EPSILON = 1e-06
 SIDES = (2, 4)
 CORNER = 6
-PICK_LIMIT = 58
 OWN_FLOPS = 7_000_000_000
 CHUNK = 1024
 F32 = jnp.float32
@@ -30,6 +29,7 @@
     def space(kind):
         return pl.BlockSpec(memory_space=kind)
 
+    far_args = [pltpu.with_memory_space_constraint(x, pltpu.HBM) for x in far_args]
     return pl.pallas_call(
         run,
         out_shape=outs,
@@ -87,8 +87,11 @@
         ref[...] = rows[CAP * j : CAP * (j + 1)].astype(BF16)
 
 
-def copy_kernel(ref, out_ref):
+def ready_kernel(ref, weighted_ref, out_ref, weights_ref):
     out_ref[...] = ref[...]
+    weights = weighted_ref[...]
+    high = weights.astype(BF16).astype(F32)
+    weights_ref[...] = jnp.concatenate([high, weights - high, high], axis=0).T.astype(BF16)
 
 
 def stack_kernel(*refs):
@@ -136,45 +139,6 @@
 
 def rows_of(n):
     return slice(CAP * n, CAP * (n + 1))
-
-
-def outward_kernel(*refs):
-    heads, sides, far_ref, outs = refs[:-5], refs[-5:-3], refs[-3], refs[-2:]
-    width = far_ref.shape[1]
-    for at in chunks(width):
-        far = jnp.concatenate([head[:, at].astype(F32) for head in heads], axis=0).astype(BF16)
-        for out in (far_ref,) + outs:
-            out[:, at] = far
-    for out, side, half in zip(outs, sides[::-1], halves(width)[::-1]):
-        parts = extras(width, len(heads), half)
-        if len(heads) == 1:
-            out[:, parts[0][1]] = side[:, parts[0][2]]
-        else:
-            size = parts[0][1].stop - width
-            held = [side[:, here].astype(F32) for _, _, here in parts]
-            held += [jnp.zeros((CAP, size), F32)] * (len(heads) - len(held))
-            held = [jnp.pad(x, ((0, 0), (0, size - x.shape[1]))) for x in held]
-            out[:, width : width + size] = jnp.concatenate(held, axis=0).astype(BF16)
-
-
-def arrived_kernel(*refs):
-    sides, corner, out_ref = refs[:2], refs[2], refs[3]
-    rows, width = corner.shape
-    blocks = rows // CAP
-    left, right = halves(width)
-    corners = {}
-    for side, half in zip(sides, (right, left)):
-        for n, there, here in extras(width, blocks, half):
-            corners[here.start] = (side, n, there)
-    edges = sorted(corners)
-    for first, last in zip(edges, edges[1:] + [width]):
-        for at in chunks(last - first):
-            here = slice(first + at.start, first + at.stop)
-            side, n, there = corners[first]
-            there = slice(there.start + at.start, there.start + at.stop)
-            parts = [ref[:, here].astype(F32) for ref in (*sides, corner)]
-            parts.append(side[:, there].astype(F32)[rows_of(n)])
-            out_ref[:, here] = jnp.concatenate(parts, axis=0).astype(BF16)
 
 
 def homeward_kernel(home_ref, back_ref, *outs):
@@ -227,20 +191,16 @@
             outs[1 - passed][:, here] = total[rows_of(2 - passed)].astype(BF16)
 
 
-def combine_kernel(weighted_ref, *refs):
+def combine_kernel(weights_ref, *refs):
     near, others, (out_ref, held_ref, sems) = refs[:3], refs[3:-3], refs[-3:]
-    weights = weighted_ref[...]
-    high = weights.astype(BF16).astype(F32)
-    weights = jnp.concatenate([high, weights - high, high], axis=0).astype(BF16)
+    weights = weights_ref[...]
     copies = []
     for n, at in enumerate(chunks(out_ref.shape[1])):
         own = sum(piece[:, at].astype(F32) for piece in near)
         rows = jnp.concatenate([own] + [piece[:, at].astype(F32) for piece in others], axis=0)
         high = rows.astype(BF16).astype(F32)
         rows = jnp.concatenate([high, high, rows - high], axis=0).astype(BF16)
-        held_ref[:, at] = lax.dot_general(
-            weights, rows, (((0,), (0,)), ((), ())), preferred_element_type=F32
-        ).astype(BF16)
+        held_ref[:, at] = jnp.dot(weights, rows, preferred_element_type=F32).astype(BF16)
         copies.append(pltpu.make_async_copy(held_ref.at[:, at], out_ref.at[:, at], sems.at[n]))
         copies[-1].start()
     for copy in copies:
@@ -265,9 +225,9 @@
 
     block = shape(CAP, width)
 
-    def stack(pieces):
+    def stack(pieces, after=()):
         rows = sum(x.shape[0] for x in pieces)
-        return call(stack_kernel, shape(rows, width), pieces, moved=4 * rows * width)
+        return call(stack_kernel, shape(rows, width), pieces, after, moved=4 * rows * width)
 
     gain = norm_gain[None, :]
     ids, gates = expert_ids.T, gate_weights.T
@@ -285,27 +245,26 @@
         ],
         flops=2 * tokens * width * CAP * waves,
         moved=tokens * width * 2,
-        limit=PICK_LIMIT,
-    )
+    )
+    side_two = swap(own, SIDES[1])
     heads = [cross(away[j - 1], j) for j in others]
-    own = call(copy_kernel, block, [own], flops=OWN_FLOPS, moved=4 * CAP * width)
-
-    first = [own] + [swap(own, s) for s in SIDES]
-    marks = [call(mark_kernel, shape(CAP, 128, F32), [x]) for x in heads]
+    own, weights = call(
+        ready_kernel,
+        [block, shape(tokens, 3 * CAP * waves)],
+        [own, weighted],
+        flops=OWN_FLOPS,
+        moved=4 * CAP * width,
+    )
+
+    first = [own, swap(own, SIDES[0]), side_two]
+    past = swap(first[2], SIDES[0])
     rows = CAP * (waves - 1)
     message = shape(rows, message_width(width, waves - 1))
-    far, *sides = call(
-        outward_kernel,
-        [shape(rows, width), message, message],
-        heads + first[1:],
-        after=marks,
-        moved=12 * rows * width,
-    )
-    early = stack(first + [far])
-    sides = [swap(x, s) for x, s in zip(sides, SIDES)]
-    late = call(
-        arrived_kernel, shape(3 * rows + CAP, width), sides + [swap(far, CORNER)], moved=16 * rows * width
-    )
+    far = heads[0] if waves == 2 else stack(heads)
+    sent = [swap(far, s) for s in SIDES + (CORNER,)]
+    marks = [call(mark_kernel, shape(CAP, 128, F32), [x]) for x in heads]
+    early = stack(first + [far], after=marks)
+    late = stack(sent + [past])
     blocks = [late, early, swap(late, 1), swap(early, 1)]
     late, early, late_away, early_away = call(
         ffn_kernel,
@@ -338,7 +297,7 @@
     return call(
         combine_kernel,
         shape(tokens, width),
-        [weighted] + near + returned,
+        [weights] + near + returned,
         after=marks,
         scratch=[pltpu.VMEM((tokens, width), BF16), pltpu.SemaphoreType.DMA((len(chunks(width)),))],
         out_kind=pl.ANY,

time: 48.5 us -> 47.1 us (0.971)
  starting transfers between devices: 17.4 us -> 20.4 us
  waiting for transfers between devices: 24.3 us -> 21.4 us
  local copies, waits for them, and re-layouts: 0.91 us -> 0.01 us
  Pallas kernels: 5.63 us -> 4.93 us
    ppermute x16 -> x17, starting transfers between devices: 17.4 us -> 20.4 us  [swap(): return lax.ppermute(x, 'tp', [(i, i ^ mask) for i in range(devices)])]
    ppermute x16 -> x17, waiting for transfers between devices: 24.3 us -> 21.4 us  [swap(): return lax.ppermute(x, 'tp', [(i, i ^ mask) for i in range(devices)])]
    unnamed x10 -> x6, local copies, waits for them, and re-layouts: 0.91 us -> 0.01 us
    pallas_call x13 -> x12, Pallas kernels: 5.63 us -> 4.93 us  [call(): pl.pallas_call(run, out_shape=outs, in_specs=[space(pltpu.HBM)] * left +...]
  transfers between devices with their start and end apart: 16 -> 17, of which waited for: 8 -> 11; matrix products, arithmetic and copies ran while one was open for 0% -> 0% of each run, Pallas kernels for 1% -> 1%
where the time goes in v4:
time: 47.1 us; the launch traced here: 46.9 us
  waiting for transfers between devices  21.4 us (45%)
  starting transfers between devices  20.4 us (43%)
  Pallas kernels  4.93 us (10%)
    ppermute x17, waiting for transfers between devices, swap(): return lax.ppermute(x, 'tp', [(i, i ^ mask) for i in range(devices)])  21.4 us
    ppermute x17, starting transfers between devices, swap(): return lax.ppermute(x, 'tp', [(i, i ^ mask) for i in range(devices)])  20.4 us
    pallas_call x12, Pallas kernels, call(): pl.pallas_call(run, out_shape=outs, in_specs=[space(pltpu.HBM)] * left +...  4.93 us
  transfers between devices with their start and end apart: 17, of which 11 were waited for; matrix products, arithmetic and copies ran while one was open for 0% of the time, Pallas kernels for 1%

profile of v4, /device:TPU:0, one launch (start us, length us, event | category | flops | bytes accessed | tf_op | source)
XLA Modules:
  0.0 46.9 jit_solution(3833488146687502547)
XLA Ops:
  0.0 1.6 %shard_map.73 = (bf16[8,7168]{1,0:T(8,128)(2,1)S(1)}, bf16[8,7168]{1,0:T(8,128)(2,1)S(1)}, f32[16,64]{1,0:T(8,128)S(1)}) custom-call(bf16[64,7168]{1,0:T(8,128)(2,1)} %refs_0_.2, f32[1,7168]{1,0:T(1,128)} %bitcast.3, s32[8,64]{1,0:T(8,128)} %bitcast.4, f32[8,64]{1,0:T(8,128)} %bitcast.5), custom_call_target="tpu_custom_call" | custom-call | flops 14680064 | bytes 917504 | tf_op jit(solution)/shard_map/pallas_call | solution.py:33
  1.6 5.1 %collective-permute-start = (bf16[8,7168]{1,0:T(8,128)(2,1)S(1)}, bf16[8,7168]{1,0:T(8,128)(2,1)S(1)}, u32[]{:S(2)}, u32[]{:S(2)}) collective-permute-start(bf16[8,7168]{1,0:T(8,128)(2,1)S(1)} %get-tuple-element.23), channel_id=1, source_target_pairs={{0,12},{1,13},{2,14},{3,15},{4,8},{5,9},{6,10},{7,11},{8,4},{9,5},... | collective-permute-start | bytes 344072 | tf_op jit(solution)/shard_map/ppermute | solution.py:218
  6.8 0.1 shard_map.74
  6.9 1.6 %collective-permute-start.6 = (bf16[8,7168]{1,0:T(8,128)(2,1)S(1)}, bf16[8,7168]{1,0:T(8,128)(2,1)S(1)}, u32[]{:S(2)}, u32[]{:S(2)}) collective-permute-start(bf16[8,7168]{1,0:T(8,128)(2,1)S(1)} %get-tuple-element.24.refs_0_), channel_id=1, source_target_pairs={{0,2},{1,3},{2,0},{3,1},{4,6},{5,7},{6,4},{7,5},{8,10},{9,11},{10,... | collective-permute-start | bytes 344072 | tf_op jit(solution)/shard_map/ppermute | solution.py:218
  8.4 2.3 %collective-permute-done.refs_0_.refs_3_ = bf16[8,7168]{1,0:T(8,128)(2,1)S(1)} collective-permute-done((bf16[8,7168]{1,0:T(8,128)(2,1)S(1)}, bf16[8,7168]{1,0:T(8,128)(2,1)S(1)}, u32[]{:S(2)}, u32[]{:S(2)}) %collective-permute-start) | collective-permute-done | bytes 114720 | tf_op jit(solution)/shard_map/ppermute | solution.py:218
  10.8 2.3 %collective-permute-start.3 = (bf16[8,7168]{1,0:T(8,128)(2,1)S(1)}, bf16[8,7168]{1,0:T(8,128)(2,1)S(1)}, u32[]{:S(2)}, u32[]{:S(2)}) collective-permute-start(bf16[8,7168]{1,0:T(8,128)(2,1)S(1)} %collective-permute-done.refs_0_.refs_3_), channel_id=1, source_target_pairs={{0,6},{1,7},{2,4},{3,5},{4,2},{5,3},{6,0},{7,1},{8,14},{9,15},{10,... | collective-permute-start | bytes 344072 | tf_op jit(solution)/shard_map/ppermute | solution.py:218
  13.0 0.9 %collective-permute-start.2 = (bf16[8,7168]{1,0:T(8,128)(2,1)S(1)}, bf16[8,7168]{1,0:T(8,128)(2,1)S(1)}, u32[]{:S(2)}, u32[]{:S(2)}) collective-permute-start(bf16[8,7168]{1,0:T(8,128)(2,1)S(1)} %collective-permute-done.refs_0_.refs_3_), channel_id=1, source_target_pairs={{0,4},{1,5},{2,6},{3,7},{4,0},{5,1},{6,2},{7,3},{8,12},{9,13},{10,... | collective-permute-start | bytes 344072 | tf_op jit(solution)/shard_map/ppermute | solution.py:218
  14.0 0.3 collective-permute-start.1
  14.3 1.7 %collective-permute-start.5 = (bf16[8,7168]{1,0:T(8,128)(2,1)S(1)}, bf16[8,7168]{1,0:T(8,128)(2,1)S(1)}, u32[]{:S(2)}, u32[]{:S(2)}) collective-permute-start(bf16[8,7168]{1,0:T(8,128)(2,1)S(1)} %collective-permute-done.4.refs_2_), channel_id=1, source_target_pairs={{0,2},{1,3},{2,0},{3,1},{4,6},{5,7},{6,4},{7,5},{8,10},{9,11},{10,... | collective-permute-start | bytes 344072 | tf_op jit(solution)/shard_map/ppermute | solution.py:218
  16.0 0.1 collective-permute-start.8
  16.1 1.1 %collective-permute-done.3.refs_2_ = bf16[8,7168]{1,0:T(8,128)(2,1)S(1)} collective-permute-done((bf16[8,7168]{1,0:T(8,128)(2,1)S(1)}, bf16[8,7168]{1,0:T(8,128)(2,1)S(1)}, u32[]{:S(2)}, u32[]{:S(2)}) %collective-permute-start.3) | collective-permute-done | bytes 114720 | tf_op jit(solution)/shard_map/ppermute | solution.py:218
  17.2 0.8 %collective-permute-done.2.refs_1_ = bf16[8,7168]{1,0:T(8,128)(2,1)S(1)} collective-permute-done((bf16[8,7168]{1,0:T(8,128)(2,1)S(1)}, bf16[8,7168]{1,0:T(8,128)(2,1)S(1)}, u32[]{:S(2)}, u32[]{:S(2)}) %collective-permute-start.2) | collective-permute-done | bytes 114720 | tf_op jit(solution)/shard_map/ppermute | solution.py:218
  18.0 1.6 %collective-permute-done.1.refs_0_ = bf16[8,7168]{1,0:T(8,128)(2,1)S(1)} collective-permute-done((bf16[8,7168]{1,0:T(8,128)(2,1)S(1)}, bf16[8,7168]{1,0:T(8,128)(2,1)S(1)}, u32[]{:S(2)}, u32[]{:S(2)}) %collective-permute-start.1) | collective-permute-done | bytes 114720 | tf_op jit(solution)/shard_map/ppermute | solution.py:218
  19.6 1.2 %collective-permute-done.5.refs_3_ = bf16[8,7168]{1,0:T(8,128)(2,1)S(1)} collective-permute-done((bf16[8,7168]{1,0:T(8,128)(2,1)S(1)}, bf16[8,7168]{1,0:T(8,128)(2,1)S(1)}, u32[]{:S(2)}, u32[]{:S(2)}) %collective-permute-start.5) | collective-permute-done | bytes 114720 | tf_op jit(solution)/shard_map/ppermute | solution.py:218
  20.8 0.1 collective-permute-start.7
  20.9 1.8 %collective-permute-done.7.refs_5_ = bf16[32,7168]{1,0:T(8,128)(2,1)S(1)} collective-permute-done((bf16[32,7168]{1,0:T(8,128)(2,1)S(1)}, bf16[32,7168]{1,0:T(8,128)(2,1)S(1)}, u32[]{:S(2)}, u32[]{:S(2)}) %collective-permute-start.7) | collective-permute-done | bytes 458784 | tf_op jit(solution)/shard_map/ppermute | solution.py:218
  22.7 1.7 %shard_map.78 = (bf16[32,7168]{1,0:T(8,128)(2,1)S(1)}, bf16[32,7168]{1,0:T(8,128)(2,1)S(1)}, bf16[32,7168]{1,0:T(8,128)(2,1)S(1)}, bf16[32,7168]{1,0:T(8,128)(2,1)S(1)}) custom-call(bf16[7168,256]{1,0:T(8,128)(2,1)S(1)} %copy-done, bf16[7168,256]{1,0:T(8,128)(2,1)S(1)} %copy-done.1, bf16[256,7168]{1,0:T(8,128)(2,1)S(1)} %copy-done.2, ...), custom_call_target="tpu_custom_call" | custom-call | flops 1409286144 | bytes 11010048 | tf_op jit(solution)/shard_map/pallas_call | solution.py:33
  24.4 0.2 collective-permute-start.10
  24.6 0.4 collective-permute-start.9
  25.0 1.3 %collective-permute-done.10.refs_1_ = bf16[32,7168]{1,0:T(8,128)(2,1)S(1)} collective-permute-done((bf16[32,7168]{1,0:T(8,128)(2,1)S(1)}, bf16[32,7168]{1,0:T(8,128)(2,1)S(1)}, u32[]{:S(2)}, u32[]{:S(2)}) %collective-permute-start.10) | collective-permute-done | bytes 458784 | tf_op jit(solution)/shard_map/ppermute | solution.py:218
  26.3 0.1 shard_map.79
  26.4 0.7 %collective-permute-start.11 = (bf16[8,10752]{1,0:T(8,128)(2,1)S(1)}, bf16[8,10752]{1,0:T(8,128)(2,1)S(1)}, u32[]{:S(2)}, u32[]{:S(2)}) collective-permute-start(bf16[8,10752]{1,0:T(8,128)(2,1)S(1)} %get-tuple-element.29), channel_id=1, source_target_pairs={{0,2},{1,3},{2,0},{3,1},{4,6},{5,7},{6,4},{7,5},{8,10},{9,11},{10,... | collective-permute-start | bytes 516104 | tf_op jit(solution)/shard_map/ppermute | solution.py:218
  27.1 1.8 %collective-permute-start.12 = (bf16[8,10752]{1,0:T(8,128)(2,1)S(1)}, bf16[8,10752]{1,0:T(8,128)(2,1)S(1)}, u32[]{:S(2)}, u32[]{:S(2)}) collective-permute-start(bf16[8,10752]{1,0:T(8,128)(2,1)S(1)} %get-tuple-element.30), channel_id=1, source_target_pairs={{0,4},{1,5},{2,6},{3,7},{4,0},{5,1},{6,2},{7,3},{8,12},{9,13},{10,... | collective-permute-start | bytes 516104 | tf_op jit(solution)/shard_map/ppermute | solution.py:218
  28.9 1.1 %collective-permute-start.13 = (bf16[8,7168]{1,0:T(8,128)(2,1)S(1)}, bf16[8,7168]{1,0:T(8,128)(2,1)S(1)}, u32[]{:S(2)}, u32[]{:S(2)}) collective-permute-start(bf16[8,7168]{1,0:T(8,128)(2,1)S(1)} %get-tuple-element.31), channel_id=1, source_target_pairs={{0,6},{1,7},{2,4},{3,5},{4,2},{5,3},{6,0},{7,1},{8,14},{9,15},{10,... | collective-permute-start | bytes 344072 | tf_op jit(solution)/shard_map/ppermute | solution.py:218
  30.0 6.5 %collective-permute-done.13.refs_3_ = bf16[8,7168]{1,0:T(8,128)(2,1)S(1)} collective-permute-done((bf16[8,7168]{1,0:T(8,128)(2,1)S(1)}, bf16[8,7168]{1,0:T(8,128)(2,1)S(1)}, u32[]{:S(2)}, u32[]{:S(2)}) %collective-permute-start.13) | collective-permute-done | bytes 114720 | tf_op jit(solution)/shard_map/ppermute | solution.py:218
  36.6 2.9 %collective-permute-start.16 = (bf16[8,7168]{1,0:T(8,128)(2,1)S(1)}, bf16[8,7168]{1,0:T(8,128)(2,1)S(1)}, u32[]{:S(2)}, u32[]{:S(2)}) collective-permute-start(bf16[8,7168]{1,0:T(8,128)(2,1)S(1)} %shard_map.81.refs_4_), channel_id=1, source_target_pairs={{0,12},{1,13},{2,14},{3,15},{4,8},{5,9},{6,10},{7,11},{8,4},{9,5},... | collective-permute-start | bytes 344072 | tf_op jit(solution)/shard_map/ppermute | solution.py:218
  39.6 0.1 shard_map.82
  39.7 1.3 %collective-permute-start.14 = (bf16[8,7168]{1,0:T(8,128)(2,1)S(1)}, bf16[8,7168]{1,0:T(8,128)(2,1)S(1)}, u32[]{:S(2)}, u32[]{:S(2)}) collective-permute-start(bf16[8,7168]{1,0:T(8,128)(2,1)S(1)} %get-tuple-element.33), channel_id=1, source_target_pairs={{0,2},{1,3},{2,0},{3,1},{4,6},{5,7},{6,4},{7,5},{8,10},{9,11},{10,... | collective-permute-start | bytes 344072 | tf_op jit(solution)/shard_map/ppermute | solution.py:218
  41.0 3.0 %collective-permute-done.16.refs_0_.refs_4_ = bf16[8,7168]{1,0:T(8,128)(2,1)S(1)} collective-permute-done((bf16[8,7168]{1,0:T(8,128)(2,1)S(1)}, bf16[8,7168]{1,0:T(8,128)(2,1)S(1)}, u32[]{:S(2)}, u32[]{:S(2)}) %collective-permute-start.16) | collective-permute-done | bytes 114720 | tf_op jit(solution)/shard_map/ppermute | solution.py:218
  44.0 0.6 %collective-permute-done.14.refs_2_ = bf16[8,7168]{1,0:T(8,128)(2,1)S(1)} collective-permute-done((bf16[8,7168]{1,0:T(8,128)(2,1)S(1)}, bf16[8,7168]{1,0:T(8,128)(2,1)S(1)}, u32[]{:S(2)}, u32[]{:S(2)}) %collective-permute-start.14) | collective-permute-done | bytes 114720 | tf_op jit(solution)/shard_map/ppermute | solution.py:218
  44.5 1.2 %collective-permute-done.15.refs_3_ = bf16[8,7168]{1,0:T(8,128)(2,1)S(1)} collective-permute-done((bf16[8,7168]{1,0:T(8,128)(2,1)S(1)}, bf16[8,7168]{1,0:T(8,128)(2,1)S(1)}, u32[]{:S(2)}, u32[]{:S(2)}) %collective-permute-start.15) | collective-permute-done | bytes 114720 | tf_op jit(solution)/shard_map/ppermute | solution.py:218
  45.7 1.2 %shard_map.84 = bf16[64,7168]{1,0:T(8,128)(2,1)} custom-call(bf16[64,48]{1,0:T(8,128)(2,1)S(1)} %get-tuple-element.22.refs_0_, f32[8,7168]{1,0:T(8,128)S(1)} %get-tuple-element.32.refs_1_, bf16[8,7168]{1,0:T(8,128)(2,1)S(1)} %collective-permute-done.14.refs_2_, bf16[8,7168]{1,0:T(8,128)(2,1)S(1)} %collective-permute-done.15.refs_3_, ...), custom_call_target="tpu_custom_call" | custom-call | flops 44040192 | bytes 1835008 | tf_op jit(solution)/shard_map/pallas_call | solution.py:33
  (20 shorter events, 0.2 us)
Async XLA Ops:
  1.6 9.1 %collective-permute-start = (bf16[8,7168]{1,0:T(8,128)(2,1)S(1)}, bf16[8,7168]{1,0:T(8,128)(2,1)S(1)}, u32[]{:S(2)}, u32[]{:S(2)}) collective-permute-start(bf16[8,7168]{1,0:T(8,128)(2,1)S(1)} %get-tuple-element.23), channel_id=1, source_target_pairs={{0,12},{1,13},{2,14},{3,15},{4,8},{5,9},{6,10},{7,11},{8,4},{9,5},... | collective-permute-start | bytes 344072 | tf_op jit(solution)/shard_map/ppermute | solution.py:218
  6.7 7.5 %collective-permute-start.4 = (bf16[8,7168]{1,0:T(8,128)(2,1)S(1)}, bf16[8,7168]{1,0:T(8,128)(2,1)S(1)}, u32[]{:S(2)}, u32[]{:S(2)}) collective-permute-start(bf16[8,7168]{1,0:T(8,128)(2,1)S(1)} %get-tuple-element.20.refs_0_), channel_id=1, source_target_pairs={{0,4},{1,5},{2,6},{3,7},{4,0},{5,1},{6,2},{7,3},{8,12},{9,13},{10,... | collective-permute-start | bytes 344072 | tf_op jit(solution)/shard_map/ppermute | solution.py:218
  6.8 15.9 %copy-start = (bf16[7168,256]{1,0:T(8,128)(2,1)S(1)}, bf16[7168,256]{1,0:T(8,128)(2,1)}, u32[]{:S(2)}) copy-start(bf16[7168,256]{1,0:T(8,128)(2,1)} %refs_0_.3) | copy-start | bytes 11010052
  6.8 15.9 %copy-start.1 = (bf16[7168,256]{1,0:T(8,128)(2,1)S(1)}, bf16[7168,256]{1,0:T(8,128)(2,1)}, u32[]{:S(2)}) copy-start(bf16[7168,256]{1,0:T(8,128)(2,1)} %refs_1_.1) | copy-start | bytes 11010052
  6.8 15.9 %copy-start.2 = (bf16[256,7168]{1,0:T(8,128)(2,1)S(1)}, bf16[256,7168]{1,0:T(8,128)(2,1)}, u32[]{:S(2)}) copy-start(bf16[256,7168]{1,0:T(8,128)(2,1)} %refs_2_.1) | copy-start | bytes 11010052
  6.9 9.1 %collective-permute-start.6 = (bf16[8,7168]{1,0:T(8,128)(2,1)S(1)}, bf16[8,7168]{1,0:T(8,128)(2,1)S(1)}, u32[]{:S(2)}, u32[]{:S(2)}) collective-permute-start(bf16[8,7168]{1,0:T(8,128)(2,1)S(1)} %get-tuple-element.24.refs_0_), channel_id=1, source_target_pairs={{0,2},{1,3},{2,0},{3,1},{4,6},{5,7},{6,4},{7,5},{8,10},{9,11},{10,... | collective-permute-start | bytes 344072 | tf_op jit(solution)/shard_map/ppermute | solution.py:218
  10.8 6.4 %collective-permute-start.3 = (bf16[8,7168]{1,0:T(8,128)(2,1)S(1)}, bf16[8,7168]{1,0:T(8,128)(2,1)S(1)}, u32[]{:S(2)}, u32[]{:S(2)}) collective-permute-start(bf16[8,7168]{1,0:T(8,128)(2,1)S(1)} %collective-permute-done.refs_0_.refs_3_), channel_id=1, source_target_pairs={{0,6},{1,7},{2,4},{3,5},{4,2},{5,3},{6,0},{7,1},{8,14},{9,15},{10,... | collective-permute-start | bytes 344072 | tf_op jit(solution)/shard_map/ppermute | solution.py:218
  13.0 5.0 %collective-permute-start.2 = (bf16[8,7168]{1,0:T(8,128)(2,1)S(1)}, bf16[8,7168]{1,0:T(8,128)(2,1)S(1)}, u32[]{:S(2)}, u32[]{:S(2)}) collective-permute-start(bf16[8,7168]{1,0:T(8,128)(2,1)S(1)} %collective-permute-done.refs_0_.refs_3_), channel_id=1, source_target_pairs={{0,4},{1,5},{2,6},{3,7},{4,0},{5,1},{6,2},{7,3},{8,12},{9,13},{10,... | collective-permute-start | bytes 344072 | tf_op jit(solution)/shard_map/ppermute | solution.py:218
  14.0 5.6 %collective-permute-start.1 = (bf16[8,7168]{1,0:T(8,128)(2,1)S(1)}, bf16[8,7168]{1,0:T(8,128)(2,1)S(1)}, u32[]{:S(2)}, u32[]{:S(2)}) collective-permute-start(bf16[8,7168]{1,0:T(8,128)(2,1)S(1)} %collective-permute-done.refs_0_.refs_3_), channel_id=1, source_target_pairs={{0,2},{1,3},{2,0},{3,1},{4,6},{5,7},{6,4},{7,5},{8,10},{9,11},{10,... | collective-permute-start | bytes 344072 | tf_op jit(solution)/shard_map/ppermute | solution.py:218
  14.3 6.5 %collective-permute-start.5 = (bf16[8,7168]{1,0:T(8,128)(2,1)S(1)}, bf16[8,7168]{1,0:T(8,128)(2,1)S(1)}, u32[]{:S(2)}, u32[]{:S(2)}) collective-permute-start(bf16[8,7168]{1,0:T(8,128)(2,1)S(1)} %collective-permute-done.4.refs_2_), channel_id=1, source_target_pairs={{0,2},{1,3},{2,0},{3,1},{4,6},{5,7},{6,4},{7,5},{8,10},{9,11},{10,... | collective-permute-start | bytes 344072 | tf_op jit(solution)/shard_map/ppermute | solution.py:218
  16.0 4.9 %collective-permute-start.8 = (bf16[32,7168]{1,0:T(8,128)(2,1)S(1)}, bf16[32,7168]{1,0:T(8,128)(2,1)S(1)}, u32[]{:S(2)}, u32[]{:S(2)}) collective-permute-start(bf16[32,7168]{1,0:T(8,128)(2,1)S(1)} %shard_map.77.refs_4_), channel_id=1, source_target_pairs={{0,1},{1,0},{2,3},{3,2},{4,5},{5,4},{6,7},{7,6},{8,9},{9,8},{10,11... | collective-permute-start | bytes 1376264 | tf_op jit(solution)/shard_map/ppermute | solution.py:218
  20.8 1.9 %collective-permute-start.7 = (bf16[32,7168]{1,0:T(8,128)(2,1)S(1)}, bf16[32,7168]{1,0:T(8,128)(2,1)S(1)}, u32[]{:S(2)}, u32[]{:S(2)}) collective-permute-start(bf16[32,7168]{1,0:T(8,128)(2,1)S(1)} %shard_map.75.refs_3_), channel_id=1, source_target_pairs={{0,1},{1,0},{2,3},{3,2},{4,5},{5,4},{6,7},{7,6},{8,9},{9,8},{10,11... | collective-permute-start | bytes 1376264 | tf_op jit(solution)/shard_map/ppermute | solution.py:218
  24.4 1.9 %collective-permute-start.10 = (bf16[32,7168]{1,0:T(8,128)(2,1)S(1)}, bf16[32,7168]{1,0:T(8,128)(2,1)S(1)}, u32[]{:S(2)}, u32[]{:S(2)}) collective-permute-start(bf16[32,7168]{1,0:T(8,128)(2,1)S(1)} %get-tuple-element.28), channel_id=1, source_target_pairs={{0,1},{1,0},{2,3},{3,2},{4,5},{5,4},{6,7},{7,6},{8,9},{9,8},{10,11... | collective-permute-start | bytes 1376264 | tf_op jit(solution)/shard_map/ppermute | solution.py:218
  24.6 5.4 %collective-permute-start.9 = (bf16[32,7168]{1,0:T(8,128)(2,1)S(1)}, bf16[32,7168]{1,0:T(8,128)(2,1)S(1)}, u32[]{:S(2)}, u32[]{:S(2)}) collective-permute-start(bf16[32,7168]{1,0:T(8,128)(2,1)S(1)} %get-tuple-element.26), channel_id=1, source_target_pairs={{0,1},{1,0},{2,3},{3,2},{4,5},{5,4},{6,7},{7,6},{8,9},{9,8},{10,11... | collective-permute-start | bytes 1376264 | tf_op jit(solution)/shard_map/ppermute | solution.py:218
  26.4 10.1 %collective-permute-start.11 = (bf16[8,10752]{1,0:T(8,128)(2,1)S(1)}, bf16[8,10752]{1,0:T(8,128)(2,1)S(1)}, u32[]{:S(2)}, u32[]{:S(2)}) collective-permute-start(bf16[8,10752]{1,0:T(8,128)(2,1)S(1)} %get-tuple-element.29), channel_id=1, source_target_pairs={{0,2},{1,3},{2,0},{3,1},{4,6},{5,7},{6,4},{7,5},{8,10},{9,11},{10,... | collective-permute-start | bytes 516104 | tf_op jit(solution)/shard_map/ppermute | solution.py:218
  27.1 9.4 %collective-permute-start.12 = (bf16[8,10752]{1,0:T(8,128)(2,1)S(1)}, bf16[8,10752]{1,0:T(8,128)(2,1)S(1)}, u32[]{:S(2)}, u32[]{:S(2)}) collective-permute-start(bf16[8,10752]{1,0:T(8,128)(2,1)S(1)} %get-tuple-element.30), channel_id=1, source_target_pairs={{0,4},{1,5},{2,6},{3,7},{4,0},{5,1},{6,2},{7,3},{8,12},{9,13},{10,... | collective-permute-start | bytes 516104 | tf_op jit(solution)/shard_map/ppermute | solution.py:218
  28.9 7.7 %collective-permute-start.13 = (bf16[8,7168]{1,0:T(8,128)(2,1)S(1)}, bf16[8,7168]{1,0:T(8,128)(2,1)S(1)}, u32[]{:S(2)}, u32[]{:S(2)}) collective-permute-start(bf16[8,7168]{1,0:T(8,128)(2,1)S(1)} %get-tuple-element.31), channel_id=1, source_target_pairs={{0,6},{1,7},{2,4},{3,5},{4,2},{5,3},{6,0},{7,1},{8,14},{9,15},{10,... | collective-permute-start | bytes 344072 | tf_op jit(solution)/shard_map/ppermute | solution.py:218
  36.6 7.3 %collective-permute-start.16 = (bf16[8,7168]{1,0:T(8,128)(2,1)S(1)}, bf16[8,7168]{1,0:T(8,128)(2,1)S(1)}, u32[]{:S(2)}, u32[]{:S(2)}) collective-permute-start(bf16[8,7168]{1,0:T(8,128)(2,1)S(1)} %shard_map.81.refs_4_), channel_id=1, source_target_pairs={{0,12},{1,13},{2,14},{3,15},{4,8},{5,9},{6,10},{7,11},{8,4},{9,5},... | collective-permute-start | bytes 344072 | tf_op jit(solution)/shard_map/ppermute | solution.py:218
  39.7 4.9 %collective-permute-start.14 = (bf16[8,7168]{1,0:T(8,128)(2,1)S(1)}, bf16[8,7168]{1,0:T(8,128)(2,1)S(1)}, u32[]{:S(2)}, u32[]{:S(2)}) collective-permute-start(bf16[8,7168]{1,0:T(8,128)(2,1)S(1)} %get-tuple-element.33), channel_id=1, source_target_pairs={{0,2},{1,3},{2,0},{3,1},{4,6},{5,7},{6,4},{7,5},{8,10},{9,11},{10,... | collective-permute-start | bytes 344072 | tf_op jit(solution)/shard_map/ppermute | solution.py:218
  40.9 4.8 %collective-permute-start.15 = (bf16[8,7168]{1,0:T(8,128)(2,1)S(1)}, bf16[8,7168]{1,0:T(8,128)(2,1)S(1)}, u32[]{:S(2)}, u32[]{:S(2)}) collective-permute-start(bf16[8,7168]{1,0:T(8,128)(2,1)S(1)} %get-tuple-element.34), channel_id=1, source_target_pairs={{0,4},{1,5},{2,6},{3,7},{4,0},{5,1},{6,2},{7,3},{8,12},{9,13},{10,... | collective-permute-start | bytes 344072 | tf_op jit(solution)/shard_map/ppermute | solution.py:218

commit v5 on v4

--- a/solution.py
+++ b/solution.py
@@ -121,52 +121,23 @@
             first += out.shape[0]
 
 
-def halves(width):
-    middle = width // 256 * 128
-    return slice(0, middle), slice(middle, width)
-
-
-def extras(width, blocks, half):
-    size = half.stop - half.start
-    per = -(-size // (128 * blocks)) * 128
-    spans = [(at, min(at + per, size)) for at in range(0, size, per)]
-    return [(n, slice(width, width + b - a), slice(half.start + a, half.start + b)) for n, (a, b) in enumerate(spans)]
-
-
-def message_width(width, blocks):
-    return width + max(-(-(h.stop - h.start) // (128 * blocks)) * 128 for h in halves(width))
-
-
 def rows_of(n):
     return slice(CAP * n, CAP * (n + 1))
 
 
-def homeward_kernel(home_ref, back_ref, *outs):
-    sides, corner = outs[:2], outs[2]
-    rows, width = corner.shape
-    blocks = rows // CAP
-    left, right = halves(width)
-    for side, half in zip(sides, (right, left)):
-        for n, there, here in extras(width, blocks, half):
-            for at in chunks(here.stop - here.start):
-                at_here = slice(here.start + at.start, here.start + at.stop)
-                at_there = slice(there.start + at.start, there.start + at.stop)
-                total = home_ref[:, at_here].astype(F32) + back_ref[:, at_here].astype(F32)
-                for k, out in enumerate(outs):
-                    out[:, at_here] = total[rows * k : rows * (k + 1)].astype(BF16)
-                mine = total[3 * rows :]
-                if blocks == 1:
-                    side[:, at_there] = mine.astype(BF16)
-                else:
-                    before = side[:, at_there].astype(F32)
-                    pieces = [mine if b == n else before[rows_of(b)] for b in range(blocks)]
-                    side[:, at_there] = jnp.concatenate(pieces, axis=0).astype(BF16)
-
-
-def kept_kernel(skip, home_ref, back_ref, out_ref):
+def pair_kernel(first, home_ref, back_ref, *outs):
     for at in chunks(home_ref.shape[1]):
         total = home_ref[:, at].astype(F32) + back_ref[:, at].astype(F32)
-        out_ref[:, at] = total[skip:]
+        row = first
+        for out in outs:
+            out[:, at] = total[row : row + out.shape[0]].astype(out.dtype)
+            row += out.shape[0]
+
+
+def passed_kernel(first, home_ref, back_ref, more_ref, out_ref):
+    for at in chunks(home_ref.shape[1]):
+        total = home_ref[:, at].astype(F32) + back_ref[:, at].astype(F32)
+        out_ref[:, at] = (total[first : first + CAP] + more_ref[:, at].astype(F32)).astype(BF16)
 
 
 def total_kernel(*refs):
@@ -175,20 +146,6 @@
         total = sum(ref[:, at].astype(F32) for ref in arrays)
         for n, out in enumerate(outs):
             out[:, at] = total[rows_of(n)].astype(BF16)
-
-
-def near_kernel(home_ref, back_ref, side_one, side_two, kept_ref, one_ref, two_ref):
-    width = home_ref.shape[1]
-    blocks = side_one.shape[0] // CAP
-    left, right = halves(width)
-    outs = (one_ref, two_ref)
-    for side, half, passed in ((side_two, left, 0), (side_one, right, 1)):
-        for n, there, here in extras(width, blocks, half):
-            total = home_ref[:, here].astype(F32) + back_ref[:, here].astype(F32)
-            kept_ref[:, here] = total[rows_of(0)]
-            more = side[:, there].astype(F32)[rows_of(n)]
-            outs[passed][:, here] = (total[rows_of(1 + passed)] + more).astype(BF16)
-            outs[1 - passed][:, here] = total[rows_of(2 - passed)].astype(BF16)
 
 
 def combine_kernel(weights_ref, *refs):
@@ -259,7 +216,6 @@
     first = [own, swap(own, SIDES[0]), side_two]
     past = swap(first[2], SIDES[0])
     rows = CAP * (waves - 1)
-    message = shape(rows, message_width(width, waves - 1))
     far = heads[0] if waves == 2 else stack(heads)
     sent = [swap(far, s) for s in SIDES + (CORNER,)]
     marks = [call(mark_kernel, shape(CAP, 128, F32), [x]) for x in heads]
@@ -275,24 +231,22 @@
         limit=24,
     )
 
-    *sides, corner = call(
-        homeward_kernel,
-        [message, message, shape(rows, width)],
-        [late, swap(late_away, 1)],
-        moved=20 * rows * width,
-    )
-    sides = [swap(x, s) for x, s in zip(sides, SIDES)]
-    corner = swap(corner, CORNER)
+    def pair(home, back, first, outs, after=()):
+        body = functools.partial(pair_kernel, CAP * first)
+        moved = sum(6 * out.shape[0] * width for out in outs)
+        return call(body, outs, [home, back], after, moved=moved)
+
+    *sent, past = pair(late, swap(late_away, 1), 0, [shape(rows, width)] * 3 + [block])
+    sent = [swap(x, s) for x, s in zip(sent, SIDES + (CORNER,))]
+    past = swap(past, SIDES[0])
     back = swap(early_away, 1)
-    kept = call(
-        functools.partial(kept_kernel, CAP * len(first)), shape(rows, width, F32), [early, back], moved=8 * rows * width
-    )
-    totals = call(total_kernel, [block] * (waves - 1), [kept] + sides + [corner], moved=10 * rows * width)
+    (kept,) = pair(early, back, len(first), [shape(rows, width, F32)])
+    totals = call(total_kernel, [block] * (waves - 1), [kept] + sent, moved=10 * rows * width)
     returned = [cross(totals[j - 1], j) for j in others]
-    kept, *near = call(
-        near_kernel, [shape(CAP, width, F32), block, block], [early, back] + sides, after=totals, moved=14 * CAP * width
-    )
-    near = [kept] + [swap(x, s) for x, s in zip(near, SIDES)]
+    kept, one = pair(early, back, 0, [shape(CAP, width, F32), block], after=totals)
+    body = functools.partial(passed_kernel, 2 * CAP)
+    two = call(body, block, [early, back, past], after=[one], moved=10 * CAP * width)
+    near = [kept, swap(one, SIDES[0]), swap(two, SIDES[1])]
     marks = [call(mark_kernel, shape(CAP, 128, F32), [x]) for x in returned]
     return call(
         combine_kernel,

time: 47.1 us -> 45.4 us (0.964)
  waiting for transfers between devices: 21.4 us -> 19.1 us
  starting transfers between devices: 20.4 us -> 21.1 us
    ppermute x17 -> x18, waiting for transfers between devices: 21.4 us -> 19.1 us  [swap(): return lax.ppermute(x, 'tp', [(i, i ^ mask) for i in range(devices)])]
    ppermute x17 -> x18, starting transfers between devices: 20.4 us -> 21.1 us  [swap(): return lax.ppermute(x, 'tp', [(i, i ^ mask) for i in range(devices)])]
    pallas_call x12 -> x13, Pallas kernels: 4.93 us -> 4.94 us  [call(): pl.pallas_call(run, out_shape=outs, in_specs=[space(pltpu.HBM)] * left +...]
  transfers between devices with their start and end apart: 17 -> 18, of which waited for: 11 -> 12; matrix products, arithmetic and copies ran while one was open for 0% -> 0% of each run, Pallas kernels for 1% -> 1%
where the time goes in v5:
time: 45.4 us; the launch traced here: 45.2 us
  starting transfers between devices  21.1 us (46%)
  waiting for transfers between devices  19.1 us (42%)
  Pallas kernels  4.94 us (11%)
    ppermute x18, starting transfers between devices, swap(): return lax.ppermute(x, 'tp', [(i, i ^ mask) for i in range(devices)])  21.1 us
    ppermute x18, waiting for transfers between devices, swap(): return lax.ppermute(x, 'tp', [(i, i ^ mask) for i in range(devices)])  19.1 us
    pallas_call x13, Pallas kernels, call(): pl.pallas_call(run, out_shape=outs, in_specs=[space(pltpu.HBM)] * left +...  4.94 us
  transfers between devices with their start and end apart: 18, of which 12 were waited for; matrix products, arithmetic and copies ran while one was open for 0% of the time, Pallas kernels for 1%

profile of v5, /device:TPU:0, one launch (start us, length us, event | category | flops | bytes accessed | tf_op | source)
XLA Modules:
  0.0 45.2 jit_solution(15892273105554611762)
XLA Ops:
  0.0 1.6 %shard_map.73 = (bf16[8,7168]{1,0:T(8,128)(2,1)S(1)}, bf16[8,7168]{1,0:T(8,128)(2,1)S(1)}, f32[16,64]{1,0:T(8,128)S(1)}) custom-call(bf16[64,7168]{1,0:T(8,128)(2,1)} %refs_0_.2, f32[1,7168]{1,0:T(1,128)} %bitcast.3, s32[8,64]{1,0:T(8,128)} %bitcast.4, f32[8,64]{1,0:T(8,128)} %bitcast.5), custom_call_target="tpu_custom_call" | custom-call | flops 14680064 | bytes 917504 | tf_op jit(solution)/shard_map/pallas_call | solution.py:33
  1.6 5.1 %collective-permute-start = (bf16[8,7168]{1,0:T(8,128)(2,1)S(1)}, bf16[8,7168]{1,0:T(8,128)(2,1)S(1)}, u32[]{:S(2)}, u32[]{:S(2)}) collective-permute-start(bf16[8,7168]{1,0:T(8,128)(2,1)S(1)} %get-tuple-element.23), channel_id=1, source_target_pairs={{0,12},{1,13},{2,14},{3,15},{4,8},{5,9},{6,10},{7,11},{8,4},{9,5},... | collective-permute-start | bytes 344072 | tf_op jit(solution)/shard_map/ppermute | solution.py:175
  6.8 0.1 shard_map.74
  6.9 1.6 %collective-permute-start.6 = (bf16[8,7168]{1,0:T(8,128)(2,1)S(1)}, bf16[8,7168]{1,0:T(8,128)(2,1)S(1)}, u32[]{:S(2)}, u32[]{:S(2)}) collective-permute-start(bf16[8,7168]{1,0:T(8,128)(2,1)S(1)} %get-tuple-element.24.refs_0_), channel_id=1, source_target_pairs={{0,2},{1,3},{2,0},{3,1},{4,6},{5,7},{6,4},{7,5},{8,10},{9,11},{10,... | collective-permute-start | bytes 344072 | tf_op jit(solution)/shard_map/ppermute | solution.py:175
  8.4 2.3 %collective-permute-done.refs_0_.refs_3_ = bf16[8,7168]{1,0:T(8,128)(2,1)S(1)} collective-permute-done((bf16[8,7168]{1,0:T(8,128)(2,1)S(1)}, bf16[8,7168]{1,0:T(8,128)(2,1)S(1)}, u32[]{:S(2)}, u32[]{:S(2)}) %collective-permute-start) | collective-permute-done | bytes 114720 | tf_op jit(solution)/shard_map/ppermute | solution.py:175
  10.8 2.3 %collective-permute-start.3 = (bf16[8,7168]{1,0:T(8,128)(2,1)S(1)}, bf16[8,7168]{1,0:T(8,128)(2,1)S(1)}, u32[]{:S(2)}, u32[]{:S(2)}) collective-permute-start(bf16[8,7168]{1,0:T(8,128)(2,1)S(1)} %collective-permute-done.refs_0_.refs_3_), channel_id=1, source_target_pairs={{0,6},{1,7},{2,4},{3,5},{4,2},{5,3},{6,0},{7,1},{8,14},{9,15},{10,... | collective-permute-start | bytes 344072 | tf_op jit(solution)/shard_map/ppermute | solution.py:175
  13.0 0.9 %collective-permute-start.2 = (bf16[8,7168]{1,0:T(8,128)(2,1)S(1)}, bf16[8,7168]{1,0:T(8,128)(2,1)S(1)}, u32[]{:S(2)}, u32[]{:S(2)}) collective-permute-start(bf16[8,7168]{1,0:T(8,128)(2,1)S(1)} %collective-permute-done.refs_0_.refs_3_), channel_id=1, source_target_pairs={{0,4},{1,5},{2,6},{3,7},{4,0},{5,1},{6,2},{7,3},{8,12},{9,13},{10,... | collective-permute-start | bytes 344072 | tf_op jit(solution)/shard_map/ppermute | solution.py:175
  14.0 0.3 collective-permute-start.1
  14.3 1.7 %collective-permute-start.5 = (bf16[8,7168]{1,0:T(8,128)(2,1)S(1)}, bf16[8,7168]{1,0:T(8,128)(2,1)S(1)}, u32[]{:S(2)}, u32[]{:S(2)}) collective-permute-start(bf16[8,7168]{1,0:T(8,128)(2,1)S(1)} %collective-permute-done.4.refs_2_), channel_id=1, source_target_pairs={{0,2},{1,3},{2,0},{3,1},{4,6},{5,7},{6,4},{7,5},{8,10},{9,11},{10,... | collective-permute-start | bytes 344072 | tf_op jit(solution)/shard_map/ppermute | solution.py:175
  16.0 0.1 collective-permute-start.8
  16.1 1.1 %collective-permute-done.3.refs_2_ = bf16[8,7168]{1,0:T(8,128)(2,1)S(1)} collective-permute-done((bf16[8,7168]{1,0:T(8,128)(2,1)S(1)}, bf16[8,7168]{1,0:T(8,128)(2,1)S(1)}, u32[]{:S(2)}, u32[]{:S(2)}) %collective-permute-start.3) | collective-permute-done | bytes 114720 | tf_op jit(solution)/shard_map/ppermute | solution.py:175
  17.2 0.8 %collective-permute-done.2.refs_1_ = bf16[8,7168]{1,0:T(8,128)(2,1)S(1)} collective-permute-done((bf16[8,7168]{1,0:T(8,128)(2,1)S(1)}, bf16[8,7168]{1,0:T(8,128)(2,1)S(1)}, u32[]{:S(2)}, u32[]{:S(2)}) %collective-permute-start.2) | collective-permute-done | bytes 114720 | tf_op jit(solution)/shard_map/ppermute | solution.py:175
  18.0 1.6 %collective-permute-done.1.refs_0_ = bf16[8,7168]{1,0:T(8,128)(2,1)S(1)} collective-permute-done((bf16[8,7168]{1,0:T(8,128)(2,1)S(1)}, bf16[8,7168]{1,0:T(8,128)(2,1)S(1)}, u32[]{:S(2)}, u32[]{:S(2)}) %collective-permute-start.1) | collective-permute-done | bytes 114720 | tf_op jit(solution)/shard_map/ppermute | solution.py:175
  19.6 1.2 %collective-permute-done.5.refs_3_ = bf16[8,7168]{1,0:T(8,128)(2,1)S(1)} collective-permute-done((bf16[8,7168]{1,0:T(8,128)(2,1)S(1)}, bf16[8,7168]{1,0:T(8,128)(2,1)S(1)}, u32[]{:S(2)}, u32[]{:S(2)}) %collective-permute-start.5) | collective-permute-done | bytes 114720 | tf_op jit(solution)/shard_map/ppermute | solution.py:175
  20.9 1.8 %collective-permute-done.7.refs_5_ = bf16[32,7168]{1,0:T(8,128)(2,1)S(1)} collective-permute-done((bf16[32,7168]{1,0:T(8,128)(2,1)S(1)}, bf16[32,7168]{1,0:T(8,128)(2,1)S(1)}, u32[]{:S(2)}, u32[]{:S(2)}) %collective-permute-start.7) | collective-permute-done | bytes 458784 | tf_op jit(solution)/shard_map/ppermute | solution.py:175
  22.7 1.7 %shard_map.78 = (bf16[32,7168]{1,0:T(8,128)(2,1)S(1)}, bf16[32,7168]{1,0:T(8,128)(2,1)S(1)}, bf16[32,7168]{1,0:T(8,128)(2,1)S(1)}, bf16[32,7168]{1,0:T(8,128)(2,1)S(1)}) custom-call(bf16[7168,256]{1,0:T(8,128)(2,1)S(1)} %copy-done, bf16[7168,256]{1,0:T(8,128)(2,1)S(1)} %copy-done.1, bf16[256,7168]{1,0:T(8,128)(2,1)S(1)} %copy-done.2, ...), custom_call_target="tpu_custom_call" | custom-call | flops 1409286144 | bytes 11010048 | tf_op jit(solution)/shard_map/pallas_call | solution.py:33
  24.4 0.2 collective-permute-start.10
  24.6 0.4 collective-permute-start.9
  25.0 1.3 %collective-permute-done.10.refs_1_ = bf16[32,7168]{1,0:T(8,128)(2,1)S(1)} collective-permute-done((bf16[32,7168]{1,0:T(8,128)(2,1)S(1)}, bf16[32,7168]{1,0:T(8,128)(2,1)S(1)}, u32[]{:S(2)}, u32[]{:S(2)}) %collective-permute-start.10) | collective-permute-done | bytes 458784 | tf_op jit(solution)/shard_map/ppermute | solution.py:175
  26.3 0.1 shard_map.80
  26.4 0.7 %collective-permute-start.11 = (bf16[8,7168]{1,0:T(8,128)(2,1)S(1)}, bf16[8,7168]{1,0:T(8,128)(2,1)S(1)}, u32[]{:S(2)}, u32[]{:S(2)}) collective-permute-start(bf16[8,7168]{1,0:T(8,128)(2,1)S(1)} %get-tuple-element.29), channel_id=1, source_target_pairs={{0,2},{1,3},{2,0},{3,1},{4,6},{5,7},{6,4},{7,5},{8,10},{9,11},{10,... | collective-permute-start | bytes 344072 | tf_op jit(solution)/shard_map/ppermute | solution.py:175
  27.1 1.8 %collective-permute-start.12 = (bf16[8,7168]{1,0:T(8,128)(2,1)S(1)}, bf16[8,7168]{1,0:T(8,128)(2,1)S(1)}, u32[]{:S(2)}, u32[]{:S(2)}) collective-permute-start(bf16[8,7168]{1,0:T(8,128)(2,1)S(1)} %get-tuple-element.30), channel_id=1, source_target_pairs={{0,4},{1,5},{2,6},{3,7},{4,0},{5,1},{6,2},{7,3},{8,12},{9,13},{10,... | collective-permute-start | bytes 344072 | tf_op jit(solution)/shard_map/ppermute | solution.py:175
  28.9 1.1 %collective-permute-start.13 = (bf16[8,7168]{1,0:T(8,128)(2,1)S(1)}, bf16[8,7168]{1,0:T(8,128)(2,1)S(1)}, u32[]{:S(2)}, u32[]{:S(2)}) collective-permute-start(bf16[8,7168]{1,0:T(8,128)(2,1)S(1)} %get-tuple-element.31), channel_id=1, source_target_pairs={{0,6},{1,7},{2,4},{3,5},{4,2},{5,3},{6,0},{7,1},{8,14},{9,15},{10,... | collective-permute-start | bytes 344072 | tf_op jit(solution)/shard_map/ppermute | solution.py:175
  30.0 0.6 %collective-permute-start.15 = (bf16[8,7168]{1,0:T(8,128)(2,1)S(1)}, bf16[8,7168]{1,0:T(8,128)(2,1)S(1)}, u32[]{:S(2)}, u32[]{:S(2)}) collective-permute-start(bf16[8,7168]{1,0:T(8,128)(2,1)S(1)} %get-tuple-element.34), channel_id=1, source_target_pairs={{0,2},{1,3},{2,0},{3,1},{4,6},{5,7},{6,4},{7,5},{8,10},{9,11},{10,... | collective-permute-start | bytes 344072 | tf_op jit(solution)/shard_map/ppermute | solution.py:175
  30.7 1.0 %collective-permute-done.11.refs_1_ = bf16[8,7168]{1,0:T(8,128)(2,1)S(1)} collective-permute-done((bf16[8,7168]{1,0:T(8,128)(2,1)S(1)}, bf16[8,7168]{1,0:T(8,128)(2,1)S(1)}, u32[]{:S(2)}, u32[]{:S(2)}) %collective-permute-start.11) | collective-permute-done | bytes 114720 | tf_op jit(solution)/shard_map/ppermute | solution.py:175
  31.7 0.8 %collective-permute-done.12.refs_2_ = bf16[8,7168]{1,0:T(8,128)(2,1)S(1)} collective-permute-done((bf16[8,7168]{1,0:T(8,128)(2,1)S(1)}, bf16[8,7168]{1,0:T(8,128)(2,1)S(1)}, u32[]{:S(2)}, u32[]{:S(2)}) %collective-permute-start.12) | collective-permute-done | bytes 114720 | tf_op jit(solution)/shard_map/ppermute | solution.py:175
  32.4 3.0 %collective-permute-done.13.refs_3_ = bf16[8,7168]{1,0:T(8,128)(2,1)S(1)} collective-permute-done((bf16[8,7168]{1,0:T(8,128)(2,1)S(1)}, bf16[8,7168]{1,0:T(8,128)(2,1)S(1)}, u32[]{:S(2)}, u32[]{:S(2)}) %collective-permute-start.13) | collective-permute-done | bytes 114720 | tf_op jit(solution)/shard_map/ppermute | solution.py:175
  35.5 2.9 %collective-permute-start.17 = (bf16[8,7168]{1,0:T(8,128)(2,1)S(1)}, bf16[8,7168]{1,0:T(8,128)(2,1)S(1)}, u32[]{:S(2)}, u32[]{:S(2)}) collective-permute-start(bf16[8,7168]{1,0:T(8,128)(2,1)S(1)} %shard_map.81.refs_2_), channel_id=1, source_target_pairs={{0,12},{1,13},{2,14},{3,15},{4,8},{5,9},{6,10},{7,11},{8,4},{9,5},... | collective-permute-start | bytes 344072 | tf_op jit(solution)/shard_map/ppermute | solution.py:175
  38.6 1.3 %collective-permute-start.14 = (bf16[8,7168]{1,0:T(8,128)(2,1)S(1)}, bf16[8,7168]{1,0:T(8,128)(2,1)S(1)}, u32[]{:S(2)}, u32[]{:S(2)}) collective-permute-start(bf16[8,7168]{1,0:T(8,128)(2,1)S(1)} %get-tuple-element.33.refs_3_), channel_id=1, source_target_pairs={{0,2},{1,3},{2,0},{3,1},{4,6},{5,7},{6,4},{7,5},{8,10},{9,11},{10,... | collective-permute-start | bytes 344072 | tf_op jit(solution)/shard_map/ppermute | solution.py:175
  39.9 3.0 %collective-permute-done.17.refs_0_.refs_4_ = bf16[8,7168]{1,0:T(8,128)(2,1)S(1)} collective-permute-done((bf16[8,7168]{1,0:T(8,128)(2,1)S(1)}, bf16[8,7168]{1,0:T(8,128)(2,1)S(1)}, u32[]{:S(2)}, u32[]{:S(2)}) %collective-permute-start.17) | collective-permute-done | bytes 114720 | tf_op jit(solution)/shard_map/ppermute | solution.py:175
  42.9 1.1 %collective-permute-done.16.refs_3_ = bf16[8,7168]{1,0:T(8,128)(2,1)S(1)} collective-permute-done((bf16[8,7168]{1,0:T(8,128)(2,1)S(1)}, bf16[8,7168]{1,0:T(8,128)(2,1)S(1)}, u32[]{:S(2)}, u32[]{:S(2)}) %collective-permute-start.16) | collective-permute-done | bytes 114720 | tf_op jit(solution)/shard_map/ppermute | solution.py:175
  44.1 1.2 %shard_map.85 = bf16[64,7168]{1,0:T(8,128)(2,1)} custom-call(bf16[64,48]{1,0:T(8,128)(2,1)S(1)} %get-tuple-element.22.refs_0_, f32[8,7168]{1,0:T(8,128)S(1)} %get-tuple-element.32.refs_1_, bf16[8,7168]{1,0:T(8,128)(2,1)S(1)} %collective-permute-done.14.refs_2_, bf16[8,7168]{1,0:T(8,128)(2,1)S(1)} %collective-permute-done.16.refs_3_, ...), custom_call_target="tpu_custom_call" | custom-call | flops 44040192 | bytes 1835008 | tf_op jit(solution)/shard_map/pallas_call | solution.py:33
  (23 shorter events, 0.4 us)
Async XLA Ops:
  1.6 9.1 %collective-permute-start = (bf16[8,7168]{1,0:T(8,128)(2,1)S(1)}, bf16[8,7168]{1,0:T(8,128)(2,1)S(1)}, u32[]{:S(2)}, u32[]{:S(2)}) collective-permute-start(bf16[8,7168]{1,0:T(8,128)(2,1)S(1)} %get-tuple-element.23), channel_id=1, source_target_pairs={{0,12},{1,13},{2,14},{3,15},{4,8},{5,9},{6,10},{7,11},{8,4},{9,5},... | collective-permute-start | bytes 344072 | tf_op jit(solution)/shard_map/ppermute | solution.py:175
  6.7 7.5 %collective-permute-start.4 = (bf16[8,7168]{1,0:T(8,128)(2,1)S(1)}, bf16[8,7168]{1,0:T(8,128)(2,1)S(1)}, u32[]{:S(2)}, u32[]{:S(2)}) collective-permute-start(bf16[8,7168]{1,0:T(8,128)(2,1)S(1)} %get-tuple-element.20.refs_0_), channel_id=1, source_target_pairs={{0,4},{1,5},{2,6},{3,7},{4,0},{5,1},{6,2},{7,3},{8,12},{9,13},{10,... | collective-permute-start | bytes 344072 | tf_op jit(solution)/shard_map/ppermute | solution.py:175
  6.8 15.9 %copy-start = (bf16[7168,256]{1,0:T(8,128)(2,1)S(1)}, bf16[7168,256]{1,0:T(8,128)(2,1)}, u32[]{:S(2)}) copy-start(bf16[7168,256]{1,0:T(8,128)(2,1)} %refs_0_.3) | copy-start | bytes 11010052
  6.8 15.9 %copy-start.1 = (bf16[7168,256]{1,0:T(8,128)(2,1)S(1)}, bf16[7168,256]{1,0:T(8,128)(2,1)}, u32[]{:S(2)}) copy-start(bf16[7168,256]{1,0:T(8,128)(2,1)} %refs_1_.1) | copy-start | bytes 11010052
  6.8 15.9 %copy-start.2 = (bf16[256,7168]{1,0:T(8,128)(2,1)S(1)}, bf16[256,7168]{1,0:T(8,128)(2,1)}, u32[]{:S(2)}) copy-start(bf16[256,7168]{1,0:T(8,128)(2,1)} %refs_2_.1) | copy-start | bytes 11010052
  6.9 9.1 %collective-permute-start.6 = (bf16[8,7168]{1,0:T(8,128)(2,1)S(1)}, bf16[8,7168]{1,0:T(8,128)(2,1)S(1)}, u32[]{:S(2)}, u32[]{:S(2)}) collective-permute-start(bf16[8,7168]{1,0:T(8,128)(2,1)S(1)} %get-tuple-element.24.refs_0_), channel_id=1, source_target_pairs={{0,2},{1,3},{2,0},{3,1},{4,6},{5,7},{6,4},{7,5},{8,10},{9,11},{10,... | collective-permute-start | bytes 344072 | tf_op jit(solution)/shard_map/ppermute | solution.py:175
  10.8 6.4 %collective-permute-start.3 = (bf16[8,7168]{1,0:T(8,128)(2,1)S(1)}, bf16[8,7168]{1,0:T(8,128)(2,1)S(1)}, u32[]{:S(2)}, u32[]{:S(2)}) collective-permute-start(bf16[8,7168]{1,0:T(8,128)(2,1)S(1)} %collective-permute-done.refs_0_.refs_3_), channel_id=1, source_target_pairs={{0,6},{1,7},{2,4},{3,5},{4,2},{5,3},{6,0},{7,1},{8,14},{9,15},{10,... | collective-permute-start | bytes 344072 | tf_op jit(solution)/shard_map/ppermute | solution.py:175
  13.0 5.0 %collective-permute-start.2 = (bf16[8,7168]{1,0:T(8,128)(2,1)S(1)}, bf16[8,7168]{1,0:T(8,128)(2,1)S(1)}, u32[]{:S(2)}, u32[]{:S(2)}) collective-permute-start(bf16[8,7168]{1,0:T(8,128)(2,1)S(1)} %collective-permute-done.refs_0_.refs_3_), channel_id=1, source_target_pairs={{0,4},{1,5},{2,6},{3,7},{4,0},{5,1},{6,2},{7,3},{8,12},{9,13},{10,... | collective-permute-start | bytes 344072 | tf_op jit(solution)/shard_map/ppermute | solution.py:175
  14.0 5.6 %collective-permute-start.1 = (bf16[8,7168]{1,0:T(8,128)(2,1)S(1)}, bf16[8,7168]{1,0:T(8,128)(2,1)S(1)}, u32[]{:S(2)}, u32[]{:S(2)}) collective-permute-start(bf16[8,7168]{1,0:T(8,128)(2,1)S(1)} %collective-permute-done.refs_0_.refs_3_), channel_id=1, source_target_pairs={{0,2},{1,3},{2,0},{3,1},{4,6},{5,7},{6,4},{7,5},{8,10},{9,11},{10,... | collective-permute-start | bytes 344072 | tf_op jit(solution)/shard_map/ppermute | solution.py:175
  14.3 6.5 %collective-permute-start.5 = (bf16[8,7168]{1,0:T(8,128)(2,1)S(1)}, bf16[8,7168]{1,0:T(8,128)(2,1)S(1)}, u32[]{:S(2)}, u32[]{:S(2)}) collective-permute-start(bf16[8,7168]{1,0:T(8,128)(2,1)S(1)} %collective-permute-done.4.refs_2_), channel_id=1, source_target_pairs={{0,2},{1,3},{2,0},{3,1},{4,6},{5,7},{6,4},{7,5},{8,10},{9,11},{10,... | collective-permute-start | bytes 344072 | tf_op jit(solution)/shard_map/ppermute | solution.py:175
  16.0 4.9 %collective-permute-start.8 = (bf16[32,7168]{1,0:T(8,128)(2,1)S(1)}, bf16[32,7168]{1,0:T(8,128)(2,1)S(1)}, u32[]{:S(2)}, u32[]{:S(2)}) collective-permute-start(bf16[32,7168]{1,0:T(8,128)(2,1)S(1)} %shard_map.77.refs_4_), channel_id=1, source_target_pairs={{0,1},{1,0},{2,3},{3,2},{4,5},{5,4},{6,7},{7,6},{8,9},{9,8},{10,11... | collective-permute-start | bytes 1376264 | tf_op jit(solution)/shard_map/ppermute | solution.py:175
  20.8 1.9 %collective-permute-start.7 = (bf16[32,7168]{1,0:T(8,128)(2,1)S(1)}, bf16[32,7168]{1,0:T(8,128)(2,1)S(1)}, u32[]{:S(2)}, u32[]{:S(2)}) collective-permute-start(bf16[32,7168]{1,0:T(8,128)(2,1)S(1)} %shard_map.75.refs_3_), channel_id=1, source_target_pairs={{0,1},{1,0},{2,3},{3,2},{4,5},{5,4},{6,7},{7,6},{8,9},{9,8},{10,11... | collective-permute-start | bytes 1376264 | tf_op jit(solution)/shard_map/ppermute | solution.py:175
  24.4 1.9 %collective-permute-start.10 = (bf16[32,7168]{1,0:T(8,128)(2,1)S(1)}, bf16[32,7168]{1,0:T(8,128)(2,1)S(1)}, u32[]{:S(2)}, u32[]{:S(2)}) collective-permute-start(bf16[32,7168]{1,0:T(8,128)(2,1)S(1)} %get-tuple-element.28), channel_id=1, source_target_pairs={{0,1},{1,0},{2,3},{3,2},{4,5},{5,4},{6,7},{7,6},{8,9},{9,8},{10,11... | collective-permute-start | bytes 1376264 | tf_op jit(solution)/shard_map/ppermute | solution.py:175
  24.6 6.0 %collective-permute-start.9 = (bf16[32,7168]{1,0:T(8,128)(2,1)S(1)}, bf16[32,7168]{1,0:T(8,128)(2,1)S(1)}, u32[]{:S(2)}, u32[]{:S(2)}) collective-permute-start(bf16[32,7168]{1,0:T(8,128)(2,1)S(1)} %get-tuple-element.26), channel_id=1, source_target_pairs={{0,1},{1,0},{2,3},{3,2},{4,5},{5,4},{6,7},{7,6},{8,9},{9,8},{10,11... | collective-permute-start | bytes 1376264 | tf_op jit(solution)/shard_map/ppermute | solution.py:175
  26.4 5.3 %collective-permute-start.11 = (bf16[8,7168]{1,0:T(8,128)(2,1)S(1)}, bf16[8,7168]{1,0:T(8,128)(2,1)S(1)}, u32[]{:S(2)}, u32[]{:S(2)}) collective-permute-start(bf16[8,7168]{1,0:T(8,128)(2,1)S(1)} %get-tuple-element.29), channel_id=1, source_target_pairs={{0,2},{1,3},{2,0},{3,1},{4,6},{5,7},{6,4},{7,5},{8,10},{9,11},{10,... | collective-permute-start | bytes 344072 | tf_op jit(solution)/shard_map/ppermute | solution.py:175
  27.1 5.3 %collective-permute-start.12 = (bf16[8,7168]{1,0:T(8,128)(2,1)S(1)}, bf16[8,7168]{1,0:T(8,128)(2,1)S(1)}, u32[]{:S(2)}, u32[]{:S(2)}) collective-permute-start(bf16[8,7168]{1,0:T(8,128)(2,1)S(1)} %get-tuple-element.30), channel_id=1, source_target_pairs={{0,4},{1,5},{2,6},{3,7},{4,0},{5,1},{6,2},{7,3},{8,12},{9,13},{10,... | collective-permute-start | bytes 344072 | tf_op jit(solution)/shard_map/ppermute | solution.py:175
  28.9 6.5 %collective-permute-start.13 = (bf16[8,7168]{1,0:T(8,128)(2,1)S(1)}, bf16[8,7168]{1,0:T(8,128)(2,1)S(1)}, u32[]{:S(2)}, u32[]{:S(2)}) collective-permute-start(bf16[8,7168]{1,0:T(8,128)(2,1)S(1)} %get-tuple-element.31), channel_id=1, source_target_pairs={{0,6},{1,7},{2,4},{3,5},{4,2},{5,3},{6,0},{7,1},{8,14},{9,15},{10,... | collective-permute-start | bytes 344072 | tf_op jit(solution)/shard_map/ppermute | solution.py:175
  30.0 8.5 %collective-permute-start.15 = (bf16[8,7168]{1,0:T(8,128)(2,1)S(1)}, bf16[8,7168]{1,0:T(8,128)(2,1)S(1)}, u32[]{:S(2)}, u32[]{:S(2)}) collective-permute-start(bf16[8,7168]{1,0:T(8,128)(2,1)S(1)} %get-tuple-element.34), channel_id=1, source_target_pairs={{0,2},{1,3},{2,0},{3,1},{4,6},{5,7},{6,4},{7,5},{8,10},{9,11},{10,... | collective-permute-start | bytes 344072 | tf_op jit(solution)/shard_map/ppermute | solution.py:175
  35.5 7.4 %collective-permute-start.17 = (bf16[8,7168]{1,0:T(8,128)(2,1)S(1)}, bf16[8,7168]{1,0:T(8,128)(2,1)S(1)}, u32[]{:S(2)}, u32[]{:S(2)}) collective-permute-start(bf16[8,7168]{1,0:T(8,128)(2,1)S(1)} %shard_map.81.refs_2_), channel_id=1, source_target_pairs={{0,12},{1,13},{2,14},{3,15},{4,8},{5,9},{6,10},{7,11},{8,4},{9,5},... | collective-permute-start | bytes 344072 | tf_op jit(solution)/shard_map/ppermute | solution.py:175
  38.5 5.5 %collective-permute-start.16 = (bf16[8,7168]{1,0:T(8,128)(2,1)S(1)}, bf16[8,7168]{1,0:T(8,128)(2,1)S(1)}, u32[]{:S(2)}, u32[]{:S(2)}) collective-permute-start(bf16[8,7168]{1,0:T(8,128)(2,1)S(1)} %shard_map.83), channel_id=1, source_target_pairs={{0,4},{1,5},{2,6},{3,7},{4,0},{5,1},{6,2},{7,3},{8,12},{9,13},{10,... | collective-permute-start | bytes 344072 | tf_op jit(solution)/shard_map/ppermute | solution.py:175
  38.6 5.4 %collective-permute-start.14 = (bf16[8,7168]{1,0:T(8,128)(2,1)S(1)}, bf16[8,7168]{1,0:T(8,128)(2,1)S(1)}, u32[]{:S(2)}, u32[]{:S(2)}) collective-permute-start(bf16[8,7168]{1,0:T(8,128)(2,1)S(1)} %get-tuple-element.33.refs_3_), channel_id=1, source_target_pairs={{0,2},{1,3},{2,0},{3,1},{4,6},{5,7},{6,4},{7,5},{8,10},{9,11},{10,... | collective-permute-start | bytes 344072 | tf_op jit(solution)/shard_map/ppermute | solution.py:175

commit v6 on v5

--- a/solution.py
+++ b/solution.py
@@ -100,6 +100,19 @@
         refs[-1][:, at] = jnp.concatenate(parts, axis=0).astype(BF16)
 
 
+def slice_kernel(start, ref, out_ref):
+    out_ref[...] = ref[:, start : start + out_ref.shape[1]]
+
+
+def late_kernel(*refs):
+    *far, left, right, out_ref = refs
+    for half, first in ((left, 0), (right, left.shape[1])):
+        for at in chunks(half.shape[1]):
+            there = slice(first + at.start, first + at.stop)
+            parts = [ref[:, there].astype(F32) for ref in far] + [half[:, at].astype(F32)]
+            out_ref[:, there] = jnp.concatenate(parts, axis=0).astype(BF16)
+
+
 def mark_kernel(ref, out_ref):
     out_ref[...] = ref[:, :128].astype(F32)
 
@@ -214,13 +227,18 @@
     )
 
     first = [own, swap(own, SIDES[0]), side_two]
-    past = swap(first[2], SIDES[0])
+    middle = width // 256 * 128
+    left = call(functools.partial(slice_kernel, 0), shape(CAP, middle), [first[1]], moved=4 * CAP * middle)
+    right = call(
+        functools.partial(slice_kernel, middle), shape(CAP, width - middle), [first[2]], moved=4 * CAP * middle
+    )
+    past = [swap(left, SIDES[1]), swap(right, SIDES[0])]
     rows = CAP * (waves - 1)
     far = heads[0] if waves == 2 else stack(heads)
     sent = [swap(far, s) for s in SIDES + (CORNER,)]
     marks = [call(mark_kernel, shape(CAP, 128, F32), [x]) for x in heads]
     early = stack(first + [far], after=marks)
-    late = stack(sent + [past])
+    late = call(late_kernel, shape(3 * rows + CAP, width), sent + past, moved=16 * rows * width)
     blocks = [late, early, swap(late, 1), swap(early, 1)]
     late, early, late_away, early_away = call(
         ffn_kernel,

time: 45.4 us -> 44.6 us (0.982)
  waiting for transfers between devices: 19.1 us -> 15.2 us
  starting transfers between devices: 21.1 us -> 24.2 us
    ppermute x18 -> x19, waiting for transfers between devices: 19.1 us -> 15.2 us  [swap(): return lax.ppermute(x, 'tp', [(i, i ^ mask) for i in range(devices)])]
    ppermute x18 -> x19, starting transfers between devices: 21.1 us -> 24.2 us  [swap(): return lax.ppermute(x, 'tp', [(i, i ^ mask) for i in range(devices)])]
    pallas_call x13 -> x15, Pallas kernels: 4.94 us -> 4.97 us  [call(): pl.pallas_call(run, out_shape=outs, in_specs=[space(pltpu.HBM)] * left +...]
  transfers between devices with their start and end apart: 18 -> 19, of which waited for: 12 -> 12; matrix products, arithmetic and copies ran while one was open for 0% -> 0% of each run, Pallas kernels for 1% -> 1%
where the time goes in v6:
time: 44.6 us; the launch traced here: 44.5 us
  starting transfers between devices  24.2 us (54%)
  waiting for transfers between devices  15.2 us (34%)
  Pallas kernels  4.97 us (11%)
    ppermute x19, starting transfers between devices, swap(): return lax.ppermute(x, 'tp', [(i, i ^ mask) for i in range(devices)])  24.2 us
    ppermute x19, waiting for transfers between devices, swap(): return lax.ppermute(x, 'tp', [(i, i ^ mask) for i in range(devices)])  15.2 us
    pallas_call x15, Pallas kernels, call(): pl.pallas_call(run, out_shape=outs, in_specs=[space(pltpu.HBM)] * left +...  4.97 us
  transfers between devices with their start and end apart: 19, of which 12 were waited for; matrix products, arithmetic and copies ran while one was open for 0% of the time, Pallas kernels for 1%

profile of v6, /device:TPU:0, one launch (start us, length us, event | category | flops | bytes accessed | tf_op | source)
XLA Modules:
  0.0 44.5 jit_solution(7574495257821741484)
XLA Ops:
  0.0 1.6 %shard_map.73 = (bf16[8,7168]{1,0:T(8,128)(2,1)S(1)}, bf16[8,7168]{1,0:T(8,128)(2,1)S(1)}, f32[16,64]{1,0:T(8,128)S(1)}) custom-call(bf16[64,7168]{1,0:T(8,128)(2,1)} %refs_0_.2, f32[1,7168]{1,0:T(1,128)} %bitcast.3, s32[8,64]{1,0:T(8,128)} %bitcast.4, f32[8,64]{1,0:T(8,128)} %bitcast.5), custom_call_target="tpu_custom_call" | custom-call | flops 14680064 | bytes 917504 | tf_op jit(solution)/shard_map/pallas_call | solution.py:33
  1.6 5.1 %collective-permute-start = (bf16[8,7168]{1,0:T(8,128)(2,1)S(1)}, bf16[8,7168]{1,0:T(8,128)(2,1)S(1)}, u32[]{:S(2)}, u32[]{:S(2)}) collective-permute-start(bf16[8,7168]{1,0:T(8,128)(2,1)S(1)} %get-tuple-element.23), channel_id=1, source_target_pairs={{0,12},{1,13},{2,14},{3,15},{4,8},{5,9},{6,10},{7,11},{8,4},{9,5},... | collective-permute-start | bytes 344072 | tf_op jit(solution)/shard_map/ppermute | solution.py:188
  6.8 1.6 %collective-permute-start.4 = (bf16[8,7168]{1,0:T(8,128)(2,1)S(1)}, bf16[8,7168]{1,0:T(8,128)(2,1)S(1)}, u32[]{:S(2)}, u32[]{:S(2)}) collective-permute-start(bf16[8,7168]{1,0:T(8,128)(2,1)S(1)} %get-tuple-element.24.refs_0_), channel_id=1, source_target_pairs={{0,2},{1,3},{2,0},{3,1},{4,6},{5,7},{6,4},{7,5},{8,10},{9,11},{10,... | collective-permute-start | bytes 344072 | tf_op jit(solution)/shard_map/ppermute | solution.py:188
  8.4 2.3 %collective-permute-done.refs_0_.refs_3_ = bf16[8,7168]{1,0:T(8,128)(2,1)S(1)} collective-permute-done((bf16[8,7168]{1,0:T(8,128)(2,1)S(1)}, bf16[8,7168]{1,0:T(8,128)(2,1)S(1)}, u32[]{:S(2)}, u32[]{:S(2)}) %collective-permute-start) | collective-permute-done | bytes 114720 | tf_op jit(solution)/shard_map/ppermute | solution.py:188
  10.7 2.3 %collective-permute-start.3 = (bf16[8,7168]{1,0:T(8,128)(2,1)S(1)}, bf16[8,7168]{1,0:T(8,128)(2,1)S(1)}, u32[]{:S(2)}, u32[]{:S(2)}) collective-permute-start(bf16[8,7168]{1,0:T(8,128)(2,1)S(1)} %collective-permute-done.refs_0_.refs_3_), channel_id=1, source_target_pairs={{0,6},{1,7},{2,4},{3,5},{4,2},{5,3},{6,0},{7,1},{8,14},{9,15},{10,... | collective-permute-start | bytes 344072 | tf_op jit(solution)/shard_map/ppermute | solution.py:188
  13.0 0.9 %collective-permute-start.2 = (bf16[8,7168]{1,0:T(8,128)(2,1)S(1)}, bf16[8,7168]{1,0:T(8,128)(2,1)S(1)}, u32[]{:S(2)}, u32[]{:S(2)}) collective-permute-start(bf16[8,7168]{1,0:T(8,128)(2,1)S(1)} %collective-permute-done.refs_0_.refs_3_), channel_id=1, source_target_pairs={{0,4},{1,5},{2,6},{3,7},{4,0},{5,1},{6,2},{7,3},{8,12},{9,13},{10,... | collective-permute-start | bytes 344072 | tf_op jit(solution)/shard_map/ppermute | solution.py:188
  14.0 0.3 collective-permute-start.1
  14.2 1.4 %collective-permute-start.5 = (bf16[8,3584]{1,0:T(8,128)(2,1)S(1)}, bf16[8,3584]{1,0:T(8,128)(2,1)S(1)}, u32[]{:S(2)}, u32[]{:S(2)}) collective-permute-start(bf16[8,3584]{1,0:T(8,128)(2,1)S(1)} %shard_map.75), channel_id=1, source_target_pairs={{0,4},{1,5},{2,6},{3,7},{4,0},{5,1},{6,2},{7,3},{8,12},{9,13},{10,... | collective-permute-start | bytes 172040 | tf_op jit(solution)/shard_map/ppermute | solution.py:188
  15.6 1.6 %collective-permute-start.7 = (bf16[8,3584]{1,0:T(8,128)(2,1)S(1)}, bf16[8,3584]{1,0:T(8,128)(2,1)S(1)}, u32[]{:S(2)}, u32[]{:S(2)}) collective-permute-start(bf16[8,3584]{1,0:T(8,128)(2,1)S(1)} %shard_map.76), channel_id=1, source_target_pairs={{0,2},{1,3},{2,0},{3,1},{4,6},{5,7},{6,4},{7,5},{8,10},{9,11},{10,... | collective-permute-start | bytes 172040 | tf_op jit(solution)/shard_map/ppermute | solution.py:188
  17.3 2.1 %collective-permute-done.5.refs_3_ = bf16[8,3584]{1,0:T(8,128)(2,1)S(1)} collective-permute-done((bf16[8,3584]{1,0:T(8,128)(2,1)S(1)}, bf16[8,3584]{1,0:T(8,128)(2,1)S(1)}, u32[]{:S(2)}, u32[]{:S(2)}) %collective-permute-start.5) | collective-permute-done | bytes 57376 | tf_op jit(solution)/shard_map/ppermute | solution.py:188
  19.4 0.5 %collective-permute-done.7.refs_4_ = bf16[8,3584]{1,0:T(8,128)(2,1)S(1)} collective-permute-done((bf16[8,3584]{1,0:T(8,128)(2,1)S(1)}, bf16[8,3584]{1,0:T(8,128)(2,1)S(1)}, u32[]{:S(2)}, u32[]{:S(2)}) %collective-permute-start.7) | collective-permute-done | bytes 57376 | tf_op jit(solution)/shard_map/ppermute | solution.py:188
  20.0 1.2 %collective-permute-done.9.refs_6_ = bf16[32,7168]{1,0:T(8,128)(2,1)S(1)} collective-permute-done((bf16[32,7168]{1,0:T(8,128)(2,1)S(1)}, bf16[32,7168]{1,0:T(8,128)(2,1)S(1)}, u32[]{:S(2)}, u32[]{:S(2)}) %collective-permute-start.9) | collective-permute-done | bytes 458784 | tf_op jit(solution)/shard_map/ppermute | solution.py:188
  21.2 0.7 %collective-permute-done.8.refs_5_ = bf16[32,7168]{1,0:T(8,128)(2,1)S(1)} collective-permute-done((bf16[32,7168]{1,0:T(8,128)(2,1)S(1)}, bf16[32,7168]{1,0:T(8,128)(2,1)S(1)}, u32[]{:S(2)}, u32[]{:S(2)}) %collective-permute-start.8) | collective-permute-done | bytes 458784 | tf_op jit(solution)/shard_map/ppermute | solution.py:188
  21.8 1.7 %shard_map.80 = (bf16[32,7168]{1,0:T(8,128)(2,1)S(1)}, bf16[32,7168]{1,0:T(8,128)(2,1)S(1)}, bf16[32,7168]{1,0:T(8,128)(2,1)S(1)}, bf16[32,7168]{1,0:T(8,128)(2,1)S(1)}) custom-call(bf16[7168,256]{1,0:T(8,128)(2,1)S(1)} %copy-done, bf16[7168,256]{1,0:T(8,128)(2,1)S(1)} %copy-done.1, bf16[256,7168]{1,0:T(8,128)(2,1)S(1)} %copy-done.2, ...), custom_call_target="tpu_custom_call" | custom-call | flops 1409286144 | bytes 11010048 | tf_op jit(solution)/shard_map/pallas_call | solution.py:33
  23.6 0.2 collective-permute-start.11
  23.8 0.4 collective-permute-start.10
  24.2 1.3 %collective-permute-done.11.refs_1_ = bf16[32,7168]{1,0:T(8,128)(2,1)S(1)} collective-permute-done((bf16[32,7168]{1,0:T(8,128)(2,1)S(1)}, bf16[32,7168]{1,0:T(8,128)(2,1)S(1)}, u32[]{:S(2)}, u32[]{:S(2)}) %collective-permute-start.11) | collective-permute-done | bytes 458784 | tf_op jit(solution)/shard_map/ppermute | solution.py:188
  25.5 0.1 shard_map.82
  25.6 1.6 %collective-permute-start.12 = (bf16[8,7168]{1,0:T(8,128)(2,1)S(1)}, bf16[8,7168]{1,0:T(8,128)(2,1)S(1)}, u32[]{:S(2)}, u32[]{:S(2)}) collective-permute-start(bf16[8,7168]{1,0:T(8,128)(2,1)S(1)} %get-tuple-element.29), channel_id=1, source_target_pairs={{0,2},{1,3},{2,0},{3,1},{4,6},{5,7},{6,4},{7,5},{8,10},{9,11},{10,... | collective-permute-start | bytes 344072 | tf_op jit(solution)/shard_map/ppermute | solution.py:188
  27.2 0.9 %collective-permute-start.13 = (bf16[8,7168]{1,0:T(8,128)(2,1)S(1)}, bf16[8,7168]{1,0:T(8,128)(2,1)S(1)}, u32[]{:S(2)}, u32[]{:S(2)}) collective-permute-start(bf16[8,7168]{1,0:T(8,128)(2,1)S(1)} %get-tuple-element.30), channel_id=1, source_target_pairs={{0,4},{1,5},{2,6},{3,7},{4,0},{5,1},{6,2},{7,3},{8,12},{9,13},{10,... | collective-permute-start | bytes 344072 | tf_op jit(solution)/shard_map/ppermute | solution.py:188
  28.1 1.1 %collective-permute-start.14 = (bf16[8,7168]{1,0:T(8,128)(2,1)S(1)}, bf16[8,7168]{1,0:T(8,128)(2,1)S(1)}, u32[]{:S(2)}, u32[]{:S(2)}) collective-permute-start(bf16[8,7168]{1,0:T(8,128)(2,1)S(1)} %get-tuple-element.31), channel_id=1, source_target_pairs={{0,6},{1,7},{2,4},{3,5},{4,2},{5,3},{6,0},{7,1},{8,14},{9,15},{10,... | collective-permute-start | bytes 344072 | tf_op jit(solution)/shard_map/ppermute | solution.py:188
  29.1 1.5 %collective-permute-start.16 = (bf16[8,7168]{1,0:T(8,128)(2,1)S(1)}, bf16[8,7168]{1,0:T(8,128)(2,1)S(1)}, u32[]{:S(2)}, u32[]{:S(2)}) collective-permute-start(bf16[8,7168]{1,0:T(8,128)(2,1)S(1)} %get-tuple-element.34), channel_id=1, source_target_pairs={{0,2},{1,3},{2,0},{3,1},{4,6},{5,7},{6,4},{7,5},{8,10},{9,11},{10,... | collective-permute-start | bytes 344072 | tf_op jit(solution)/shard_map/ppermute | solution.py:188
  30.7 0.2 collective-permute-done.12.refs_1_
  30.8 2.4 %collective-permute-done.13.refs_2_ = bf16[8,7168]{1,0:T(8,128)(2,1)S(1)} collective-permute-done((bf16[8,7168]{1,0:T(8,128)(2,1)S(1)}, bf16[8,7168]{1,0:T(8,128)(2,1)S(1)}, u32[]{:S(2)}, u32[]{:S(2)}) %collective-permute-start.13) | collective-permute-done | bytes 114720 | tf_op jit(solution)/shard_map/ppermute | solution.py:188
  33.2 1.3 %collective-permute-done.14.refs_3_ = bf16[8,7168]{1,0:T(8,128)(2,1)S(1)} collective-permute-done((bf16[8,7168]{1,0:T(8,128)(2,1)S(1)}, bf16[8,7168]{1,0:T(8,128)(2,1)S(1)}, u32[]{:S(2)}, u32[]{:S(2)}) %collective-permute-start.14) | collective-permute-done | bytes 114720 | tf_op jit(solution)/shard_map/ppermute | solution.py:188
  34.6 3.2 %collective-permute-start.18 = (bf16[8,7168]{1,0:T(8,128)(2,1)S(1)}, bf16[8,7168]{1,0:T(8,128)(2,1)S(1)}, u32[]{:S(2)}, u32[]{:S(2)}) collective-permute-start(bf16[8,7168]{1,0:T(8,128)(2,1)S(1)} %shard_map.83.refs_2_), channel_id=1, source_target_pairs={{0,12},{1,13},{2,14},{3,15},{4,8},{5,9},{6,10},{7,11},{8,4},{9,5},... | collective-permute-start | bytes 344072 | tf_op jit(solution)/shard_map/ppermute | solution.py:188
  37.9 0.6 %collective-permute-start.17 = (bf16[8,7168]{1,0:T(8,128)(2,1)S(1)}, bf16[8,7168]{1,0:T(8,128)(2,1)S(1)}, u32[]{:S(2)}, u32[]{:S(2)}) collective-permute-start(bf16[8,7168]{1,0:T(8,128)(2,1)S(1)} %shard_map.85), channel_id=1, source_target_pairs={{0,4},{1,5},{2,6},{3,7},{4,0},{5,1},{6,2},{7,3},{8,12},{9,13},{10,... | collective-permute-start | bytes 344072 | tf_op jit(solution)/shard_map/ppermute | solution.py:188
  38.5 1.5 %collective-permute-start.15 = (bf16[8,7168]{1,0:T(8,128)(2,1)S(1)}, bf16[8,7168]{1,0:T(8,128)(2,1)S(1)}, u32[]{:S(2)}, u32[]{:S(2)}) collective-permute-start(bf16[8,7168]{1,0:T(8,128)(2,1)S(1)} %get-tuple-element.33.refs_3_), channel_id=1, source_target_pairs={{0,2},{1,3},{2,0},{3,1},{4,6},{5,7},{6,4},{7,5},{8,10},{9,11},{10,... | collective-permute-start | bytes 344072 | tf_op jit(solution)/shard_map/ppermute | solution.py:188
  40.0 2.2 %collective-permute-done.18.refs_0_.refs_4_ = bf16[8,7168]{1,0:T(8,128)(2,1)S(1)} collective-permute-done((bf16[8,7168]{1,0:T(8,128)(2,1)S(1)}, bf16[8,7168]{1,0:T(8,128)(2,1)S(1)}, u32[]{:S(2)}, u32[]{:S(2)}) %collective-permute-start.18) | collective-permute-done | bytes 114720 | tf_op jit(solution)/shard_map/ppermute | solution.py:188
  42.2 1.0 %collective-permute-done.17.refs_3_ = bf16[8,7168]{1,0:T(8,128)(2,1)S(1)} collective-permute-done((bf16[8,7168]{1,0:T(8,128)(2,1)S(1)}, bf16[8,7168]{1,0:T(8,128)(2,1)S(1)}, u32[]{:S(2)}, u32[]{:S(2)}) %collective-permute-start.17) | collective-permute-done | bytes 114720 | tf_op jit(solution)/shard_map/ppermute | solution.py:188
  43.2 0.1 collective-permute-done.15.refs_2_
  43.3 1.2 %shard_map.87 = bf16[64,7168]{1,0:T(8,128)(2,1)} custom-call(bf16[64,48]{1,0:T(8,128)(2,1)S(1)} %get-tuple-element.22.refs_0_, f32[8,7168]{1,0:T(8,128)S(1)} %get-tuple-element.32.refs_1_, bf16[8,7168]{1,0:T(8,128)(2,1)S(1)} %collective-permute-done.15.refs_2_, bf16[8,7168]{1,0:T(8,128)(2,1)S(1)} %collective-permute-done.17.refs_3_, ...), custom_call_target="tpu_custom_call" | custom-call | flops 44040192 | bytes 1835008 | tf_op jit(solution)/shard_map/pallas_call | solution.py:33
  (27 shorter events, 0.4 us)
Async XLA Ops:
  1.6 9.1 %collective-permute-start = (bf16[8,7168]{1,0:T(8,128)(2,1)S(1)}, bf16[8,7168]{1,0:T(8,128)(2,1)S(1)}, u32[]{:S(2)}, u32[]{:S(2)}) collective-permute-start(bf16[8,7168]{1,0:T(8,128)(2,1)S(1)} %get-tuple-element.23), channel_id=1, source_target_pairs={{0,12},{1,13},{2,14},{3,15},{4,8},{5,9},{6,10},{7,11},{8,4},{9,5},... | collective-permute-start | bytes 344072 | tf_op jit(solution)/shard_map/ppermute | solution.py:188
  6.7 15.1 %copy-start = (bf16[7168,256]{1,0:T(8,128)(2,1)S(1)}, bf16[7168,256]{1,0:T(8,128)(2,1)}, u32[]{:S(2)}) copy-start(bf16[7168,256]{1,0:T(8,128)(2,1)} %refs_0_.3) | copy-start | bytes 11010052
  6.8 15.1 %copy-start.1 = (bf16[7168,256]{1,0:T(8,128)(2,1)S(1)}, bf16[7168,256]{1,0:T(8,128)(2,1)}, u32[]{:S(2)}) copy-start(bf16[7168,256]{1,0:T(8,128)(2,1)} %refs_1_.1) | copy-start | bytes 11010052
  6.8 15.1 %copy-start.2 = (bf16[256,7168]{1,0:T(8,128)(2,1)S(1)}, bf16[256,7168]{1,0:T(8,128)(2,1)}, u32[]{:S(2)}) copy-start(bf16[256,7168]{1,0:T(8,128)(2,1)} %refs_2_.1) | copy-start | bytes 11010052
  6.8 7.4 %collective-permute-start.4 = (bf16[8,7168]{1,0:T(8,128)(2,1)S(1)}, bf16[8,7168]{1,0:T(8,128)(2,1)S(1)}, u32[]{:S(2)}, u32[]{:S(2)}) collective-permute-start(bf16[8,7168]{1,0:T(8,128)(2,1)S(1)} %get-tuple-element.24.refs_0_), channel_id=1, source_target_pairs={{0,2},{1,3},{2,0},{3,1},{4,6},{5,7},{6,4},{7,5},{8,10},{9,11},{10,... | collective-permute-start | bytes 344072 | tf_op jit(solution)/shard_map/ppermute | solution.py:188
  8.4 7.2 %collective-permute-start.6 = (bf16[8,7168]{1,0:T(8,128)(2,1)S(1)}, bf16[8,7168]{1,0:T(8,128)(2,1)S(1)}, u32[]{:S(2)}, u32[]{:S(2)}) collective-permute-start(bf16[8,7168]{1,0:T(8,128)(2,1)S(1)} %get-tuple-element.20.refs_0_), channel_id=1, source_target_pairs={{0,4},{1,5},{2,6},{3,7},{4,0},{5,1},{6,2},{7,3},{8,12},{9,13},{10,... | collective-permute-start | bytes 344072 | tf_op jit(solution)/shard_map/ppermute | solution.py:188
  10.7 9.2 %collective-permute-start.3 = (bf16[8,7168]{1,0:T(8,128)(2,1)S(1)}, bf16[8,7168]{1,0:T(8,128)(2,1)S(1)}, u32[]{:S(2)}, u32[]{:S(2)}) collective-permute-start(bf16[8,7168]{1,0:T(8,128)(2,1)S(1)} %collective-permute-done.refs_0_.refs_3_), channel_id=1, source_target_pairs={{0,6},{1,7},{2,4},{3,5},{4,2},{5,3},{6,0},{7,1},{8,14},{9,15},{10,... | collective-permute-start | bytes 344072 | tf_op jit(solution)/shard_map/ppermute | solution.py:188
  13.0 6.9 %collective-permute-start.2 = (bf16[8,7168]{1,0:T(8,128)(2,1)S(1)}, bf16[8,7168]{1,0:T(8,128)(2,1)S(1)}, u32[]{:S(2)}, u32[]{:S(2)}) collective-permute-start(bf16[8,7168]{1,0:T(8,128)(2,1)S(1)} %collective-permute-done.refs_0_.refs_3_), channel_id=1, source_target_pairs={{0,4},{1,5},{2,6},{3,7},{4,0},{5,1},{6,2},{7,3},{8,12},{9,13},{10,... | collective-permute-start | bytes 344072 | tf_op jit(solution)/shard_map/ppermute | solution.py:188
  14.0 5.9 %collective-permute-start.1 = (bf16[8,7168]{1,0:T(8,128)(2,1)S(1)}, bf16[8,7168]{1,0:T(8,128)(2,1)S(1)}, u32[]{:S(2)}, u32[]{:S(2)}) collective-permute-start(bf16[8,7168]{1,0:T(8,128)(2,1)S(1)} %collective-permute-done.refs_0_.refs_3_), channel_id=1, source_target_pairs={{0,2},{1,3},{2,0},{3,1},{4,6},{5,7},{6,4},{7,5},{8,10},{9,11},{10,... | collective-permute-start | bytes 344072 | tf_op jit(solution)/shard_map/ppermute | solution.py:188
  14.2 5.1 %collective-permute-start.5 = (bf16[8,3584]{1,0:T(8,128)(2,1)S(1)}, bf16[8,3584]{1,0:T(8,128)(2,1)S(1)}, u32[]{:S(2)}, u32[]{:S(2)}) collective-permute-start(bf16[8,3584]{1,0:T(8,128)(2,1)S(1)} %shard_map.75), channel_id=1, source_target_pairs={{0,4},{1,5},{2,6},{3,7},{4,0},{5,1},{6,2},{7,3},{8,12},{9,13},{10,... | collective-permute-start | bytes 172040 | tf_op jit(solution)/shard_map/ppermute | solution.py:188
  15.6 4.2 %collective-permute-start.7 = (bf16[8,3584]{1,0:T(8,128)(2,1)S(1)}, bf16[8,3584]{1,0:T(8,128)(2,1)S(1)}, u32[]{:S(2)}, u32[]{:S(2)}) collective-permute-start(bf16[8,3584]{1,0:T(8,128)(2,1)S(1)} %shard_map.76), channel_id=1, source_target_pairs={{0,2},{1,3},{2,0},{3,1},{4,6},{5,7},{6,4},{7,5},{8,10},{9,11},{10,... | collective-permute-start | bytes 172040 | tf_op jit(solution)/shard_map/ppermute | solution.py:188
  19.4 1.8 %collective-permute-start.9 = (bf16[32,7168]{1,0:T(8,128)(2,1)S(1)}, bf16[32,7168]{1,0:T(8,128)(2,1)S(1)}, u32[]{:S(2)}, u32[]{:S(2)}) collective-permute-start(bf16[32,7168]{1,0:T(8,128)(2,1)S(1)} %shard_map.79.refs_4_), channel_id=1, source_target_pairs={{0,1},{1,0},{2,3},{3,2},{4,5},{5,4},{6,7},{7,6},{8,9},{9,8},{10,11... | collective-permute-start | bytes 1376264 | tf_op jit(solution)/shard_map/ppermute | solution.py:188
  19.9 1.9 %collective-permute-start.8 = (bf16[32,7168]{1,0:T(8,128)(2,1)S(1)}, bf16[32,7168]{1,0:T(8,128)(2,1)S(1)}, u32[]{:S(2)}, u32[]{:S(2)}) collective-permute-start(bf16[32,7168]{1,0:T(8,128)(2,1)S(1)} %shard_map.77.refs_3_), channel_id=1, source_target_pairs={{0,1},{1,0},{2,3},{3,2},{4,5},{5,4},{6,7},{7,6},{8,9},{9,8},{10,11... | collective-permute-start | bytes 1376264 | tf_op jit(solution)/shard_map/ppermute | solution.py:188
  23.6 1.9 %collective-permute-start.11 = (bf16[32,7168]{1,0:T(8,128)(2,1)S(1)}, bf16[32,7168]{1,0:T(8,128)(2,1)S(1)}, u32[]{:S(2)}, u32[]{:S(2)}) collective-permute-start(bf16[32,7168]{1,0:T(8,128)(2,1)S(1)} %get-tuple-element.28), channel_id=1, source_target_pairs={{0,1},{1,0},{2,3},{3,2},{4,5},{5,4},{6,7},{7,6},{8,9},{9,8},{10,11... | collective-permute-start | bytes 1376264 | tf_op jit(solution)/shard_map/ppermute | solution.py:188
  23.8 6.9 %collective-permute-start.10 = (bf16[32,7168]{1,0:T(8,128)(2,1)S(1)}, bf16[32,7168]{1,0:T(8,128)(2,1)S(1)}, u32[]{:S(2)}, u32[]{:S(2)}) collective-permute-start(bf16[32,7168]{1,0:T(8,128)(2,1)S(1)} %get-tuple-element.26), channel_id=1, source_target_pairs={{0,1},{1,0},{2,3},{3,2},{4,5},{5,4},{6,7},{7,6},{8,9},{9,8},{10,11... | collective-permute-start | bytes 1376264 | tf_op jit(solution)/shard_map/ppermute | solution.py:188
  25.6 5.3 %collective-permute-start.12 = (bf16[8,7168]{1,0:T(8,128)(2,1)S(1)}, bf16[8,7168]{1,0:T(8,128)(2,1)S(1)}, u32[]{:S(2)}, u32[]{:S(2)}) collective-permute-start(bf16[8,7168]{1,0:T(8,128)(2,1)S(1)} %get-tuple-element.29), channel_id=1, source_target_pairs={{0,2},{1,3},{2,0},{3,1},{4,6},{5,7},{6,4},{7,5},{8,10},{9,11},{10,... | collective-permute-start | bytes 344072 | tf_op jit(solution)/shard_map/ppermute | solution.py:188
  27.2 6.0 %collective-permute-start.13 = (bf16[8,7168]{1,0:T(8,128)(2,1)S(1)}, bf16[8,7168]{1,0:T(8,128)(2,1)S(1)}, u32[]{:S(2)}, u32[]{:S(2)}) collective-permute-start(bf16[8,7168]{1,0:T(8,128)(2,1)S(1)} %get-tuple-element.30), channel_id=1, source_target_pairs={{0,4},{1,5},{2,6},{3,7},{4,0},{5,1},{6,2},{7,3},{8,12},{9,13},{10,... | collective-permute-start | bytes 344072 | tf_op jit(solution)/shard_map/ppermute | solution.py:188
  28.1 6.4 %collective-permute-start.14 = (bf16[8,7168]{1,0:T(8,128)(2,1)S(1)}, bf16[8,7168]{1,0:T(8,128)(2,1)S(1)}, u32[]{:S(2)}, u32[]{:S(2)}) collective-permute-start(bf16[8,7168]{1,0:T(8,128)(2,1)S(1)} %get-tuple-element.31), channel_id=1, source_target_pairs={{0,6},{1,7},{2,4},{3,5},{4,2},{5,3},{6,0},{7,1},{8,14},{9,15},{10,... | collective-permute-start | bytes 344072 | tf_op jit(solution)/shard_map/ppermute | solution.py:188
  29.1 8.7 %collective-permute-start.16 = (bf16[8,7168]{1,0:T(8,128)(2,1)S(1)}, bf16[8,7168]{1,0:T(8,128)(2,1)S(1)}, u32[]{:S(2)}, u32[]{:S(2)}) collective-permute-start(bf16[8,7168]{1,0:T(8,128)(2,1)S(1)} %get-tuple-element.34), channel_id=1, source_target_pairs={{0,2},{1,3},{2,0},{3,1},{4,6},{5,7},{6,4},{7,5},{8,10},{9,11},{10,... | collective-permute-start | bytes 344072 | tf_op jit(solution)/shard_map/ppermute | solution.py:188
  34.6 7.6 %collective-permute-start.18 = (bf16[8,7168]{1,0:T(8,128)(2,1)S(1)}, bf16[8,7168]{1,0:T(8,128)(2,1)S(1)}, u32[]{:S(2)}, u32[]{:S(2)}) collective-permute-start(bf16[8,7168]{1,0:T(8,128)(2,1)S(1)} %shard_map.83.refs_2_), channel_id=1, source_target_pairs={{0,12},{1,13},{2,14},{3,15},{4,8},{5,9},{6,10},{7,11},{8,4},{9,5},... | collective-permute-start | bytes 344072 | tf_op jit(solution)/shard_map/ppermute | solution.py:188
  37.9 5.3 %collective-permute-start.17 = (bf16[8,7168]{1,0:T(8,128)(2,1)S(1)}, bf16[8,7168]{1,0:T(8,128)(2,1)S(1)}, u32[]{:S(2)}, u32[]{:S(2)}) collective-permute-start(bf16[8,7168]{1,0:T(8,128)(2,1)S(1)} %shard_map.85), channel_id=1, source_target_pairs={{0,4},{1,5},{2,6},{3,7},{4,0},{5,1},{6,2},{7,3},{8,12},{9,13},{10,... | collective-permute-start | bytes 344072 | tf_op jit(solution)/shard_map/ppermute | solution.py:188
  38.5 4.8 %collective-permute-start.15 = (bf16[8,7168]{1,0:T(8,128)(2,1)S(1)}, bf16[8,7168]{1,0:T(8,128)(2,1)S(1)}, u32[]{:S(2)}, u32[]{:S(2)}) collective-permute-start(bf16[8,7168]{1,0:T(8,128)(2,1)S(1)} %get-tuple-element.33.refs_3_), channel_id=1, source_target_pairs={{0,2},{1,3},{2,0},{3,1},{4,6},{5,7},{6,4},{7,5},{8,10},{9,11},{10,... | collective-permute-start | bytes 344072 | tf_op jit(solution)/shard_map/ppermute | solution.py:188

commit v7 on v5

--- a/solution.py
+++ b/solution.py
@@ -12,10 +12,13 @@
 SPLIT = 8
 CAP = 8
 EPSILON = 1e-06
-SIDES = (2, 4)
-CORNER = 6
+SIDES = ((2, 2), (4, 4))
+MIXED = ((2, 4), (4, 2))
+CORNER = (6, 6)
+OTHER = (1, 1)
 OWN_FLOPS = 7_000_000_000
 CHUNK = 1024
+OUT_CHUNK = 1792
 F32 = jnp.float32
 BF16 = jnp.bfloat16
 
@@ -41,19 +44,13 @@
     )(*far_args, *args, *after)
 
 
-def chunks(width):
-    return [slice(at, min(at + CHUNK, width)) for at in range(0, width, CHUNK)]
-
-
-def normed(picked, states_ref, gain_ref):
-    rows = jnp.dot(picked, states_ref[...], preferred_element_type=F32)
-    squares = jnp.mean(rows * rows, axis=1, keepdims=True)
-    return rows * lax.rsqrt(squares + EPSILON) * gain_ref[...]
+def chunks(width, size=CHUNK):
+    return [slice(at, min(at + size, width)) for at in range(0, width, size)]
 
 
 def pick_kernel(waves, states_hbm, gain_hbm, ids_hbm, gates_hbm, *refs):
     row_refs, weighted_ref = refs[:waves], refs[waves]
-    states_ref, gain_ref, ids_ref, gates_ref, sems = refs[waves + 1 :]
+    states_ref, rows_ref, gain_ref, ids_ref, gates_ref, sems = refs[waves + 1 :]
     copies = [
         pltpu.make_async_copy(source, target, sems.at[n])
         for n, (source, target) in enumerate(
@@ -82,9 +79,18 @@
         matched = ids_ref[...] == lax.bitwise_xor(own, j) * (EXPERTS // NODES)
         score = jnp.sum(jnp.where(matched, gates_ref[...], 0.0), axis=0, keepdims=True)
         weighted_ref[CAP * j : CAP * (j + 1), :] = picked * score
-    rows = normed(jnp.concatenate(picks, axis=0).astype(BF16), states_ref, gain_ref)
-    for j, ref in enumerate(row_refs):
-        ref[...] = rows[CAP * j : CAP * (j + 1)].astype(BF16)
+    picked = jnp.concatenate(picks, axis=0).astype(BF16)
+    width = states_ref.shape[1]
+    squares = 0.0
+    for at in chunks(width):
+        rows = jnp.dot(picked, states_ref[:, at], preferred_element_type=F32)
+        rows_ref[:, at] = rows
+        squares += jnp.sum(rows * rows, axis=1, keepdims=True)
+    scale = lax.rsqrt(squares / width + EPSILON)
+    for at in chunks(width):
+        rows = rows_ref[:, at] * scale * gain_ref[:, at]
+        for j, ref in enumerate(row_refs):
+            ref[:, at] = rows[CAP * j : CAP * (j + 1)].astype(BF16)
 
 
 def ready_kernel(ref, weighted_ref, out_ref, weights_ref):
@@ -100,6 +106,18 @@
         refs[-1][:, at] = jnp.concatenate(parts, axis=0).astype(BF16)
 
 
+def choose_kernel(even_ref, odd_ref, out_ref):
+    even = lax.axis_index("tp") % 2 == 0
+
+    @pl.when(even)
+    def _():
+        out_ref[...] = even_ref[...]
+
+    @pl.when(jnp.logical_not(even))
+    def _():
+        out_ref[...] = odd_ref[...]
+
+
 def mark_kernel(ref, out_ref):
     out_ref[...] = ref[:, :128].astype(F32)
 
@@ -109,7 +127,7 @@
     width = blocks[0].shape[1]
     gated = up = 0.0
     for at in chunks(width):
-        both = jnp.concatenate([block[:, at].astype(F32) for block in blocks], axis=0).astype(BF16)
+        both = jnp.concatenate([block[:, at] for block in blocks], axis=0)
         gated += jnp.dot(both, gate_ref[at, :], preferred_element_type=F32)
         up += jnp.dot(both, up_ref[at, :], preferred_element_type=F32)
     hidden = (gated / (1.0 + jnp.exp(-gated)) * up).astype(BF16)
@@ -152,7 +170,7 @@
     near, others, (out_ref, held_ref, sems) = refs[:3], refs[3:-3], refs[-3:]
     weights = weights_ref[...]
     copies = []
-    for n, at in enumerate(chunks(out_ref.shape[1])):
+    for n, at in enumerate(chunks(out_ref.shape[1], OUT_CHUNK)):
         own = sum(piece[:, at].astype(F32) for piece in near)
         rows = jnp.concatenate([own] + [piece[:, at].astype(F32) for piece in others], axis=0)
         high = rows.astype(BF16).astype(F32)
@@ -172,10 +190,10 @@
     others = range(1, waves)
 
     def swap(x, mask):
-        return lax.ppermute(x, "tp", [(i, i ^ mask) for i in range(devices)])
+        return lax.ppermute(x, "tp", [(i, i ^ mask[i % 2]) for i in range(devices)])
 
     def cross(x, j):
-        return swap(x, SPLIT * j + 4)
+        return swap(x, (SPLIT * j + 4,) * 2)
 
     def shape(rows, columns, dtype=BF16):
         return jax.ShapeDtypeStruct((rows, columns), dtype)
@@ -195,6 +213,7 @@
         far_args=[states, gain, ids, gates],
         scratch=[
             pltpu.VMEM((tokens, width), BF16),
+            pltpu.VMEM((CAP * waves, width), F32),
             pltpu.VMEM((1, width), F32),
             pltpu.VMEM(ids.shape, ids.dtype),
             pltpu.VMEM(gates.shape, F32),
@@ -214,14 +233,15 @@
     )
 
     first = [own, swap(own, SIDES[0]), side_two]
-    past = swap(first[2], SIDES[0])
+    past = call(choose_kernel, block, [first[2], first[1]], moved=6 * CAP * width)
+    past = swap(past, MIXED[0])
     rows = CAP * (waves - 1)
     far = heads[0] if waves == 2 else stack(heads)
-    sent = [swap(far, s) for s in SIDES + (CORNER,)]
+    sent = [swap(far, s) for s in MIXED + (CORNER,)]
     marks = [call(mark_kernel, shape(CAP, 128, F32), [x]) for x in heads]
     early = stack(first + [far], after=marks)
     late = stack(sent + [past])
-    blocks = [late, early, swap(late, 1), swap(early, 1)]
+    blocks = [late, early, swap(late, OTHER), swap(early, OTHER)]
     late, early, late_away, early_away = call(
         ffn_kernel,
         [shape(*x.shape) for x in blocks],
@@ -236,10 +256,10 @@
         moved = sum(6 * out.shape[0] * width for out in outs)
         return call(body, outs, [home, back], after, moved=moved)
 
-    *sent, past = pair(late, swap(late_away, 1), 0, [shape(rows, width)] * 3 + [block])
-    sent = [swap(x, s) for x, s in zip(sent, SIDES + (CORNER,))]
+    *sent, past = pair(late, swap(late_away, OTHER), 0, [shape(rows, width)] * 3 + [block])
+    sent = [swap(x, s) for x, s in zip(sent, MIXED + (CORNER,))]
     past = swap(past, SIDES[0])
-    back = swap(early_away, 1)
+    back = swap(early_away, OTHER)
     (kept,) = pair(early, back, len(first), [shape(rows, width, F32)])
     totals = call(total_kernel, [block] * (waves - 1), [kept] + sent, moved=10 * rows * width)
     returned = [cross(totals[j - 1], j) for j in others]
@@ -253,7 +273,7 @@
         shape(tokens, width),
         [weights] + near + returned,
         after=marks,
-        scratch=[pltpu.VMEM((tokens, width), BF16), pltpu.SemaphoreType.DMA((len(chunks(width)),))],
+        scratch=[pltpu.VMEM((tokens, width), BF16), pltpu.SemaphoreType.DMA((len(chunks(width, OUT_CHUNK)),))],
         out_kind=pl.ANY,
         flops=6 * tokens * width * CAP * waves,
         moved=tokens * width * 4,

time: 45.4 us -> 44.5 us (0.980)
  waiting for transfers between devices: 19.1 us -> 17.3 us
  starting transfers between devices: 21.1 us -> 21.9 us
    ppermute x18, waiting for transfers between devices: 19.1 us -> 17.3 us  [swap(): return lax.ppermute(x, 'tp', [(i, i ^ mask[i % 2]) for i in range(devices)])]
    ppermute x18, starting transfers between devices: 21.1 us -> 21.9 us  [swap(): return lax.ppermute(x, 'tp', [(i, i ^ mask[i % 2]) for i in range(devices)])]
    pallas_call x13 -> x14, Pallas kernels: 4.94 us -> 4.94 us  [call(): pl.pallas_call(run, out_shape=outs, in_specs=[space(pltpu.HBM)] * left +...]
  transfers between devices with their start and end apart: 18 -> 18, of which waited for: 12 -> 11; matrix products, arithmetic and copies ran while one was open for 0% -> 0% of each run, Pallas kernels for 1% -> 1%
where the time goes in v7:
time: 44.5 us; the launch traced here: 44.3 us
  starting transfers between devices  21.9 us (49%)
  waiting for transfers between devices  17.3 us (39%)
  Pallas kernels  4.94 us (11%)
    ppermute x18, starting transfers between devices, swap(): return lax.ppermute(x, 'tp', [(i, i ^ mask[i % 2]) for i in range(devices)])  21.9 us
    ppermute x18, waiting for transfers between devices, swap(): return lax.ppermute(x, 'tp', [(i, i ^ mask[i % 2]) for i in range(devices)])  17.3 us
    pallas_call x14, Pallas kernels, call(): pl.pallas_call(run, out_shape=outs, in_specs=[space(pltpu.HBM)] * left +...  4.94 us
  transfers between devices with their start and end apart: 18, of which 11 were waited for; matrix products, arithmetic and copies ran while one was open for 0% of the time, Pallas kernels for 1%

profile of v7, /device:TPU:0, one launch (start us, length us, event | category | flops | bytes accessed | tf_op | source)
XLA Modules:
  0.0 44.3 jit_solution(13871209352838106349)
XLA Ops:
  0.0 1.6 %shard_map.73 = (bf16[8,7168]{1,0:T(8,128)(2,1)S(1)}, bf16[8,7168]{1,0:T(8,128)(2,1)S(1)}, f32[16,64]{1,0:T(8,128)S(1)}) custom-call(bf16[64,7168]{1,0:T(8,128)(2,1)} %refs_0_.2, f32[1,7168]{1,0:T(1,128)} %bitcast.3, s32[8,64]{1,0:T(8,128)} %bitcast.4, f32[8,64]{1,0:T(8,128)} %bitcast.5), custom_call_target="tpu_custom_call" | custom-call | flops 14680064 | bytes 917504 | tf_op jit(solution)/shard_map/pallas_call | solution.py:36
  1.6 5.1 %collective-permute-start = (bf16[8,7168]{1,0:T(8,128)(2,1)S(1)}, bf16[8,7168]{1,0:T(8,128)(2,1)S(1)}, u32[]{:S(2)}, u32[]{:S(2)}) collective-permute-start(bf16[8,7168]{1,0:T(8,128)(2,1)S(1)} %get-tuple-element.23), channel_id=1, source_target_pairs={{0,12},{1,13},{2,14},{3,15},{4,8},{5,9},{6,10},{7,11},{8,4},{9,5},... | collective-permute-start | bytes 344072 | tf_op jit(solution)/shard_map/ppermute | solution.py:193
  6.7 0.1 shard_map.74
  6.8 1.6 %collective-permute-start.5 = (bf16[8,7168]{1,0:T(8,128)(2,1)S(1)}, bf16[8,7168]{1,0:T(8,128)(2,1)S(1)}, u32[]{:S(2)}, u32[]{:S(2)}) collective-permute-start(bf16[8,7168]{1,0:T(8,128)(2,1)S(1)} %get-tuple-element.24.refs_0_), channel_id=1, source_target_pairs={{0,2},{1,3},{2,0},{3,1},{4,6},{5,7},{6,4},{7,5},{8,10},{9,11},{10,... | collective-permute-start | bytes 344072 | tf_op jit(solution)/shard_map/ppermute | solution.py:193
  8.4 2.3 %collective-permute-done.refs_0_.refs_3_ = bf16[8,7168]{1,0:T(8,128)(2,1)S(1)} collective-permute-done((bf16[8,7168]{1,0:T(8,128)(2,1)S(1)}, bf16[8,7168]{1,0:T(8,128)(2,1)S(1)}, u32[]{:S(2)}, u32[]{:S(2)}) %collective-permute-start) | collective-permute-done | bytes 114720 | tf_op jit(solution)/shard_map/ppermute | solution.py:193
  10.7 2.3 %collective-permute-start.3 = (bf16[8,7168]{1,0:T(8,128)(2,1)S(1)}, bf16[8,7168]{1,0:T(8,128)(2,1)S(1)}, u32[]{:S(2)}, u32[]{:S(2)}) collective-permute-start(bf16[8,7168]{1,0:T(8,128)(2,1)S(1)} %collective-permute-done.refs_0_.refs_3_), channel_id=1, source_target_pairs={{0,6},{1,7},{2,4},{3,5},{4,2},{5,3},{6,0},{7,1},{8,14},{9,15},{10,... | collective-permute-start | bytes 344072 | tf_op jit(solution)/shard_map/ppermute | solution.py:193
  13.0 0.9 %collective-permute-start.2 = (bf16[8,7168]{1,0:T(8,128)(2,1)S(1)}, bf16[8,7168]{1,0:T(8,128)(2,1)S(1)}, u32[]{:S(2)}, u32[]{:S(2)}) collective-permute-start(bf16[8,7168]{1,0:T(8,128)(2,1)S(1)} %collective-permute-done.refs_0_.refs_3_), channel_id=1, source_target_pairs={{0,4},{1,3},{2,6},{3,1},{4,0},{5,7},{6,2},{7,5},{8,12},{9,11},{10,... | collective-permute-start | bytes 344072 | tf_op jit(solution)/shard_map/ppermute | solution.py:193
  13.9 0.3 collective-permute-start.1
  14.2 1.8 %collective-permute-start.6 = (bf16[8,7168]{1,0:T(8,128)(2,1)S(1)}, bf16[8,7168]{1,0:T(8,128)(2,1)S(1)}, u32[]{:S(2)}, u32[]{:S(2)}) collective-permute-start(bf16[8,7168]{1,0:T(8,128)(2,1)S(1)} %shard_map.75), channel_id=1, source_target_pairs={{0,2},{1,5},{2,0},{3,7},{4,6},{5,1},{6,4},{7,3},{8,10},{9,13},{10,... | collective-permute-start | bytes 344072 | tf_op jit(solution)/shard_map/ppermute | solution.py:193
  16.1 0.1 collective-permute-start.8
  16.2 1.4 %collective-permute-done.3.refs_2_ = bf16[8,7168]{1,0:T(8,128)(2,1)S(1)} collective-permute-done((bf16[8,7168]{1,0:T(8,128)(2,1)S(1)}, bf16[8,7168]{1,0:T(8,128)(2,1)S(1)}, u32[]{:S(2)}, u32[]{:S(2)}) %collective-permute-start.3) | collective-permute-done | bytes 114720 | tf_op jit(solution)/shard_map/ppermute | solution.py:193
  17.6 1.8 %collective-permute-done.2.refs_1_ = bf16[8,7168]{1,0:T(8,128)(2,1)S(1)} collective-permute-done((bf16[8,7168]{1,0:T(8,128)(2,1)S(1)}, bf16[8,7168]{1,0:T(8,128)(2,1)S(1)}, u32[]{:S(2)}, u32[]{:S(2)}) %collective-permute-start.2) | collective-permute-done | bytes 114720 | tf_op jit(solution)/shard_map/ppermute | solution.py:193
  19.4 0.6 %collective-permute-done.6.refs_3_ = bf16[8,7168]{1,0:T(8,128)(2,1)S(1)} collective-permute-done((bf16[8,7168]{1,0:T(8,128)(2,1)S(1)}, bf16[8,7168]{1,0:T(8,128)(2,1)S(1)}, u32[]{:S(2)}, u32[]{:S(2)}) %collective-permute-start.6) | collective-permute-done | bytes 114720 | tf_op jit(solution)/shard_map/ppermute | solution.py:193
  20.0 0.1 collective-permute-start.7
  20.1 1.8 %collective-permute-done.7.refs_5_ = bf16[32,7168]{1,0:T(8,128)(2,1)S(1)} collective-permute-done((bf16[32,7168]{1,0:T(8,128)(2,1)S(1)}, bf16[32,7168]{1,0:T(8,128)(2,1)S(1)}, u32[]{:S(2)}, u32[]{:S(2)}) %collective-permute-start.7) | collective-permute-done | bytes 458784 | tf_op jit(solution)/shard_map/ppermute | solution.py:193
  21.9 1.7 %shard_map.79 = (bf16[32,7168]{1,0:T(8,128)(2,1)S(1)}, bf16[32,7168]{1,0:T(8,128)(2,1)S(1)}, bf16[32,7168]{1,0:T(8,128)(2,1)S(1)}, bf16[32,7168]{1,0:T(8,128)(2,1)S(1)}) custom-call(bf16[7168,256]{1,0:T(8,128)(2,1)S(1)} %copy-done, bf16[7168,256]{1,0:T(8,128)(2,1)S(1)} %copy-done.1, bf16[256,7168]{1,0:T(8,128)(2,1)S(1)} %copy-done.2, ...), custom_call_target="tpu_custom_call" | custom-call | flops 1409286144 | bytes 11010048 | tf_op jit(solution)/shard_map/pallas_call | solution.py:36
  23.7 0.2 collective-permute-start.10
  23.9 0.4 collective-permute-start.9
  24.2 1.3 %collective-permute-done.10.refs_1_ = bf16[32,7168]{1,0:T(8,128)(2,1)S(1)} collective-permute-done((bf16[32,7168]{1,0:T(8,128)(2,1)S(1)}, bf16[32,7168]{1,0:T(8,128)(2,1)S(1)}, u32[]{:S(2)}, u32[]{:S(2)}) %collective-permute-start.10) | collective-permute-done | bytes 458784 | tf_op jit(solution)/shard_map/ppermute | solution.py:193
  25.6 0.1 shard_map.81
  25.7 1.1 %collective-permute-start.11 = (bf16[8,7168]{1,0:T(8,128)(2,1)S(1)}, bf16[8,7168]{1,0:T(8,128)(2,1)S(1)}, u32[]{:S(2)}, u32[]{:S(2)}) collective-permute-start(bf16[8,7168]{1,0:T(8,128)(2,1)S(1)} %get-tuple-element.29), channel_id=1, source_target_pairs={{0,2},{1,5},{2,0},{3,7},{4,6},{5,1},{6,4},{7,3},{8,10},{9,13},{10,... | collective-permute-start | bytes 344072 | tf_op jit(solution)/shard_map/ppermute | solution.py:193
  26.8 1.2 %collective-permute-start.12 = (bf16[8,7168]{1,0:T(8,128)(2,1)S(1)}, bf16[8,7168]{1,0:T(8,128)(2,1)S(1)}, u32[]{:S(2)}, u32[]{:S(2)}) collective-permute-start(bf16[8,7168]{1,0:T(8,128)(2,1)S(1)} %get-tuple-element.30), channel_id=1, source_target_pairs={{0,4},{1,3},{2,6},{3,1},{4,0},{5,7},{6,2},{7,5},{8,12},{9,11},{10,... | collective-permute-start | bytes 344072 | tf_op jit(solution)/shard_map/ppermute | solution.py:193
  28.0 1.2 %collective-permute-start.13 = (bf16[8,7168]{1,0:T(8,128)(2,1)S(1)}, bf16[8,7168]{1,0:T(8,128)(2,1)S(1)}, u32[]{:S(2)}, u32[]{:S(2)}) collective-permute-start(bf16[8,7168]{1,0:T(8,128)(2,1)S(1)} %get-tuple-element.31), channel_id=1, source_target_pairs={{0,6},{1,7},{2,4},{3,5},{4,2},{5,3},{6,0},{7,1},{8,14},{9,15},{10,... | collective-permute-start | bytes 344072 | tf_op jit(solution)/shard_map/ppermute | solution.py:193
  29.2 1.0 %collective-permute-start.15 = (bf16[8,7168]{1,0:T(8,128)(2,1)S(1)}, bf16[8,7168]{1,0:T(8,128)(2,1)S(1)}, u32[]{:S(2)}, u32[]{:S(2)}) collective-permute-start(bf16[8,7168]{1,0:T(8,128)(2,1)S(1)} %get-tuple-element.34), channel_id=1, source_target_pairs={{0,2},{1,3},{2,0},{3,1},{4,6},{5,7},{6,4},{7,5},{8,10},{9,11},{10,... | collective-permute-start | bytes 344072 | tf_op jit(solution)/shard_map/ppermute | solution.py:193
  30.3 1.8 %collective-permute-done.11.refs_1_ = bf16[8,7168]{1,0:T(8,128)(2,1)S(1)} collective-permute-done((bf16[8,7168]{1,0:T(8,128)(2,1)S(1)}, bf16[8,7168]{1,0:T(8,128)(2,1)S(1)}, u32[]{:S(2)}, u32[]{:S(2)}) %collective-permute-start.11) | collective-permute-done | bytes 114720 | tf_op jit(solution)/shard_map/ppermute | solution.py:193
  32.1 0.4 collective-permute-done.12.refs_2_
  32.5 2.1 %collective-permute-done.13.refs_3_ = bf16[8,7168]{1,0:T(8,128)(2,1)S(1)} collective-permute-done((bf16[8,7168]{1,0:T(8,128)(2,1)S(1)}, bf16[8,7168]{1,0:T(8,128)(2,1)S(1)}, u32[]{:S(2)}, u32[]{:S(2)}) %collective-permute-start.13) | collective-permute-done | bytes 114720 | tf_op jit(solution)/shard_map/ppermute | solution.py:193
  34.6 3.2 %collective-permute-start.17 = (bf16[8,7168]{1,0:T(8,128)(2,1)S(1)}, bf16[8,7168]{1,0:T(8,128)(2,1)S(1)}, u32[]{:S(2)}, u32[]{:S(2)}) collective-permute-start(bf16[8,7168]{1,0:T(8,128)(2,1)S(1)} %shard_map.82.refs_2_), channel_id=1, source_target_pairs={{0,12},{1,13},{2,14},{3,15},{4,8},{5,9},{6,10},{7,11},{8,4},{9,5},... | collective-permute-start | bytes 344072 | tf_op jit(solution)/shard_map/ppermute | solution.py:193
  38.0 1.3 %collective-permute-start.14 = (bf16[8,7168]{1,0:T(8,128)(2,1)S(1)}, bf16[8,7168]{1,0:T(8,128)(2,1)S(1)}, u32[]{:S(2)}, u32[]{:S(2)}) collective-permute-start(bf16[8,7168]{1,0:T(8,128)(2,1)S(1)} %get-tuple-element.33.refs_3_), channel_id=1, source_target_pairs={{0,2},{1,3},{2,0},{3,1},{4,6},{5,7},{6,4},{7,5},{8,10},{9,11},{10,... | collective-permute-start | bytes 344072 | tf_op jit(solution)/shard_map/ppermute | solution.py:193
  39.4 2.3 %collective-permute-done.17.refs_0_.refs_4_ = bf16[8,7168]{1,0:T(8,128)(2,1)S(1)} collective-permute-done((bf16[8,7168]{1,0:T(8,128)(2,1)S(1)}, bf16[8,7168]{1,0:T(8,128)(2,1)S(1)}, u32[]{:S(2)}, u32[]{:S(2)}) %collective-permute-start.17) | collective-permute-done | bytes 114720 | tf_op jit(solution)/shard_map/ppermute | solution.py:193
  41.7 1.4 %collective-permute-done.16.refs_3_ = bf16[8,7168]{1,0:T(8,128)(2,1)S(1)} collective-permute-done((bf16[8,7168]{1,0:T(8,128)(2,1)S(1)}, bf16[8,7168]{1,0:T(8,128)(2,1)S(1)}, u32[]{:S(2)}, u32[]{:S(2)}) %collective-permute-start.16) | collective-permute-done | bytes 114720 | tf_op jit(solution)/shard_map/ppermute | solution.py:193
  43.1 1.2 %shard_map.86 = bf16[64,7168]{1,0:T(8,128)(2,1)} custom-call(bf16[64,48]{1,0:T(8,128)(2,1)S(1)} %get-tuple-element.22.refs_0_, f32[8,7168]{1,0:T(8,128)S(1)} %get-tuple-element.32.refs_1_, bf16[8,7168]{1,0:T(8,128)(2,1)S(1)} %collective-permute-done.14.refs_2_, bf16[8,7168]{1,0:T(8,128)(2,1)S(1)} %collective-permute-done.16.refs_3_, ...), custom_call_target="tpu_custom_call" | custom-call | flops 44040192 | bytes 1835008 | tf_op jit(solution)/shard_map/pallas_call | solution.py:36
  (24 shorter events, 0.4 us)
Async XLA Ops:
  1.6 9.1 %collective-permute-start = (bf16[8,7168]{1,0:T(8,128)(2,1)S(1)}, bf16[8,7168]{1,0:T(8,128)(2,1)S(1)}, u32[]{:S(2)}, u32[]{:S(2)}) collective-permute-start(bf16[8,7168]{1,0:T(8,128)(2,1)S(1)} %get-tuple-element.23), channel_id=1, source_target_pairs={{0,12},{1,13},{2,14},{3,15},{4,8},{5,9},{6,10},{7,11},{8,4},{9,5},... | collective-permute-start | bytes 344072 | tf_op jit(solution)/shard_map/ppermute | solution.py:193
  6.7 15.2 %copy-start = (bf16[7168,256]{1,0:T(8,128)(2,1)S(1)}, bf16[7168,256]{1,0:T(8,128)(2,1)}, u32[]{:S(2)}) copy-start(bf16[7168,256]{1,0:T(8,128)(2,1)} %refs_0_.3) | copy-start | bytes 11010052
  6.7 15.2 %copy-start.1 = (bf16[7168,256]{1,0:T(8,128)(2,1)S(1)}, bf16[7168,256]{1,0:T(8,128)(2,1)}, u32[]{:S(2)}) copy-start(bf16[7168,256]{1,0:T(8,128)(2,1)} %refs_1_.1) | copy-start | bytes 11010052
  6.7 15.2 %copy-start.2 = (bf16[256,7168]{1,0:T(8,128)(2,1)S(1)}, bf16[256,7168]{1,0:T(8,128)(2,1)}, u32[]{:S(2)}) copy-start(bf16[256,7168]{1,0:T(8,128)(2,1)} %refs_2_.1) | copy-start | bytes 11010052
  6.8 7.4 %collective-permute-start.5 = (bf16[8,7168]{1,0:T(8,128)(2,1)S(1)}, bf16[8,7168]{1,0:T(8,128)(2,1)S(1)}, u32[]{:S(2)}, u32[]{:S(2)}) collective-permute-start(bf16[8,7168]{1,0:T(8,128)(2,1)S(1)} %get-tuple-element.24.refs_0_), channel_id=1, source_target_pairs={{0,2},{1,3},{2,0},{3,1},{4,6},{5,7},{6,4},{7,5},{8,10},{9,11},{10,... | collective-permute-start | bytes 344072 | tf_op jit(solution)/shard_map/ppermute | solution.py:193
  8.4 5.8 %collective-permute-start.4 = (bf16[8,7168]{1,0:T(8,128)(2,1)S(1)}, bf16[8,7168]{1,0:T(8,128)(2,1)S(1)}, u32[]{:S(2)}, u32[]{:S(2)}) collective-permute-start(bf16[8,7168]{1,0:T(8,128)(2,1)S(1)} %get-tuple-element.20.refs_0_), channel_id=1, source_target_pairs={{0,4},{1,5},{2,6},{3,7},{4,0},{5,1},{6,2},{7,3},{8,12},{9,13},{10,... | collective-permute-start | bytes 344072 | tf_op jit(solution)/shard_map/ppermute | solution.py:193
  10.7 6.9 %collective-permute-start.3 = (bf16[8,7168]{1,0:T(8,128)(2,1)S(1)}, bf16[8,7168]{1,0:T(8,128)(2,1)S(1)}, u32[]{:S(2)}, u32[]{:S(2)}) collective-permute-start(bf16[8,7168]{1,0:T(8,128)(2,1)S(1)} %collective-permute-done.refs_0_.refs_3_), channel_id=1, source_target_pairs={{0,6},{1,7},{2,4},{3,5},{4,2},{5,3},{6,0},{7,1},{8,14},{9,15},{10,... | collective-permute-start | bytes 344072 | tf_op jit(solution)/shard_map/ppermute | solution.py:193
  13.0 6.4 %collective-permute-start.2 = (bf16[8,7168]{1,0:T(8,128)(2,1)S(1)}, bf16[8,7168]{1,0:T(8,128)(2,1)S(1)}, u32[]{:S(2)}, u32[]{:S(2)}) collective-permute-start(bf16[8,7168]{1,0:T(8,128)(2,1)S(1)} %collective-permute-done.refs_0_.refs_3_), channel_id=1, source_target_pairs={{0,4},{1,3},{2,6},{3,1},{4,0},{5,7},{6,2},{7,5},{8,12},{9,11},{10,... | collective-permute-start | bytes 344072 | tf_op jit(solution)/shard_map/ppermute | solution.py:193
  13.9 5.5 %collective-permute-start.1 = (bf16[8,7168]{1,0:T(8,128)(2,1)S(1)}, bf16[8,7168]{1,0:T(8,128)(2,1)S(1)}, u32[]{:S(2)}, u32[]{:S(2)}) collective-permute-start(bf16[8,7168]{1,0:T(8,128)(2,1)S(1)} %collective-permute-done.refs_0_.refs_3_), channel_id=1, source_target_pairs={{0,2},{1,5},{2,0},{3,7},{4,6},{5,1},{6,4},{7,3},{8,10},{9,13},{10,... | collective-permute-start | bytes 344072 | tf_op jit(solution)/shard_map/ppermute | solution.py:193
  14.2 5.8 %collective-permute-start.6 = (bf16[8,7168]{1,0:T(8,128)(2,1)S(1)}, bf16[8,7168]{1,0:T(8,128)(2,1)S(1)}, u32[]{:S(2)}, u32[]{:S(2)}) collective-permute-start(bf16[8,7168]{1,0:T(8,128)(2,1)S(1)} %shard_map.75), channel_id=1, source_target_pairs={{0,2},{1,5},{2,0},{3,7},{4,6},{5,1},{6,4},{7,3},{8,10},{9,13},{10,... | collective-permute-start | bytes 344072 | tf_op jit(solution)/shard_map/ppermute | solution.py:193
  16.1 4.0 %collective-permute-start.8 = (bf16[32,7168]{1,0:T(8,128)(2,1)S(1)}, bf16[32,7168]{1,0:T(8,128)(2,1)S(1)}, u32[]{:S(2)}, u32[]{:S(2)}) collective-permute-start(bf16[32,7168]{1,0:T(8,128)(2,1)S(1)} %shard_map.78.refs_4_), channel_id=1, source_target_pairs={{0,1},{1,0},{2,3},{3,2},{4,5},{5,4},{6,7},{7,6},{8,9},{9,8},{10,11... | collective-permute-start | bytes 1376264 | tf_op jit(solution)/shard_map/ppermute | solution.py:193
  20.0 1.9 %collective-permute-start.7 = (bf16[32,7168]{1,0:T(8,128)(2,1)S(1)}, bf16[32,7168]{1,0:T(8,128)(2,1)S(1)}, u32[]{:S(2)}, u32[]{:S(2)}) collective-permute-start(bf16[32,7168]{1,0:T(8,128)(2,1)S(1)} %shard_map.76.refs_3_), channel_id=1, source_target_pairs={{0,1},{1,0},{2,3},{3,2},{4,5},{5,4},{6,7},{7,6},{8,9},{9,8},{10,11... | collective-permute-start | bytes 1376264 | tf_op jit(solution)/shard_map/ppermute | solution.py:193
  23.7 1.9 %collective-permute-start.10 = (bf16[32,7168]{1,0:T(8,128)(2,1)S(1)}, bf16[32,7168]{1,0:T(8,128)(2,1)S(1)}, u32[]{:S(2)}, u32[]{:S(2)}) collective-permute-start(bf16[32,7168]{1,0:T(8,128)(2,1)S(1)} %get-tuple-element.28), channel_id=1, source_target_pairs={{0,1},{1,0},{2,3},{3,2},{4,5},{5,4},{6,7},{7,6},{8,9},{9,8},{10,11... | collective-permute-start | bytes 1376264 | tf_op jit(solution)/shard_map/ppermute | solution.py:193
  23.9 6.4 %collective-permute-start.9 = (bf16[32,7168]{1,0:T(8,128)(2,1)S(1)}, bf16[32,7168]{1,0:T(8,128)(2,1)S(1)}, u32[]{:S(2)}, u32[]{:S(2)}) collective-permute-start(bf16[32,7168]{1,0:T(8,128)(2,1)S(1)} %get-tuple-element.26), channel_id=1, source_target_pairs={{0,1},{1,0},{2,3},{3,2},{4,5},{5,4},{6,7},{7,6},{8,9},{9,8},{10,11... | collective-permute-start | bytes 1376264 | tf_op jit(solution)/shard_map/ppermute | solution.py:193
  25.7 6.4 %collective-permute-start.11 = (bf16[8,7168]{1,0:T(8,128)(2,1)S(1)}, bf16[8,7168]{1,0:T(8,128)(2,1)S(1)}, u32[]{:S(2)}, u32[]{:S(2)}) collective-permute-start(bf16[8,7168]{1,0:T(8,128)(2,1)S(1)} %get-tuple-element.29), channel_id=1, source_target_pairs={{0,2},{1,5},{2,0},{3,7},{4,6},{5,1},{6,4},{7,3},{8,10},{9,13},{10,... | collective-permute-start | bytes 344072 | tf_op jit(solution)/shard_map/ppermute | solution.py:193
  26.8 5.7 %collective-permute-start.12 = (bf16[8,7168]{1,0:T(8,128)(2,1)S(1)}, bf16[8,7168]{1,0:T(8,128)(2,1)S(1)}, u32[]{:S(2)}, u32[]{:S(2)}) collective-permute-start(bf16[8,7168]{1,0:T(8,128)(2,1)S(1)} %get-tuple-element.30), channel_id=1, source_target_pairs={{0,4},{1,3},{2,6},{3,1},{4,0},{5,7},{6,2},{7,5},{8,12},{9,11},{10,... | collective-permute-start | bytes 344072 | tf_op jit(solution)/shard_map/ppermute | solution.py:193
  28.0 6.5 %collective-permute-start.13 = (bf16[8,7168]{1,0:T(8,128)(2,1)S(1)}, bf16[8,7168]{1,0:T(8,128)(2,1)S(1)}, u32[]{:S(2)}, u32[]{:S(2)}) collective-permute-start(bf16[8,7168]{1,0:T(8,128)(2,1)S(1)} %get-tuple-element.31), channel_id=1, source_target_pairs={{0,6},{1,7},{2,4},{3,5},{4,2},{5,3},{6,0},{7,1},{8,14},{9,15},{10,... | collective-permute-start | bytes 344072 | tf_op jit(solution)/shard_map/ppermute | solution.py:193
  29.2 8.7 %collective-permute-start.15 = (bf16[8,7168]{1,0:T(8,128)(2,1)S(1)}, bf16[8,7168]{1,0:T(8,128)(2,1)S(1)}, u32[]{:S(2)}, u32[]{:S(2)}) collective-permute-start(bf16[8,7168]{1,0:T(8,128)(2,1)S(1)} %get-tuple-element.34), channel_id=1, source_target_pairs={{0,2},{1,3},{2,0},{3,1},{4,6},{5,7},{6,4},{7,5},{8,10},{9,11},{10,... | collective-permute-start | bytes 344072 | tf_op jit(solution)/shard_map/ppermute | solution.py:193
  34.6 7.1 %collective-permute-start.17 = (bf16[8,7168]{1,0:T(8,128)(2,1)S(1)}, bf16[8,7168]{1,0:T(8,128)(2,1)S(1)}, u32[]{:S(2)}, u32[]{:S(2)}) collective-permute-start(bf16[8,7168]{1,0:T(8,128)(2,1)S(1)} %shard_map.82.refs_2_), channel_id=1, source_target_pairs={{0,12},{1,13},{2,14},{3,15},{4,8},{5,9},{6,10},{7,11},{8,4},{9,5},... | collective-permute-start | bytes 344072 | tf_op jit(solution)/shard_map/ppermute | solution.py:193
  37.9 5.2 %collective-permute-start.16 = (bf16[8,7168]{1,0:T(8,128)(2,1)S(1)}, bf16[8,7168]{1,0:T(8,128)(2,1)S(1)}, u32[]{:S(2)}, u32[]{:S(2)}) collective-permute-start(bf16[8,7168]{1,0:T(8,128)(2,1)S(1)} %shard_map.84), channel_id=1, source_target_pairs={{0,4},{1,5},{2,6},{3,7},{4,0},{5,1},{6,2},{7,3},{8,12},{9,13},{10,... | collective-permute-start | bytes 344072 | tf_op jit(solution)/shard_map/ppermute | solution.py:193
  38.0 5.1 %collective-permute-start.14 = (bf16[8,7168]{1,0:T(8,128)(2,1)S(1)}, bf16[8,7168]{1,0:T(8,128)(2,1)S(1)}, u32[]{:S(2)}, u32[]{:S(2)}) collective-permute-start(bf16[8,7168]{1,0:T(8,128)(2,1)S(1)} %get-tuple-element.33.refs_3_), channel_id=1, source_target_pairs={{0,2},{1,3},{2,0},{3,1},{4,6},{5,7},{6,4},{7,5},{8,10},{9,11},{10,... | collective-permute-start | bytes 344072 | tf_op jit(solution)/shard_map/ppermute | solution.py:193

commit v8 on v7

--- a/solution.py
+++ b/solution.py
@@ -13,7 +13,7 @@
 CAP = 8
 EPSILON = 1e-06
 SIDES = ((2, 2), (4, 4))
-MIXED = ((2, 4), (4, 2))
+MIXED = ((4, 2), (2, 4))
 CORNER = (6, 6)
 OTHER = (1, 1)
 OWN_FLOPS = 7_000_000_000
@@ -233,7 +233,7 @@
     )
 
     first = [own, swap(own, SIDES[0]), side_two]
-    past = call(choose_kernel, block, [first[2], first[1]], moved=6 * CAP * width)
+    past = call(choose_kernel, block, [first[1], first[2]], moved=6 * CAP * width)
     past = swap(past, MIXED[0])
     rows = CAP * (waves - 1)
     far = heads[0] if waves == 2 else stack(heads)
@@ -261,7 +261,7 @@
     past = swap(past, SIDES[0])
     back = swap(early_away, OTHER)
     (kept,) = pair(early, back, len(first), [shape(rows, width, F32)])
-    totals = call(total_kernel, [block] * (waves - 1), [kept] + sent, moved=10 * rows * width)
+    totals = call(total_kernel, [block] * (waves - 1), [kept, sent[1], sent[0], sent[2]], moved=10 * rows * width)
     returned = [cross(totals[j - 1], j) for j in others]
     kept, one = pair(early, back, 0, [shape(CAP, width, F32), block], after=totals)
     body = functools.partial(passed_kernel, 2 * CAP)

time: 44.5 us -> 44.2 us (level)
  waiting for transfers between devices: 17.3 us -> 16.6 us
  starting transfers between devices: 21.9 us -> 22.4 us
    ppermute x18, waiting for transfers between devices: 17.3 us -> 16.6 us  [swap(): return lax.ppermute(x, 'tp', [(i, i ^ mask[i % 2]) for i in range(devices)])]
    ppermute x18, starting transfers between devices: 21.9 us -> 22.4 us  [swap(): return lax.ppermute(x, 'tp', [(i, i ^ mask[i % 2]) for i in range(devices)])]
  transfers between devices with their start and end apart: 18 -> 18, of which waited for: 11 -> 10; matrix products, arithmetic and copies ran while one was open for 0% -> 0% of each run, Pallas kernels for 1% -> 1%
where the time goes in v8:
time: 44.2 us; the launch traced here: 44 us
  starting transfers between devices  22.4 us (51%)
  waiting for transfers between devices  16.6 us (38%)
  Pallas kernels  4.95 us (11%)
    ppermute x18, starting transfers between devices, swap(): return lax.ppermute(x, 'tp', [(i, i ^ mask[i % 2]) for i in range(devices)])  22.4 us
    ppermute x18, waiting for transfers between devices, swap(): return lax.ppermute(x, 'tp', [(i, i ^ mask[i % 2]) for i in range(devices)])  16.6 us
    pallas_call x14, Pallas kernels, call(): pl.pallas_call(run, out_shape=outs, in_specs=[space(pltpu.HBM)] * left +...  4.95 us
  transfers between devices with their start and end apart: 18, of which 10 were waited for; matrix products, arithmetic and copies ran while one was open for 0% of the time, Pallas kernels for 1%

profile of v8, /device:TPU:0, one launch (start us, length us, event | category | flops | bytes accessed | tf_op | source)
XLA Modules:
  0.0 44.0 jit_solution(13908370453483256583)
XLA Ops:
  0.0 1.6 %shard_map.73 = (bf16[8,7168]{1,0:T(8,128)(2,1)S(1)}, bf16[8,7168]{1,0:T(8,128)(2,1)S(1)}, f32[16,64]{1,0:T(8,128)S(1)}) custom-call(bf16[64,7168]{1,0:T(8,128)(2,1)} %refs_0_.2, f32[1,7168]{1,0:T(1,128)} %bitcast.3, s32[8,64]{1,0:T(8,128)} %bitcast.4, f32[8,64]{1,0:T(8,128)} %bitcast.5), custom_call_target="tpu_custom_call" | custom-call | flops 14680064 | bytes 917504 | tf_op jit(solution)/shard_map/pallas_call | solution.py:36
  1.6 5.1 %collective-permute-start = (bf16[8,7168]{1,0:T(8,128)(2,1)S(1)}, bf16[8,7168]{1,0:T(8,128)(2,1)S(1)}, u32[]{:S(2)}, u32[]{:S(2)}) collective-permute-start(bf16[8,7168]{1,0:T(8,128)(2,1)S(1)} %get-tuple-element.23), channel_id=1, source_target_pairs={{0,12},{1,13},{2,14},{3,15},{4,8},{5,9},{6,10},{7,11},{8,4},{9,5},... | collective-permute-start | bytes 344072 | tf_op jit(solution)/shard_map/ppermute | solution.py:193
  6.7 0.1 shard_map.74
  6.8 1.6 %collective-permute-start.4 = (bf16[8,7168]{1,0:T(8,128)(2,1)S(1)}, bf16[8,7168]{1,0:T(8,128)(2,1)S(1)}, u32[]{:S(2)}, u32[]{:S(2)}) collective-permute-start(bf16[8,7168]{1,0:T(8,128)(2,1)S(1)} %get-tuple-element.24.refs_0_), channel_id=1, source_target_pairs={{0,2},{1,3},{2,0},{3,1},{4,6},{5,7},{6,4},{7,5},{8,10},{9,11},{10,... | collective-permute-start | bytes 344072 | tf_op jit(solution)/shard_map/ppermute | solution.py:193
  8.4 2.3 %collective-permute-done.refs_0_.refs_3_ = bf16[8,7168]{1,0:T(8,128)(2,1)S(1)} collective-permute-done((bf16[8,7168]{1,0:T(8,128)(2,1)S(1)}, bf16[8,7168]{1,0:T(8,128)(2,1)S(1)}, u32[]{:S(2)}, u32[]{:S(2)}) %collective-permute-start) | collective-permute-done | bytes 114720 | tf_op jit(solution)/shard_map/ppermute | solution.py:193
  10.7 2.3 %collective-permute-start.3 = (bf16[8,7168]{1,0:T(8,128)(2,1)S(1)}, bf16[8,7168]{1,0:T(8,128)(2,1)S(1)}, u32[]{:S(2)}, u32[]{:S(2)}) collective-permute-start(bf16[8,7168]{1,0:T(8,128)(2,1)S(1)} %collective-permute-done.refs_0_.refs_3_), channel_id=1, source_target_pairs={{0,6},{1,7},{2,4},{3,5},{4,2},{5,3},{6,0},{7,1},{8,14},{9,15},{10,... | collective-permute-start | bytes 344072 | tf_op jit(solution)/shard_map/ppermute | solution.py:193
  13.0 0.5 %collective-permute-start.2 = (bf16[8,7168]{1,0:T(8,128)(2,1)S(1)}, bf16[8,7168]{1,0:T(8,128)(2,1)S(1)}, u32[]{:S(2)}, u32[]{:S(2)}) collective-permute-start(bf16[8,7168]{1,0:T(8,128)(2,1)S(1)} %collective-permute-done.refs_0_.refs_3_), channel_id=1, source_target_pairs={{0,2},{1,5},{2,0},{3,7},{4,6},{5,1},{6,4},{7,3},{8,10},{9,13},{10,... | collective-permute-start | bytes 344072 | tf_op jit(solution)/shard_map/ppermute | solution.py:193
  13.5 0.7 %collective-permute-start.1 = (bf16[8,7168]{1,0:T(8,128)(2,1)S(1)}, bf16[8,7168]{1,0:T(8,128)(2,1)S(1)}, u32[]{:S(2)}, u32[]{:S(2)}) collective-permute-start(bf16[8,7168]{1,0:T(8,128)(2,1)S(1)} %collective-permute-done.refs_0_.refs_3_), channel_id=1, source_target_pairs={{0,4},{1,3},{2,6},{3,1},{4,0},{5,7},{6,2},{7,5},{8,12},{9,11},{10,... | collective-permute-start | bytes 344072 | tf_op jit(solution)/shard_map/ppermute | solution.py:193
  14.2 1.4 %collective-permute-start.6 = (bf16[8,7168]{1,0:T(8,128)(2,1)S(1)}, bf16[8,7168]{1,0:T(8,128)(2,1)S(1)}, u32[]{:S(2)}, u32[]{:S(2)}) collective-permute-start(bf16[8,7168]{1,0:T(8,128)(2,1)S(1)} %shard_map.75), channel_id=1, source_target_pairs={{0,4},{1,3},{2,6},{3,1},{4,0},{5,7},{6,2},{7,5},{8,12},{9,11},{10,... | collective-permute-start | bytes 344072 | tf_op jit(solution)/shard_map/ppermute | solution.py:193
  15.7 0.1 collective-permute-start.8
  15.7 1.5 %collective-permute-done.3.refs_2_ = bf16[8,7168]{1,0:T(8,128)(2,1)S(1)} collective-permute-done((bf16[8,7168]{1,0:T(8,128)(2,1)S(1)}, bf16[8,7168]{1,0:T(8,128)(2,1)S(1)}, u32[]{:S(2)}, u32[]{:S(2)}) %collective-permute-start.3) | collective-permute-done | bytes 114720 | tf_op jit(solution)/shard_map/ppermute | solution.py:193
  17.3 2.2 %collective-permute-done.2.refs_1_ = bf16[8,7168]{1,0:T(8,128)(2,1)S(1)} collective-permute-done((bf16[8,7168]{1,0:T(8,128)(2,1)S(1)}, bf16[8,7168]{1,0:T(8,128)(2,1)S(1)}, u32[]{:S(2)}, u32[]{:S(2)}) %collective-permute-start.2) | collective-permute-done | bytes 114720 | tf_op jit(solution)/shard_map/ppermute | solution.py:193
  19.6 0.1 collective-permute-start.7
  19.7 1.8 %collective-permute-done.7.refs_5_ = bf16[32,7168]{1,0:T(8,128)(2,1)S(1)} collective-permute-done((bf16[32,7168]{1,0:T(8,128)(2,1)S(1)}, bf16[32,7168]{1,0:T(8,128)(2,1)S(1)}, u32[]{:S(2)}, u32[]{:S(2)}) %collective-permute-start.7) | collective-permute-done | bytes 458784 | tf_op jit(solution)/shard_map/ppermute | solution.py:193
  21.5 1.7 %shard_map.79 = (bf16[32,7168]{1,0:T(8,128)(2,1)S(1)}, bf16[32,7168]{1,0:T(8,128)(2,1)S(1)}, bf16[32,7168]{1,0:T(8,128)(2,1)S(1)}, bf16[32,7168]{1,0:T(8,128)(2,1)S(1)}) custom-call(bf16[7168,256]{1,0:T(8,128)(2,1)S(1)} %copy-done, bf16[7168,256]{1,0:T(8,128)(2,1)S(1)} %copy-done.1, bf16[256,7168]{1,0:T(8,128)(2,1)S(1)} %copy-done.2, ...), custom_call_target="tpu_custom_call" | custom-call | flops 1409286144 | bytes 11010048 | tf_op jit(solution)/shard_map/pallas_call | solution.py:36
  23.2 0.2 collective-permute-start.10
  23.4 0.4 collective-permute-start.9
  23.8 1.3 %collective-permute-done.10.refs_1_ = bf16[32,7168]{1,0:T(8,128)(2,1)S(1)} collective-permute-done((bf16[32,7168]{1,0:T(8,128)(2,1)S(1)}, bf16[32,7168]{1,0:T(8,128)(2,1)S(1)}, u32[]{:S(2)}, u32[]{:S(2)}) %collective-permute-start.10) | collective-permute-done | bytes 458784 | tf_op jit(solution)/shard_map/ppermute | solution.py:193
  25.1 0.1 shard_map.81
  25.2 1.6 %collective-permute-start.11 = (bf16[8,7168]{1,0:T(8,128)(2,1)S(1)}, bf16[8,7168]{1,0:T(8,128)(2,1)S(1)}, u32[]{:S(2)}, u32[]{:S(2)}) collective-permute-start(bf16[8,7168]{1,0:T(8,128)(2,1)S(1)} %get-tuple-element.29), channel_id=1, source_target_pairs={{0,2},{1,5},{2,0},{3,7},{4,6},{5,1},{6,4},{7,3},{8,10},{9,13},{10,... | collective-permute-start | bytes 344072 | tf_op jit(solution)/shard_map/ppermute | solution.py:193
  26.8 0.9 %collective-permute-start.12 = (bf16[8,7168]{1,0:T(8,128)(2,1)S(1)}, bf16[8,7168]{1,0:T(8,128)(2,1)S(1)}, u32[]{:S(2)}, u32[]{:S(2)}) collective-permute-start(bf16[8,7168]{1,0:T(8,128)(2,1)S(1)} %get-tuple-element.30), channel_id=1, source_target_pairs={{0,4},{1,3},{2,6},{3,1},{4,0},{5,7},{6,2},{7,5},{8,12},{9,11},{10,... | collective-permute-start | bytes 344072 | tf_op jit(solution)/shard_map/ppermute | solution.py:193
  27.7 1.0 %collective-permute-start.13 = (bf16[8,7168]{1,0:T(8,128)(2,1)S(1)}, bf16[8,7168]{1,0:T(8,128)(2,1)S(1)}, u32[]{:S(2)}, u32[]{:S(2)}) collective-permute-start(bf16[8,7168]{1,0:T(8,128)(2,1)S(1)} %get-tuple-element.31), channel_id=1, source_target_pairs={{0,6},{1,7},{2,4},{3,5},{4,2},{5,3},{6,0},{7,1},{8,14},{9,15},{10,... | collective-permute-start | bytes 344072 | tf_op jit(solution)/shard_map/ppermute | solution.py:193
  28.7 1.5 %collective-permute-start.15 = (bf16[8,7168]{1,0:T(8,128)(2,1)S(1)}, bf16[8,7168]{1,0:T(8,128)(2,1)S(1)}, u32[]{:S(2)}, u32[]{:S(2)}) collective-permute-start(bf16[8,7168]{1,0:T(8,128)(2,1)S(1)} %get-tuple-element.34), channel_id=1, source_target_pairs={{0,2},{1,3},{2,0},{3,1},{4,6},{5,7},{6,4},{7,5},{8,10},{9,11},{10,... | collective-permute-start | bytes 344072 | tf_op jit(solution)/shard_map/ppermute | solution.py:193
  30.3 1.0 %collective-permute-done.11.refs_1_ = bf16[8,7168]{1,0:T(8,128)(2,1)S(1)} collective-permute-done((bf16[8,7168]{1,0:T(8,128)(2,1)S(1)}, bf16[8,7168]{1,0:T(8,128)(2,1)S(1)}, u32[]{:S(2)}, u32[]{:S(2)}) %collective-permute-start.11) | collective-permute-done | bytes 114720 | tf_op jit(solution)/shard_map/ppermute | solution.py:193
  31.3 1.4 %collective-permute-done.12.refs_2_ = bf16[8,7168]{1,0:T(8,128)(2,1)S(1)} collective-permute-done((bf16[8,7168]{1,0:T(8,128)(2,1)S(1)}, bf16[8,7168]{1,0:T(8,128)(2,1)S(1)}, u32[]{:S(2)}, u32[]{:S(2)}) %collective-permute-start.12) | collective-permute-done | bytes 114720 | tf_op jit(solution)/shard_map/ppermute | solution.py:193
  32.7 1.3 %collective-permute-done.13.refs_3_ = bf16[8,7168]{1,0:T(8,128)(2,1)S(1)} collective-permute-done((bf16[8,7168]{1,0:T(8,128)(2,1)S(1)}, bf16[8,7168]{1,0:T(8,128)(2,1)S(1)}, u32[]{:S(2)}, u32[]{:S(2)}) %collective-permute-start.13) | collective-permute-done | bytes 114720 | tf_op jit(solution)/shard_map/ppermute | solution.py:193
  34.1 3.5 %collective-permute-start.17 = (bf16[8,7168]{1,0:T(8,128)(2,1)S(1)}, bf16[8,7168]{1,0:T(8,128)(2,1)S(1)}, u32[]{:S(2)}, u32[]{:S(2)}) collective-permute-start(bf16[8,7168]{1,0:T(8,128)(2,1)S(1)} %shard_map.82.refs_2_), channel_id=1, source_target_pairs={{0,12},{1,13},{2,14},{3,15},{4,8},{5,9},{6,10},{7,11},{8,4},{9,5},... | collective-permute-start | bytes 344072 | tf_op jit(solution)/shard_map/ppermute | solution.py:193
  37.7 0.3 collective-permute-start.16
  38.0 1.2 %collective-permute-start.14 = (bf16[8,7168]{1,0:T(8,128)(2,1)S(1)}, bf16[8,7168]{1,0:T(8,128)(2,1)S(1)}, u32[]{:S(2)}, u32[]{:S(2)}) collective-permute-start(bf16[8,7168]{1,0:T(8,128)(2,1)S(1)} %get-tuple-element.33.refs_3_), channel_id=1, source_target_pairs={{0,2},{1,3},{2,0},{3,1},{4,6},{5,7},{6,4},{7,5},{8,10},{9,11},{10,... | collective-permute-start | bytes 344072 | tf_op jit(solution)/shard_map/ppermute | solution.py:193
  39.2 1.6 %collective-permute-done.17.refs_0_.refs_4_ = bf16[8,7168]{1,0:T(8,128)(2,1)S(1)} collective-permute-done((bf16[8,7168]{1,0:T(8,128)(2,1)S(1)}, bf16[8,7168]{1,0:T(8,128)(2,1)S(1)}, u32[]{:S(2)}, u32[]{:S(2)}) %collective-permute-start.17) | collective-permute-done | bytes 114720 | tf_op jit(solution)/shard_map/ppermute | solution.py:193
  40.9 2.0 %collective-permute-done.16.refs_3_ = bf16[8,7168]{1,0:T(8,128)(2,1)S(1)} collective-permute-done((bf16[8,7168]{1,0:T(8,128)(2,1)S(1)}, bf16[8,7168]{1,0:T(8,128)(2,1)S(1)}, u32[]{:S(2)}, u32[]{:S(2)}) %collective-permute-start.16) | collective-permute-done | bytes 114720 | tf_op jit(solution)/shard_map/ppermute | solution.py:193
  42.9 1.2 %shard_map.86 = bf16[64,7168]{1,0:T(8,128)(2,1)} custom-call(bf16[64,48]{1,0:T(8,128)(2,1)S(1)} %get-tuple-element.22.refs_0_, f32[8,7168]{1,0:T(8,128)S(1)} %get-tuple-element.32.refs_1_, bf16[8,7168]{1,0:T(8,128)(2,1)S(1)} %collective-permute-done.14.refs_2_, bf16[8,7168]{1,0:T(8,128)(2,1)S(1)} %collective-permute-done.16.refs_3_, ...), custom_call_target="tpu_custom_call" | custom-call | flops 44040192 | bytes 1835008 | tf_op jit(solution)/shard_map/pallas_call | solution.py:36
  (24 shorter events, 0.3 us)
Async XLA Ops:
  1.6 9.1 %collective-permute-start = (bf16[8,7168]{1,0:T(8,128)(2,1)S(1)}, bf16[8,7168]{1,0:T(8,128)(2,1)S(1)}, u32[]{:S(2)}, u32[]{:S(2)}) collective-permute-start(bf16[8,7168]{1,0:T(8,128)(2,1)S(1)} %get-tuple-element.23), channel_id=1, source_target_pairs={{0,12},{1,13},{2,14},{3,15},{4,8},{5,9},{6,10},{7,11},{8,4},{9,5},... | collective-permute-start | bytes 344072 | tf_op jit(solution)/shard_map/ppermute | solution.py:193
  6.7 14.7 %copy-start = (bf16[7168,256]{1,0:T(8,128)(2,1)S(1)}, bf16[7168,256]{1,0:T(8,128)(2,1)}, u32[]{:S(2)}) copy-start(bf16[7168,256]{1,0:T(8,128)(2,1)} %refs_0_.3) | copy-start | bytes 11010052
  6.7 14.7 %copy-start.1 = (bf16[7168,256]{1,0:T(8,128)(2,1)S(1)}, bf16[7168,256]{1,0:T(8,128)(2,1)}, u32[]{:S(2)}) copy-start(bf16[7168,256]{1,0:T(8,128)(2,1)} %refs_1_.1) | copy-start | bytes 11010052
  6.7 14.7 %copy-start.2 = (bf16[256,7168]{1,0:T(8,128)(2,1)S(1)}, bf16[256,7168]{1,0:T(8,128)(2,1)}, u32[]{:S(2)}) copy-start(bf16[256,7168]{1,0:T(8,128)(2,1)} %refs_2_.1) | copy-start | bytes 11010052
  6.8 7.4 %collective-permute-start.4 = (bf16[8,7168]{1,0:T(8,128)(2,1)S(1)}, bf16[8,7168]{1,0:T(8,128)(2,1)S(1)}, u32[]{:S(2)}, u32[]{:S(2)}) collective-permute-start(bf16[8,7168]{1,0:T(8,128)(2,1)S(1)} %get-tuple-element.24.refs_0_), channel_id=1, source_target_pairs={{0,2},{1,3},{2,0},{3,1},{4,6},{5,7},{6,4},{7,5},{8,10},{9,11},{10,... | collective-permute-start | bytes 344072 | tf_op jit(solution)/shard_map/ppermute | solution.py:193
  8.4 5.8 %collective-permute-start.5 = (bf16[8,7168]{1,0:T(8,128)(2,1)S(1)}, bf16[8,7168]{1,0:T(8,128)(2,1)S(1)}, u32[]{:S(2)}, u32[]{:S(2)}) collective-permute-start(bf16[8,7168]{1,0:T(8,128)(2,1)S(1)} %get-tuple-element.20.refs_0_), channel_id=1, source_target_pairs={{0,4},{1,5},{2,6},{3,7},{4,0},{5,1},{6,2},{7,3},{8,12},{9,13},{10,... | collective-permute-start | bytes 344072 | tf_op jit(solution)/shard_map/ppermute | solution.py:193
  10.7 6.5 %collective-permute-start.3 = (bf16[8,7168]{1,0:T(8,128)(2,1)S(1)}, bf16[8,7168]{1,0:T(8,128)(2,1)S(1)}, u32[]{:S(2)}, u32[]{:S(2)}) collective-permute-start(bf16[8,7168]{1,0:T(8,128)(2,1)S(1)} %collective-permute-done.refs_0_.refs_3_), channel_id=1, source_target_pairs={{0,6},{1,7},{2,4},{3,5},{4,2},{5,3},{6,0},{7,1},{8,14},{9,15},{10,... | collective-permute-start | bytes 344072 | tf_op jit(solution)/shard_map/ppermute | solution.py:193
  13.0 6.5 %collective-permute-start.2 = (bf16[8,7168]{1,0:T(8,128)(2,1)S(1)}, bf16[8,7168]{1,0:T(8,128)(2,1)S(1)}, u32[]{:S(2)}, u32[]{:S(2)}) collective-permute-start(bf16[8,7168]{1,0:T(8,128)(2,1)S(1)} %collective-permute-done.refs_0_.refs_3_), channel_id=1, source_target_pairs={{0,2},{1,5},{2,0},{3,7},{4,6},{5,1},{6,4},{7,3},{8,10},{9,13},{10,... | collective-permute-start | bytes 344072 | tf_op jit(solution)/shard_map/ppermute | solution.py:193
  13.5 6.0 %collective-permute-start.1 = (bf16[8,7168]{1,0:T(8,128)(2,1)S(1)}, bf16[8,7168]{1,0:T(8,128)(2,1)S(1)}, u32[]{:S(2)}, u32[]{:S(2)}) collective-permute-start(bf16[8,7168]{1,0:T(8,128)(2,1)S(1)} %collective-permute-done.refs_0_.refs_3_), channel_id=1, source_target_pairs={{0,4},{1,3},{2,6},{3,1},{4,0},{5,7},{6,2},{7,5},{8,12},{9,11},{10,... | collective-permute-start | bytes 344072 | tf_op jit(solution)/shard_map/ppermute | solution.py:193
  14.2 5.3 %collective-permute-start.6 = (bf16[8,7168]{1,0:T(8,128)(2,1)S(1)}, bf16[8,7168]{1,0:T(8,128)(2,1)S(1)}, u32[]{:S(2)}, u32[]{:S(2)}) collective-permute-start(bf16[8,7168]{1,0:T(8,128)(2,1)S(1)} %shard_map.75), channel_id=1, source_target_pairs={{0,4},{1,3},{2,6},{3,1},{4,0},{5,7},{6,2},{7,5},{8,12},{9,11},{10,... | collective-permute-start | bytes 344072 | tf_op jit(solution)/shard_map/ppermute | solution.py:193
  15.7 4.0 %collective-permute-start.8 = (bf16[32,7168]{1,0:T(8,128)(2,1)S(1)}, bf16[32,7168]{1,0:T(8,128)(2,1)S(1)}, u32[]{:S(2)}, u32[]{:S(2)}) collective-permute-start(bf16[32,7168]{1,0:T(8,128)(2,1)S(1)} %shard_map.78.refs_4_), channel_id=1, source_target_pairs={{0,1},{1,0},{2,3},{3,2},{4,5},{5,4},{6,7},{7,6},{8,9},{9,8},{10,11... | collective-permute-start | bytes 1376264 | tf_op jit(solution)/shard_map/ppermute | solution.py:193
  19.6 1.9 %collective-permute-start.7 = (bf16[32,7168]{1,0:T(8,128)(2,1)S(1)}, bf16[32,7168]{1,0:T(8,128)(2,1)S(1)}, u32[]{:S(2)}, u32[]{:S(2)}) collective-permute-start(bf16[32,7168]{1,0:T(8,128)(2,1)S(1)} %shard_map.76.refs_3_), channel_id=1, source_target_pairs={{0,1},{1,0},{2,3},{3,2},{4,5},{5,4},{6,7},{7,6},{8,9},{9,8},{10,11... | collective-permute-start | bytes 1376264 | tf_op jit(solution)/shard_map/ppermute | solution.py:193
  23.2 1.9 %collective-permute-start.10 = (bf16[32,7168]{1,0:T(8,128)(2,1)S(1)}, bf16[32,7168]{1,0:T(8,128)(2,1)S(1)}, u32[]{:S(2)}, u32[]{:S(2)}) collective-permute-start(bf16[32,7168]{1,0:T(8,128)(2,1)S(1)} %get-tuple-element.28), channel_id=1, source_target_pairs={{0,1},{1,0},{2,3},{3,2},{4,5},{5,4},{6,7},{7,6},{8,9},{9,8},{10,11... | collective-permute-start | bytes 1376264 | tf_op jit(solution)/shard_map/ppermute | solution.py:193
  23.4 6.9 %collective-permute-start.9 = (bf16[32,7168]{1,0:T(8,128)(2,1)S(1)}, bf16[32,7168]{1,0:T(8,128)(2,1)S(1)}, u32[]{:S(2)}, u32[]{:S(2)}) collective-permute-start(bf16[32,7168]{1,0:T(8,128)(2,1)S(1)} %get-tuple-element.26), channel_id=1, source_target_pairs={{0,1},{1,0},{2,3},{3,2},{4,5},{5,4},{6,7},{7,6},{8,9},{9,8},{10,11... | collective-permute-start | bytes 1376264 | tf_op jit(solution)/shard_map/ppermute | solution.py:193
  25.2 6.1 %collective-permute-start.11 = (bf16[8,7168]{1,0:T(8,128)(2,1)S(1)}, bf16[8,7168]{1,0:T(8,128)(2,1)S(1)}, u32[]{:S(2)}, u32[]{:S(2)}) collective-permute-start(bf16[8,7168]{1,0:T(8,128)(2,1)S(1)} %get-tuple-element.29), channel_id=1, source_target_pairs={{0,2},{1,5},{2,0},{3,7},{4,6},{5,1},{6,4},{7,3},{8,10},{9,13},{10,... | collective-permute-start | bytes 344072 | tf_op jit(solution)/shard_map/ppermute | solution.py:193
  26.8 5.9 %collective-permute-start.12 = (bf16[8,7168]{1,0:T(8,128)(2,1)S(1)}, bf16[8,7168]{1,0:T(8,128)(2,1)S(1)}, u32[]{:S(2)}, u32[]{:S(2)}) collective-permute-start(bf16[8,7168]{1,0:T(8,128)(2,1)S(1)} %get-tuple-element.30), channel_id=1, source_target_pairs={{0,4},{1,3},{2,6},{3,1},{4,0},{5,7},{6,2},{7,5},{8,12},{9,11},{10,... | collective-permute-start | bytes 344072 | tf_op jit(solution)/shard_map/ppermute | solution.py:193
  27.7 6.3 %collective-permute-start.13 = (bf16[8,7168]{1,0:T(8,128)(2,1)S(1)}, bf16[8,7168]{1,0:T(8,128)(2,1)S(1)}, u32[]{:S(2)}, u32[]{:S(2)}) collective-permute-start(bf16[8,7168]{1,0:T(8,128)(2,1)S(1)} %get-tuple-element.31), channel_id=1, source_target_pairs={{0,6},{1,7},{2,4},{3,5},{4,2},{5,3},{6,0},{7,1},{8,14},{9,15},{10,... | collective-permute-start | bytes 344072 | tf_op jit(solution)/shard_map/ppermute | solution.py:193
  28.7 8.9 %collective-permute-start.15 = (bf16[8,7168]{1,0:T(8,128)(2,1)S(1)}, bf16[8,7168]{1,0:T(8,128)(2,1)S(1)}, u32[]{:S(2)}, u32[]{:S(2)}) collective-permute-start(bf16[8,7168]{1,0:T(8,128)(2,1)S(1)} %get-tuple-element.34), channel_id=1, source_target_pairs={{0,2},{1,3},{2,0},{3,1},{4,6},{5,7},{6,4},{7,5},{8,10},{9,11},{10,... | collective-permute-start | bytes 344072 | tf_op jit(solution)/shard_map/ppermute | solution.py:193
  34.1 6.8 %collective-permute-start.17 = (bf16[8,7168]{1,0:T(8,128)(2,1)S(1)}, bf16[8,7168]{1,0:T(8,128)(2,1)S(1)}, u32[]{:S(2)}, u32[]{:S(2)}) collective-permute-start(bf16[8,7168]{1,0:T(8,128)(2,1)S(1)} %shard_map.82.refs_2_), channel_id=1, source_target_pairs={{0,12},{1,13},{2,14},{3,15},{4,8},{5,9},{6,10},{7,11},{8,4},{9,5},... | collective-permute-start | bytes 344072 | tf_op jit(solution)/shard_map/ppermute | solution.py:193
  37.7 5.2 %collective-permute-start.16 = (bf16[8,7168]{1,0:T(8,128)(2,1)S(1)}, bf16[8,7168]{1,0:T(8,128)(2,1)S(1)}, u32[]{:S(2)}, u32[]{:S(2)}) collective-permute-start(bf16[8,7168]{1,0:T(8,128)(2,1)S(1)} %shard_map.84), channel_id=1, source_target_pairs={{0,4},{1,5},{2,6},{3,7},{4,0},{5,1},{6,2},{7,3},{8,12},{9,13},{10,... | collective-permute-start | bytes 344072 | tf_op jit(solution)/shard_map/ppermute | solution.py:193
  38.0 4.9 %collective-permute-start.14 = (bf16[8,7168]{1,0:T(8,128)(2,1)S(1)}, bf16[8,7168]{1,0:T(8,128)(2,1)S(1)}, u32[]{:S(2)}, u32[]{:S(2)}) collective-permute-start(bf16[8,7168]{1,0:T(8,128)(2,1)S(1)} %get-tuple-element.33.refs_3_), channel_id=1, source_target_pairs={{0,2},{1,3},{2,0},{3,1},{4,6},{5,7},{6,4},{7,5},{8,10},{9,11},{10,... | collective-permute-start | bytes 344072 | tf_op jit(solution)/shard_map/ppermute | solution.py:193

commit v9 on v8

--- a/solution.py
+++ b/solution.py
@@ -237,7 +237,7 @@
     past = swap(past, MIXED[0])
     rows = CAP * (waves - 1)
     far = heads[0] if waves == 2 else stack(heads)
-    sent = [swap(far, s) for s in MIXED + (CORNER,)]
+    sent = [swap(far, s) for s in (CORNER,) + MIXED[::-1]]
     marks = [call(mark_kernel, shape(CAP, 128, F32), [x]) for x in heads]
     early = stack(first + [far], after=marks)
     late = stack(sent + [past])
@@ -257,11 +257,11 @@
         return call(body, outs, [home, back], after, moved=moved)
 
     *sent, past = pair(late, swap(late_away, OTHER), 0, [shape(rows, width)] * 3 + [block])
-    sent = [swap(x, s) for x, s in zip(sent, MIXED + (CORNER,))]
+    sent = [swap(x, s) for x, s in zip(sent, (CORNER,) + MIXED[::-1])]
     past = swap(past, SIDES[0])
     back = swap(early_away, OTHER)
     (kept,) = pair(early, back, len(first), [shape(rows, width, F32)])
-    totals = call(total_kernel, [block] * (waves - 1), [kept, sent[1], sent[0], sent[2]], moved=10 * rows * width)
+    totals = call(total_kernel, [block] * (waves - 1), [kept, sent[1], sent[2], sent[0]], moved=10 * rows * width)
     returned = [cross(totals[j - 1], j) for j in others]
     kept, one = pair(early, back, 0, [shape(CAP, width, F32), block], after=totals)
     body = functools.partial(passed_kernel, 2 * CAP)

time: 44.2 us -> 44.2 us (level)
  no operation moved by 1% of the time
where the time goes in v9:
time: 44.2 us; the launch traced here: 44 us
  starting transfers between devices  22.4 us (51%)
  waiting for transfers between devices  16.5 us (37%)
  Pallas kernels  4.95 us (11%)
    ppermute x18, starting transfers between devices, swap(): return lax.ppermute(x, 'tp', [(i, i ^ mask[i % 2]) for i in range(devices)])  22.4 us
    ppermute x18, waiting for transfers between devices, swap(): return lax.ppermute(x, 'tp', [(i, i ^ mask[i % 2]) for i in range(devices)])  16.5 us
    pallas_call x14, Pallas kernels, call(): pl.pallas_call(run, out_shape=outs, in_specs=[space(pltpu.HBM)] * left +...  4.95 us
  transfers between devices with their start and end apart: 18, of which 10 were waited for; matrix products, arithmetic and copies ran while one was open for 0% of the time, Pallas kernels for 1%

profile of v9, /device:TPU:0, one launch (start us, length us, event | category | flops | bytes accessed | tf_op | source)
XLA Modules:
  0.0 44.0 jit_solution(12123024432034341530)
XLA Ops:
  0.0 1.6 %shard_map.73 = (bf16[8,7168]{1,0:T(8,128)(2,1)S(1)}, bf16[8,7168]{1,0:T(8,128)(2,1)S(1)}, f32[16,64]{1,0:T(8,128)S(1)}) custom-call(bf16[64,7168]{1,0:T(8,128)(2,1)} %refs_0_.2, f32[1,7168]{1,0:T(1,128)} %bitcast.3, s32[8,64]{1,0:T(8,128)} %bitcast.4, f32[8,64]{1,0:T(8,128)} %bitcast.5), custom_call_target="tpu_custom_call" | custom-call | flops 14680064 | bytes 917504 | tf_op jit(solution)/shard_map/pallas_call | solution.py:36
  1.6 5.1 %collective-permute-start = (bf16[8,7168]{1,0:T(8,128)(2,1)S(1)}, bf16[8,7168]{1,0:T(8,128)(2,1)S(1)}, u32[]{:S(2)}, u32[]{:S(2)}) collective-permute-start(bf16[8,7168]{1,0:T(8,128)(2,1)S(1)} %get-tuple-element.23), channel_id=1, source_target_pairs={{0,12},{1,13},{2,14},{3,15},{4,8},{5,9},{6,10},{7,11},{8,4},{9,5},... | collective-permute-start | bytes 344072 | tf_op jit(solution)/shard_map/ppermute | solution.py:193
  6.7 0.1 shard_map.74
  6.8 1.6 %collective-permute-start.4 = (bf16[8,7168]{1,0:T(8,128)(2,1)S(1)}, bf16[8,7168]{1,0:T(8,128)(2,1)S(1)}, u32[]{:S(2)}, u32[]{:S(2)}) collective-permute-start(bf16[8,7168]{1,0:T(8,128)(2,1)S(1)} %get-tuple-element.24.refs_0_), channel_id=1, source_target_pairs={{0,2},{1,3},{2,0},{3,1},{4,6},{5,7},{6,4},{7,5},{8,10},{9,11},{10,... | collective-permute-start | bytes 344072 | tf_op jit(solution)/shard_map/ppermute | solution.py:193
  8.4 2.3 %collective-permute-done.refs_0_.refs_3_ = bf16[8,7168]{1,0:T(8,128)(2,1)S(1)} collective-permute-done((bf16[8,7168]{1,0:T(8,128)(2,1)S(1)}, bf16[8,7168]{1,0:T(8,128)(2,1)S(1)}, u32[]{:S(2)}, u32[]{:S(2)}) %collective-permute-start) | collective-permute-done | bytes 114720 | tf_op jit(solution)/shard_map/ppermute | solution.py:193
  10.7 1.3 %collective-permute-start.3 = (bf16[8,7168]{1,0:T(8,128)(2,1)S(1)}, bf16[8,7168]{1,0:T(8,128)(2,1)S(1)}, u32[]{:S(2)}, u32[]{:S(2)}) collective-permute-start(bf16[8,7168]{1,0:T(8,128)(2,1)S(1)} %collective-permute-done.refs_0_.refs_3_), channel_id=1, source_target_pairs={{0,4},{1,3},{2,6},{3,1},{4,0},{5,7},{6,2},{7,5},{8,12},{9,11},{10,... | collective-permute-start | bytes 344072 | tf_op jit(solution)/shard_map/ppermute | solution.py:193
  12.0 1.5 %collective-permute-start.2 = (bf16[8,7168]{1,0:T(8,128)(2,1)S(1)}, bf16[8,7168]{1,0:T(8,128)(2,1)S(1)}, u32[]{:S(2)}, u32[]{:S(2)}) collective-permute-start(bf16[8,7168]{1,0:T(8,128)(2,1)S(1)} %collective-permute-done.refs_0_.refs_3_), channel_id=1, source_target_pairs={{0,2},{1,5},{2,0},{3,7},{4,6},{5,1},{6,4},{7,3},{8,10},{9,13},{10,... | collective-permute-start | bytes 344072 | tf_op jit(solution)/shard_map/ppermute | solution.py:193
  13.6 0.6 %collective-permute-start.1 = (bf16[8,7168]{1,0:T(8,128)(2,1)S(1)}, bf16[8,7168]{1,0:T(8,128)(2,1)S(1)}, u32[]{:S(2)}, u32[]{:S(2)}) collective-permute-start(bf16[8,7168]{1,0:T(8,128)(2,1)S(1)} %collective-permute-done.refs_0_.refs_3_), channel_id=1, source_target_pairs={{0,6},{1,7},{2,4},{3,5},{4,2},{5,3},{6,0},{7,1},{8,14},{9,15},{10,... | collective-permute-start | bytes 344072 | tf_op jit(solution)/shard_map/ppermute | solution.py:193
  14.2 1.4 %collective-permute-start.6 = (bf16[8,7168]{1,0:T(8,128)(2,1)S(1)}, bf16[8,7168]{1,0:T(8,128)(2,1)S(1)}, u32[]{:S(2)}, u32[]{:S(2)}) collective-permute-start(bf16[8,7168]{1,0:T(8,128)(2,1)S(1)} %shard_map.75), channel_id=1, source_target_pairs={{0,4},{1,3},{2,6},{3,1},{4,0},{5,7},{6,2},{7,5},{8,12},{9,11},{10,... | collective-permute-start | bytes 344072 | tf_op jit(solution)/shard_map/ppermute | solution.py:193
  15.7 0.1 collective-permute-start.8
  15.7 1.1 %collective-permute-done.3.refs_2_ = bf16[8,7168]{1,0:T(8,128)(2,1)S(1)} collective-permute-done((bf16[8,7168]{1,0:T(8,128)(2,1)S(1)}, bf16[8,7168]{1,0:T(8,128)(2,1)S(1)}, u32[]{:S(2)}, u32[]{:S(2)}) %collective-permute-start.3) | collective-permute-done | bytes 114720 | tf_op jit(solution)/shard_map/ppermute | solution.py:193
  16.8 2.7 %collective-permute-done.2.refs_1_ = bf16[8,7168]{1,0:T(8,128)(2,1)S(1)} collective-permute-done((bf16[8,7168]{1,0:T(8,128)(2,1)S(1)}, bf16[8,7168]{1,0:T(8,128)(2,1)S(1)}, u32[]{:S(2)}, u32[]{:S(2)}) %collective-permute-start.2) | collective-permute-done | bytes 114720 | tf_op jit(solution)/shard_map/ppermute | solution.py:193
  19.6 0.1 collective-permute-start.7
  19.7 1.8 %collective-permute-done.7.refs_5_ = bf16[32,7168]{1,0:T(8,128)(2,1)S(1)} collective-permute-done((bf16[32,7168]{1,0:T(8,128)(2,1)S(1)}, bf16[32,7168]{1,0:T(8,128)(2,1)S(1)}, u32[]{:S(2)}, u32[]{:S(2)}) %collective-permute-start.7) | collective-permute-done | bytes 458784 | tf_op jit(solution)/shard_map/ppermute | solution.py:193
  21.5 1.7 %shard_map.79 = (bf16[32,7168]{1,0:T(8,128)(2,1)S(1)}, bf16[32,7168]{1,0:T(8,128)(2,1)S(1)}, bf16[32,7168]{1,0:T(8,128)(2,1)S(1)}, bf16[32,7168]{1,0:T(8,128)(2,1)S(1)}) custom-call(bf16[7168,256]{1,0:T(8,128)(2,1)S(1)} %copy-done, bf16[7168,256]{1,0:T(8,128)(2,1)S(1)} %copy-done.1, bf16[256,7168]{1,0:T(8,128)(2,1)S(1)} %copy-done.2, ...), custom_call_target="tpu_custom_call" | custom-call | flops 1409286144 | bytes 11010048 | tf_op jit(solution)/shard_map/pallas_call | solution.py:36
  23.2 0.2 collective-permute-start.10
  23.4 0.4 collective-permute-start.9
  23.8 1.3 %collective-permute-done.10.refs_1_ = bf16[32,7168]{1,0:T(8,128)(2,1)S(1)} collective-permute-done((bf16[32,7168]{1,0:T(8,128)(2,1)S(1)}, bf16[32,7168]{1,0:T(8,128)(2,1)S(1)}, u32[]{:S(2)}, u32[]{:S(2)}) %collective-permute-start.10) | collective-permute-done | bytes 458784 | tf_op jit(solution)/shard_map/ppermute | solution.py:193
  25.1 0.1 shard_map.81
  25.2 1.6 %collective-permute-start.11 = (bf16[8,7168]{1,0:T(8,128)(2,1)S(1)}, bf16[8,7168]{1,0:T(8,128)(2,1)S(1)}, u32[]{:S(2)}, u32[]{:S(2)}) collective-permute-start(bf16[8,7168]{1,0:T(8,128)(2,1)S(1)} %get-tuple-element.29), channel_id=1, source_target_pairs={{0,2},{1,5},{2,0},{3,7},{4,6},{5,1},{6,4},{7,3},{8,10},{9,13},{10,... | collective-permute-start | bytes 344072 | tf_op jit(solution)/shard_map/ppermute | solution.py:193
  26.8 1.4 %collective-permute-start.12 = (bf16[8,7168]{1,0:T(8,128)(2,1)S(1)}, bf16[8,7168]{1,0:T(8,128)(2,1)S(1)}, u32[]{:S(2)}, u32[]{:S(2)}) collective-permute-start(bf16[8,7168]{1,0:T(8,128)(2,1)S(1)} %get-tuple-element.30), channel_id=1, source_target_pairs={{0,4},{1,3},{2,6},{3,1},{4,0},{5,7},{6,2},{7,5},{8,12},{9,11},{10,... | collective-permute-start | bytes 344072 | tf_op jit(solution)/shard_map/ppermute | solution.py:193
  28.2 0.5 %collective-permute-start.13 = (bf16[8,7168]{1,0:T(8,128)(2,1)S(1)}, bf16[8,7168]{1,0:T(8,128)(2,1)S(1)}, u32[]{:S(2)}, u32[]{:S(2)}) collective-permute-start(bf16[8,7168]{1,0:T(8,128)(2,1)S(1)} %get-tuple-element.31), channel_id=1, source_target_pairs={{0,6},{1,7},{2,4},{3,5},{4,2},{5,3},{6,0},{7,1},{8,14},{9,15},{10,... | collective-permute-start | bytes 344072 | tf_op jit(solution)/shard_map/ppermute | solution.py:193
  28.7 1.6 %collective-permute-start.15 = (bf16[8,7168]{1,0:T(8,128)(2,1)S(1)}, bf16[8,7168]{1,0:T(8,128)(2,1)S(1)}, u32[]{:S(2)}, u32[]{:S(2)}) collective-permute-start(bf16[8,7168]{1,0:T(8,128)(2,1)S(1)} %get-tuple-element.34), channel_id=1, source_target_pairs={{0,2},{1,3},{2,0},{3,1},{4,6},{5,7},{6,4},{7,5},{8,10},{9,11},{10,... | collective-permute-start | bytes 344072 | tf_op jit(solution)/shard_map/ppermute | solution.py:193
  30.4 0.4 collective-permute-done.11.refs_1_
  30.8 1.9 %collective-permute-done.12.refs_2_ = bf16[8,7168]{1,0:T(8,128)(2,1)S(1)} collective-permute-done((bf16[8,7168]{1,0:T(8,128)(2,1)S(1)}, bf16[8,7168]{1,0:T(8,128)(2,1)S(1)}, u32[]{:S(2)}, u32[]{:S(2)}) %collective-permute-start.12) | collective-permute-done | bytes 114720 | tf_op jit(solution)/shard_map/ppermute | solution.py:193
  32.7 1.4 %collective-permute-done.13.refs_3_ = bf16[8,7168]{1,0:T(8,128)(2,1)S(1)} collective-permute-done((bf16[8,7168]{1,0:T(8,128)(2,1)S(1)}, bf16[8,7168]{1,0:T(8,128)(2,1)S(1)}, u32[]{:S(2)}, u32[]{:S(2)}) %collective-permute-start.13) | collective-permute-done | bytes 114720 | tf_op jit(solution)/shard_map/ppermute | solution.py:193
  34.1 3.5 %collective-permute-start.17 = (bf16[8,7168]{1,0:T(8,128)(2,1)S(1)}, bf16[8,7168]{1,0:T(8,128)(2,1)S(1)}, u32[]{:S(2)}, u32[]{:S(2)}) collective-permute-start(bf16[8,7168]{1,0:T(8,128)(2,1)S(1)} %shard_map.82.refs_2_), channel_id=1, source_target_pairs={{0,12},{1,13},{2,14},{3,15},{4,8},{5,9},{6,10},{7,11},{8,4},{9,5},... | collective-permute-start | bytes 344072 | tf_op jit(solution)/shard_map/ppermute | solution.py:193
  37.7 0.3 collective-permute-start.16
  38.0 1.2 %collective-permute-start.14 = (bf16[8,7168]{1,0:T(8,128)(2,1)S(1)}, bf16[8,7168]{1,0:T(8,128)(2,1)S(1)}, u32[]{:S(2)}, u32[]{:S(2)}) collective-permute-start(bf16[8,7168]{1,0:T(8,128)(2,1)S(1)} %get-tuple-element.33.refs_3_), channel_id=1, source_target_pairs={{0,2},{1,3},{2,0},{3,1},{4,6},{5,7},{6,4},{7,5},{8,10},{9,11},{10,... | collective-permute-start | bytes 344072 | tf_op jit(solution)/shard_map/ppermute | solution.py:193
  39.2 1.7 %collective-permute-done.17.refs_0_.refs_4_ = bf16[8,7168]{1,0:T(8,128)(2,1)S(1)} collective-permute-done((bf16[8,7168]{1,0:T(8,128)(2,1)S(1)}, bf16[8,7168]{1,0:T(8,128)(2,1)S(1)}, u32[]{:S(2)}, u32[]{:S(2)}) %collective-permute-start.17) | collective-permute-done | bytes 114720 | tf_op jit(solution)/shard_map/ppermute | solution.py:193
  40.9 1.9 %collective-permute-done.16.refs_3_ = bf16[8,7168]{1,0:T(8,128)(2,1)S(1)} collective-permute-done((bf16[8,7168]{1,0:T(8,128)(2,1)S(1)}, bf16[8,7168]{1,0:T(8,128)(2,1)S(1)}, u32[]{:S(2)}, u32[]{:S(2)}) %collective-permute-start.16) | collective-permute-done | bytes 114720 | tf_op jit(solution)/shard_map/ppermute | solution.py:193
  42.9 1.2 %shard_map.86 = bf16[64,7168]{1,0:T(8,128)(2,1)} custom-call(bf16[64,48]{1,0:T(8,128)(2,1)S(1)} %get-tuple-element.22.refs_0_, f32[8,7168]{1,0:T(8,128)S(1)} %get-tuple-element.32.refs_1_, bf16[8,7168]{1,0:T(8,128)(2,1)S(1)} %collective-permute-done.14.refs_2_, bf16[8,7168]{1,0:T(8,128)(2,1)S(1)} %collective-permute-done.16.refs_3_, ...), custom_call_target="tpu_custom_call" | custom-call | flops 44040192 | bytes 1835008 | tf_op jit(solution)/shard_map/pallas_call | solution.py:36
  (24 shorter events, 0.3 us)
Async XLA Ops:
  1.6 9.1 %collective-permute-start = (bf16[8,7168]{1,0:T(8,128)(2,1)S(1)}, bf16[8,7168]{1,0:T(8,128)(2,1)S(1)}, u32[]{:S(2)}, u32[]{:S(2)}) collective-permute-start(bf16[8,7168]{1,0:T(8,128)(2,1)S(1)} %get-tuple-element.23), channel_id=1, source_target_pairs={{0,12},{1,13},{2,14},{3,15},{4,8},{5,9},{6,10},{7,11},{8,4},{9,5},... | collective-permute-start | bytes 344072 | tf_op jit(solution)/shard_map/ppermute | solution.py:193
  6.7 14.7 %copy-start = (bf16[7168,256]{1,0:T(8,128)(2,1)S(1)}, bf16[7168,256]{1,0:T(8,128)(2,1)}, u32[]{:S(2)}) copy-start(bf16[7168,256]{1,0:T(8,128)(2,1)} %refs_0_.3) | copy-start | bytes 11010052
  6.7 14.7 %copy-start.1 = (bf16[7168,256]{1,0:T(8,128)(2,1)S(1)}, bf16[7168,256]{1,0:T(8,128)(2,1)}, u32[]{:S(2)}) copy-start(bf16[7168,256]{1,0:T(8,128)(2,1)} %refs_1_.1) | copy-start | bytes 11010052
  6.7 14.7 %copy-start.2 = (bf16[256,7168]{1,0:T(8,128)(2,1)S(1)}, bf16[256,7168]{1,0:T(8,128)(2,1)}, u32[]{:S(2)}) copy-start(bf16[256,7168]{1,0:T(8,128)(2,1)} %refs_2_.1) | copy-start | bytes 11010052
  6.8 7.4 %collective-permute-start.4 = (bf16[8,7168]{1,0:T(8,128)(2,1)S(1)}, bf16[8,7168]{1,0:T(8,128)(2,1)S(1)}, u32[]{:S(2)}, u32[]{:S(2)}) collective-permute-start(bf16[8,7168]{1,0:T(8,128)(2,1)S(1)} %get-tuple-element.24.refs_0_), channel_id=1, source_target_pairs={{0,2},{1,3},{2,0},{3,1},{4,6},{5,7},{6,4},{7,5},{8,10},{9,11},{10,... | collective-permute-start | bytes 344072 | tf_op jit(solution)/shard_map/ppermute | solution.py:193
  8.4 5.8 %collective-permute-start.5 = (bf16[8,7168]{1,0:T(8,128)(2,1)S(1)}, bf16[8,7168]{1,0:T(8,128)(2,1)S(1)}, u32[]{:S(2)}, u32[]{:S(2)}) collective-permute-start(bf16[8,7168]{1,0:T(8,128)(2,1)S(1)} %get-tuple-element.20.refs_0_), channel_id=1, source_target_pairs={{0,4},{1,5},{2,6},{3,7},{4,0},{5,1},{6,2},{7,3},{8,12},{9,13},{10,... | collective-permute-start | bytes 344072 | tf_op jit(solution)/shard_map/ppermute | solution.py:193
  10.7 6.1 %collective-permute-start.3 = (bf16[8,7168]{1,0:T(8,128)(2,1)S(1)}, bf16[8,7168]{1,0:T(8,128)(2,1)S(1)}, u32[]{:S(2)}, u32[]{:S(2)}) collective-permute-start(bf16[8,7168]{1,0:T(8,128)(2,1)S(1)} %collective-permute-done.refs_0_.refs_3_), channel_id=1, source_target_pairs={{0,4},{1,3},{2,6},{3,1},{4,0},{5,7},{6,2},{7,5},{8,12},{9,11},{10,... | collective-permute-start | bytes 344072 | tf_op jit(solution)/shard_map/ppermute | solution.py:193
  12.0 7.5 %collective-permute-start.2 = (bf16[8,7168]{1,0:T(8,128)(2,1)S(1)}, bf16[8,7168]{1,0:T(8,128)(2,1)S(1)}, u32[]{:S(2)}, u32[]{:S(2)}) collective-permute-start(bf16[8,7168]{1,0:T(8,128)(2,1)S(1)} %collective-permute-done.refs_0_.refs_3_), channel_id=1, source_target_pairs={{0,2},{1,5},{2,0},{3,7},{4,6},{5,1},{6,4},{7,3},{8,10},{9,13},{10,... | collective-permute-start | bytes 344072 | tf_op jit(solution)/shard_map/ppermute | solution.py:193
  13.6 5.9 %collective-permute-start.1 = (bf16[8,7168]{1,0:T(8,128)(2,1)S(1)}, bf16[8,7168]{1,0:T(8,128)(2,1)S(1)}, u32[]{:S(2)}, u32[]{:S(2)}) collective-permute-start(bf16[8,7168]{1,0:T(8,128)(2,1)S(1)} %collective-permute-done.refs_0_.refs_3_), channel_id=1, source_target_pairs={{0,6},{1,7},{2,4},{3,5},{4,2},{5,3},{6,0},{7,1},{8,14},{9,15},{10,... | collective-permute-start | bytes 344072 | tf_op jit(solution)/shard_map/ppermute | solution.py:193
  14.2 5.3 %collective-permute-start.6 = (bf16[8,7168]{1,0:T(8,128)(2,1)S(1)}, bf16[8,7168]{1,0:T(8,128)(2,1)S(1)}, u32[]{:S(2)}, u32[]{:S(2)}) collective-permute-start(bf16[8,7168]{1,0:T(8,128)(2,1)S(1)} %shard_map.75), channel_id=1, source_target_pairs={{0,4},{1,3},{2,6},{3,1},{4,0},{5,7},{6,2},{7,5},{8,12},{9,11},{10,... | collective-permute-start | bytes 344072 | tf_op jit(solution)/shard_map/ppermute | solution.py:193
  15.7 4.0 %collective-permute-start.8 = (bf16[32,7168]{1,0:T(8,128)(2,1)S(1)}, bf16[32,7168]{1,0:T(8,128)(2,1)S(1)}, u32[]{:S(2)}, u32[]{:S(2)}) collective-permute-start(bf16[32,7168]{1,0:T(8,128)(2,1)S(1)} %shard_map.78.refs_4_), channel_id=1, source_target_pairs={{0,1},{1,0},{2,3},{3,2},{4,5},{5,4},{6,7},{7,6},{8,9},{9,8},{10,11... | collective-permute-start | bytes 1376264 | tf_op jit(solution)/shard_map/ppermute | solution.py:193
  19.6 1.9 %collective-permute-start.7 = (bf16[32,7168]{1,0:T(8,128)(2,1)S(1)}, bf16[32,7168]{1,0:T(8,128)(2,1)S(1)}, u32[]{:S(2)}, u32[]{:S(2)}) collective-permute-start(bf16[32,7168]{1,0:T(8,128)(2,1)S(1)} %shard_map.76.refs_3_), channel_id=1, source_target_pairs={{0,1},{1,0},{2,3},{3,2},{4,5},{5,4},{6,7},{7,6},{8,9},{9,8},{10,11... | collective-permute-start | bytes 1376264 | tf_op jit(solution)/shard_map/ppermute | solution.py:193
  23.2 1.9 %collective-permute-start.10 = (bf16[32,7168]{1,0:T(8,128)(2,1)S(1)}, bf16[32,7168]{1,0:T(8,128)(2,1)S(1)}, u32[]{:S(2)}, u32[]{:S(2)}) collective-permute-start(bf16[32,7168]{1,0:T(8,128)(2,1)S(1)} %get-tuple-element.28), channel_id=1, source_target_pairs={{0,1},{1,0},{2,3},{3,2},{4,5},{5,4},{6,7},{7,6},{8,9},{9,8},{10,11... | collective-permute-start | bytes 1376264 | tf_op jit(solution)/shard_map/ppermute | solution.py:193
  23.4 6.9 %collective-permute-start.9 = (bf16[32,7168]{1,0:T(8,128)(2,1)S(1)}, bf16[32,7168]{1,0:T(8,128)(2,1)S(1)}, u32[]{:S(2)}, u32[]{:S(2)}) collective-permute-start(bf16[32,7168]{1,0:T(8,128)(2,1)S(1)} %get-tuple-element.26), channel_id=1, source_target_pairs={{0,1},{1,0},{2,3},{3,2},{4,5},{5,4},{6,7},{7,6},{8,9},{9,8},{10,11... | collective-permute-start | bytes 1376264 | tf_op jit(solution)/shard_map/ppermute | solution.py:193
  25.2 5.6 %collective-permute-start.11 = (bf16[8,7168]{1,0:T(8,128)(2,1)S(1)}, bf16[8,7168]{1,0:T(8,128)(2,1)S(1)}, u32[]{:S(2)}, u32[]{:S(2)}) collective-permute-start(bf16[8,7168]{1,0:T(8,128)(2,1)S(1)} %get-tuple-element.29), channel_id=1, source_target_pairs={{0,2},{1,5},{2,0},{3,7},{4,6},{5,1},{6,4},{7,3},{8,10},{9,13},{10,... | collective-permute-start | bytes 344072 | tf_op jit(solution)/shard_map/ppermute | solution.py:193
  26.8 5.8 %collective-permute-start.12 = (bf16[8,7168]{1,0:T(8,128)(2,1)S(1)}, bf16[8,7168]{1,0:T(8,128)(2,1)S(1)}, u32[]{:S(2)}, u32[]{:S(2)}) collective-permute-start(bf16[8,7168]{1,0:T(8,128)(2,1)S(1)} %get-tuple-element.30), channel_id=1, source_target_pairs={{0,4},{1,3},{2,6},{3,1},{4,0},{5,7},{6,2},{7,5},{8,12},{9,11},{10,... | collective-permute-start | bytes 344072 | tf_op jit(solution)/shard_map/ppermute | solution.py:193
  28.2 5.8 %collective-permute-start.13 = (bf16[8,7168]{1,0:T(8,128)(2,1)S(1)}, bf16[8,7168]{1,0:T(8,128)(2,1)S(1)}, u32[]{:S(2)}, u32[]{:S(2)}) collective-permute-start(bf16[8,7168]{1,0:T(8,128)(2,1)S(1)} %get-tuple-element.31), channel_id=1, source_target_pairs={{0,6},{1,7},{2,4},{3,5},{4,2},{5,3},{6,0},{7,1},{8,14},{9,15},{10,... | collective-permute-start | bytes 344072 | tf_op jit(solution)/shard_map/ppermute | solution.py:193
  28.7 8.9 %collective-permute-start.15 = (bf16[8,7168]{1,0:T(8,128)(2,1)S(1)}, bf16[8,7168]{1,0:T(8,128)(2,1)S(1)}, u32[]{:S(2)}, u32[]{:S(2)}) collective-permute-start(bf16[8,7168]{1,0:T(8,128)(2,1)S(1)} %get-tuple-element.34), channel_id=1, source_target_pairs={{0,2},{1,3},{2,0},{3,1},{4,6},{5,7},{6,4},{7,5},{8,10},{9,11},{10,... | collective-permute-start | bytes 344072 | tf_op jit(solution)/shard_map/ppermute | solution.py:193
  34.1 6.8 %collective-permute-start.17 = (bf16[8,7168]{1,0:T(8,128)(2,1)S(1)}, bf16[8,7168]{1,0:T(8,128)(2,1)S(1)}, u32[]{:S(2)}, u32[]{:S(2)}) collective-permute-start(bf16[8,7168]{1,0:T(8,128)(2,1)S(1)} %shard_map.82.refs_2_), channel_id=1, source_target_pairs={{0,12},{1,13},{2,14},{3,15},{4,8},{5,9},{6,10},{7,11},{8,4},{9,5},... | collective-permute-start | bytes 344072 | tf_op jit(solution)/shard_map/ppermute | solution.py:193
  37.7 5.2 %collective-permute-start.16 = (bf16[8,7168]{1,0:T(8,128)(2,1)S(1)}, bf16[8,7168]{1,0:T(8,128)(2,1)S(1)}, u32[]{:S(2)}, u32[]{:S(2)}) collective-permute-start(bf16[8,7168]{1,0:T(8,128)(2,1)S(1)} %shard_map.84), channel_id=1, source_target_pairs={{0,4},{1,5},{2,6},{3,7},{4,0},{5,1},{6,2},{7,3},{8,12},{9,13},{10,... | collective-permute-start | bytes 344072 | tf_op jit(solution)/shard_map/ppermute | solution.py:193
  38.0 4.9 %collective-permute-start.14 = (bf16[8,7168]{1,0:T(8,128)(2,1)S(1)}, bf16[8,7168]{1,0:T(8,128)(2,1)S(1)}, u32[]{:S(2)}, u32[]{:S(2)}) collective-permute-start(bf16[8,7168]{1,0:T(8,128)(2,1)S(1)} %get-tuple-element.33.refs_3_), channel_id=1, source_target_pairs={{0,2},{1,3},{2,0},{3,1},{4,6},{5,7},{6,4},{7,5},{8,10},{9,11},{10,... | collective-permute-start | bytes 344072 | tf_op jit(solution)/shard_map/ppermute | solution.py:193
